TPU v7x, 32 devices: a whole 2x2x4 slice. The times are simulated.
32 devices in a mesh: row: 4 (over z), col: 8 (over y, x, core).
Axes of the slice: x: 2, y: 2, z: 4, core: 2. Of those that a mesh axis runs over, the one named last changes fastest.
Arguments:
- tokens: bfloat16 [16384, 1024], P('row', 'col'), may hold values from -6 to 6
- cotangent: bfloat16 [16384, 1024], P('row', 'col'), may hold values from -6 to 6
- adapter_ids: int32 [16, 4], P('row'), may hold values from 0 to 7
- qkv_weight: bfloat16 [2, 1024, 3, 1024], P(None, 'row', None, 'col'), may hold values from -0.09375 to 0.09375
- qkv_bias: bfloat16 [2, 3, 1024], P(None, None, 'col'), may hold values from -1.796875 to 1.796875
- proj_weight: bfloat16 [2, 1024, 1024], P(None, 'col', 'row'), may hold values from -4 to 4
- proj_bias: bfloat16 [2, 1024], P(None, 'col'), may hold values from -1.796875 to 1.796875
- up_weight: bfloat16 [2, 1024, 4096], P(None, 'row', 'col'), may hold values from -0.09375 to 0.09375
- up_bias: bfloat16 [2, 4096], P(None, 'col'), may hold values from -1.796875 to 1.796875
- down_weight: bfloat16 [2, 4096, 1024], P(None, 'col', 'row'), may hold values from -0.09375 to 0.09375
- down_bias: bfloat16 [2, 1024], P(None, 'col'), may hold values from -1.796875 to 1.796875
- first_gain: bfloat16 [2, 1024], P(None, 'col'), may hold values from 0.5 to 1.5
- first_shift: bfloat16 [2, 1024], P(None, 'col'), may hold values from -1.796875 to 1.796875
- second_gain: bfloat16 [2, 1024], P(None, 'col'), may hold values from 0.5 to 1.5
- second_shift: bfloat16 [2, 1024], P(None, 'col'), may hold values from -1.796875 to 1.796875
- qkv_lower: bfloat16 [2, 8, 1024, 16], replicated, may hold values from -0.1875 to 0.1875
- qkv_raise: bfloat16 [2, 8, 16, 3, 1024], replicated, may hold values from -0.75 to 0.75
- proj_lower: bfloat16 [2, 8, 1024, 16], replicated, may hold values from -4 to 4
- proj_raise: bfloat16 [2, 8, 16, 1024], replicated, may hold values from -0.75 to 0.75
- up_lower: bfloat16 [2, 8, 1024, 16], replicated, may hold values from -0.1875 to 0.1875
- up_raise: bfloat16 [2, 8, 16, 4096], replicated, may hold values from -0.75 to 0.75
- down_lower: bfloat16 [2, 8, 4096, 16], replicated, may hold values from -0.09375 to 0.09375
- down_raise: bfloat16 [2, 8, 16, 1024], replicated, may hold values from -0.75 to 0.75
Outputs:
- result: float32 [16384, 1024], P('row', 'col')
- input_grad: float32 [16384, 1024], P('row', 'col')
- grad_qkv_lower: float32 [2, 8, 1024, 16], P(None, None, 'col')
- grad_qkv_raise: float32 [2, 8, 16, 3, 1024], P(None, None, None, None, 'col')
- grad_proj_lower: float32 [2, 8, 1024, 16], P(None, None, 'col')
- grad_proj_raise: float32 [2, 8, 16, 1024], P(None, None, None, 'col')
- grad_up_lower: float32 [2, 8, 1024, 16], P(None, None, 'col')
- grad_up_raise: float32 [2, 8, 16, 4096], P(None, None, None, 'col')
- grad_down_lower: float32 [2, 8, 4096, 16], P(None, None, 'col')
- grad_down_raise: float32 [2, 8, 16, 1024], P(None, None, None, 'col')
Inputs may be any that keep to these rules, and one draw needn't show every extreme that they name: adapter_ids[s, k] names the adapter of sequence s at site k.
All inputs are finite; a program needn't handle non-finite values.
Results may differ from a plain program's by a relative error of at most 0.018.
Values may be sent and summed in bfloat16 or wider, within the bound.
A program may use at most 256 MiB of HBM per device.

v0:
```python
from functools import partial

import jax
import jax.numpy as jnp
from jax import lax
from jax.sharding import PartitionSpec as P

D = 1024
HD = 64
RANK = 16
ADAPTERS = 8
LAYERS = 2
LEN = 1024
BLOCK = 256


epsilon = 1e-05


def shortened(x):
    return jax.tree.map(lambda a: a.astype(jnp.bfloat16) if a.dtype == jnp.float32 else a, x)


def column_sums(values):
    return lax.psum(values, "col")


def spread_rows(values):
    return lax.all_gather(values, "col", axis=1, tiled=True)


def spread_grads(values):
    return lax.all_gather(values, "col", axis=1, tiled=True)


def column_parts(values):
    return lax.psum_scatter(
        values.astype(jnp.bfloat16), "col", scatter_dimension=1, tiled=True
    ).astype(jnp.float32)


def pick_table(onehot, matrix):
    flattened = matrix.reshape(matrix.shape[0], -1)
    chosen = jnp.dot(onehot, flattened, preferred_element_type=jnp.float32)
    return chosen.astype(jnp.bfloat16).reshape((onehot.shape[0],) + matrix.shape[1:])


def spread_table(onehot, per_group):
    flattened = per_group.reshape(per_group.shape[0], -1)
    placed = jnp.dot(onehot.astype(jnp.float32).T, flattened, precision=lax.Precision.HIGHEST)
    return placed.reshape((onehot.shape[1],) + per_group.shape[1:])


def grouped_rows(values, group_count):
    return values.reshape((group_count, values.shape[0] // group_count) + values.shape[1:])


def group_forward(values, matrix):
    grouped = grouped_rows(values, matrix.shape[0])
    joined = jnp.einsum("slx,sxy->sly", grouped, matrix, preferred_element_type=jnp.float32)
    return joined.reshape(values.shape[0], matrix.shape[2])


def group_backward(gradient, matrix):
    grouped = grouped_rows(gradient, matrix.shape[0])
    joined = jnp.einsum("sly,sxy->slx", grouped, matrix, preferred_element_type=jnp.float32)
    return joined.reshape(gradient.shape[0], matrix.shape[1])


def group_outer(left_side, right_side, group_count):
    return jnp.einsum(
        "slx,sly->sxy",
        grouped_rows(left_side, group_count),
        grouped_rows(right_side, group_count),
        preferred_element_type=jnp.float32,
    )


def finish_norm(stream, totals, squares, gain_row, shift_row):
    center = totals[:, None] / D
    spread = squares[:, None] / D - center * center
    inverse = lax.rsqrt(spread + epsilon)
    scaled = (stream - center) * inverse
    return (scaled * gain_row.astype(jnp.float32) + shift_row.astype(jnp.float32), scaled, inverse)


def norm_share(stream, gain_row, shift_row):
    totals, squares = column_sums((jnp.sum(stream, axis=1), jnp.sum(stream * stream, axis=1)))
    return finish_norm(stream, totals, squares, gain_row, shift_row)


def back_share(grad_normed, scaled, inverse, gain_row):
    weighted = grad_normed * gain_row.astype(jnp.float32)
    first_sum, second_sum = column_sums(
        (jnp.sum(weighted, axis=1), jnp.sum(weighted * scaled, axis=1))
    )
    return inverse * (weighted - first_sum[:, None] / D - scaled * (second_sum[:, None] / D))


def gelu_back(hidden, grad_active):
    forward_value, pullback = jax.vjp(partial(jax.nn.gelu, approximate=True), hidden)
    return pullback(grad_active)[0]


def block_mask(length):
    places = lax.iota(jnp.int32, length) // BLOCK
    return places[None, :] <= places[:, None]


def masked_scores(query_rows, key_rows):
    scores = jnp.einsum(
        "qhd,khd->hqk", query_rows, key_rows, preferred_element_type=jnp.float32
    ) * HD ** (-0.5)
    return jnp.where(block_mask(query_rows.shape[0])[None], scores, -1e30)


def attend_block(packed):
    query_rows, key_rows, value_rows = (packed[:, 0], packed[:, 1], packed[:, 2])
    scores = masked_scores(query_rows, key_rows)
    highest = jnp.max(scores, axis=2, keepdims=True)
    raised = jnp.exp(scores - highest)
    totals = jnp.sum(raised, axis=2, keepdims=True)
    softmax_low = (raised / totals).astype(jnp.bfloat16)
    attended = jnp.einsum(
        "hqk,khd->qhd", softmax_low, value_rows, preferred_element_type=jnp.float32
    )
    return (attended.astype(jnp.bfloat16), (highest + jnp.log(totals))[:, :, 0])


def attend_back(bundle):
    packed, sums_log, grad_out = bundle
    query_rows, key_rows, value_rows = (packed[:, 0], packed[:, 1], packed[:, 2])
    scale_factor = HD ** (-0.5)
    softmax_full = jnp.exp(masked_scores(query_rows, key_rows) - sums_log[:, :, None])
    grad_soft = jnp.einsum("qhd,khd->hqk", grad_out, value_rows, preferred_element_type=jnp.float32)
    grad_values = jnp.einsum(
        "hqk,qhd->khd",
        softmax_full.astype(jnp.bfloat16),
        grad_out,
        preferred_element_type=jnp.float32,
    )
    inner_sum = jnp.sum(softmax_full * grad_soft, axis=2, keepdims=True)
    grad_scores = (softmax_full * (grad_soft - inner_sum)).astype(jnp.bfloat16)
    grad_queries = (
        jnp.einsum("hqk,khd->qhd", grad_scores, key_rows, preferred_element_type=jnp.float32)
        * scale_factor
    )
    grad_keys = (
        jnp.einsum("hqk,qhd->khd", grad_scores, query_rows, preferred_element_type=jnp.float32)
        * scale_factor
    )
    return jnp.stack([grad_queries, grad_keys, grad_values], axis=1).astype(jnp.bfloat16)


def shards(
    tokens,
    cotangent,
    adapter_ids,
    qkv_weight,
    qkv_bias,
    proj_weight,
    proj_bias,
    up_weight,
    up_bias,
    down_weight,
    down_bias,
    first_gain,
    first_shift,
    second_gain,
    second_shift,
    qkv_lower,
    qkv_raise,
    proj_lower,
    proj_raise,
    up_lower,
    up_raise,
    down_lower,
    down_raise,
):
    row_count = tokens.shape[0]
    share_width = tokens.shape[1]
    unit_share = up_weight.shape[2]
    seq_count = row_count // LEN
    head_count = share_width // HD
    col_start = lax.axis_index("col") * share_width
    unit_start = lax.axis_index("col") * unit_share
    labels = lax.iota(jnp.int32, ADAPTERS)
    onehots = [
        (adapter_ids[:, number][:, None] == labels[None, :]).astype(jnp.bfloat16)
        for number in range(4)
    ]
    stream = tokens.astype(jnp.float32)
    records = []
    for layer_index in range(LAYERS):
        qkv_full, up_full, proj_full, down_full = (
            lax.all_gather(qkv_weight[layer_index], "row", axis=0, tiled=True),
            lax.all_gather(up_weight[layer_index], "row", axis=0, tiled=True),
            lax.all_gather(proj_weight[layer_index], "row", axis=1, tiled=True),
            lax.all_gather(down_weight[layer_index], "row", axis=1, tiled=True),
        )
        stored = {}
        stored["qkv_flat"] = qkv_full.reshape(D, 3 * share_width)
        stored["proj_full"] = proj_full
        lower_qkv = pick_table(onehots[0], qkv_lower[layer_index])
        stored["lower_qkv_share"] = lax.dynamic_slice_in_dim(lower_qkv, col_start, share_width, 1)
        stored["raise_qkv"] = pick_table(
            onehots[0], lax.dynamic_slice_in_dim(qkv_raise[layer_index], col_start, share_width, 3)
        ).reshape(seq_count, RANK, 3 * share_width)
        stored["lower_proj"] = pick_table(
            onehots[1], lax.dynamic_slice_in_dim(proj_lower[layer_index], col_start, share_width, 1)
        )
        stored["raise_proj_full"] = pick_table(onehots[1], proj_raise[layer_index])
        raise_proj = lax.dynamic_slice_in_dim(stored["raise_proj_full"], col_start, share_width, 2)
        normed_share, stored["scaled_one"], stored["inverse_one"] = norm_share(
            stream, first_gain[layer_index], first_shift[layer_index]
        )
        stored["normed_low"] = normed_share.astype(jnp.bfloat16)
        normed = spread_rows(stored["normed_low"])
        stored["reduced"] = group_forward(normed, lower_qkv).astype(jnp.bfloat16)
        mixed_rows = (
            jnp.dot(normed, stored["qkv_flat"], preferred_element_type=jnp.float32)
            + qkv_bias[layer_index].reshape(-1).astype(jnp.float32)
            + group_forward(stored["reduced"], stored["raise_qkv"])
        )
        stored["packed"] = mixed_rows.astype(jnp.bfloat16).reshape(
            seq_count, LEN, 3, head_count, HD
        )
        attended, stored["sums_log"] = lax.map(attend_block, stored["packed"])
        stored["attended_rows"] = attended.reshape(row_count, share_width)
        stored["reduced_proj"] = column_sums(
            group_forward(stored["attended_rows"], stored["lower_proj"])
        ).astype(jnp.bfloat16)
        projected = column_parts(
            jnp.dot(stored["attended_rows"], proj_full, preferred_element_type=jnp.float32)
        )
        middle = (
            stream
            + projected
            + proj_bias[layer_index].astype(jnp.float32)
            + group_forward(stored["reduced_proj"], raise_proj)
        )
        lower_up = pick_table(onehots[2], up_lower[layer_index])
        stored["lower_up_share"] = lax.dynamic_slice_in_dim(lower_up, col_start, share_width, 1)
        stored["raise_up"] = pick_table(
            onehots[2], lax.dynamic_slice_in_dim(up_raise[layer_index], unit_start, unit_share, 2)
        )
        stored["lower_down"] = pick_table(
            onehots[3], lax.dynamic_slice_in_dim(down_lower[layer_index], unit_start, unit_share, 1)
        )
        stored["raise_down_full"] = pick_table(onehots[3], down_raise[layer_index])
        raise_down = lax.dynamic_slice_in_dim(stored["raise_down_full"], col_start, share_width, 2)
        stored["up_full"] = up_full
        stored["down_full"] = down_full
        normed_two_share, stored["scaled_two"], stored["inverse_two"] = norm_share(
            middle, second_gain[layer_index], second_shift[layer_index]
        )
        stored["normed_two_low"] = normed_two_share.astype(jnp.bfloat16)
        normed_two = spread_rows(stored["normed_two_low"])
        stored["reduced_up"] = group_forward(normed_two, lower_up).astype(jnp.bfloat16)
        stored["hidden"] = (
            jnp.dot(normed_two, up_full, preferred_element_type=jnp.float32)
            + up_bias[layer_index].astype(jnp.float32)
            + group_forward(stored["reduced_up"], stored["raise_up"])
        )
        stored["active"] = jax.nn.gelu(stored["hidden"], approximate=True).astype(jnp.bfloat16)
        stored["reduced_down"] = column_sums(
            group_forward(stored["active"], stored["lower_down"])
        ).astype(jnp.bfloat16)
        branch_two = (
            column_parts(jnp.dot(stored["active"], down_full, preferred_element_type=jnp.float32))
            + down_bias[layer_index].astype(jnp.float32)
            + group_forward(stored["reduced_down"], raise_down)
        )
        records.append(stored)
        stream = middle + branch_two
    grad_stream = cotangent.astype(jnp.float32)
    layer_grads = [None] * LAYERS
    for layer_index in reversed(range(LAYERS)):
        stored = records[layer_index]
        grad_branch_two = grad_stream.astype(jnp.bfloat16)
        outer_raise_down = group_outer(stored["reduced_down"], grad_branch_two, seq_count)
        grad_two_whole = spread_grads(grad_branch_two)
        grad_reduced_down = group_backward(grad_two_whole, stored["raise_down_full"]).astype(
            jnp.bfloat16
        )
        outer_lower_down = group_outer(stored["active"], grad_reduced_down, seq_count)
        grad_active = jnp.einsum(
            "rd,fd->rf", grad_two_whole, stored["down_full"], preferred_element_type=jnp.float32
        ) + group_backward(grad_reduced_down, stored["lower_down"])
        grad_hidden = gelu_back(stored["hidden"], grad_active).astype(jnp.bfloat16)
        outer_raise_up = group_outer(stored["reduced_up"], grad_hidden, seq_count)
        grad_reduced_up = column_sums(group_backward(grad_hidden, stored["raise_up"])).astype(
            jnp.bfloat16
        )
        outer_lower_up = group_outer(stored["normed_two_low"], grad_reduced_up, seq_count)
        grad_normed_two = column_parts(
            jnp.einsum(
                "rf,df->rd", grad_hidden, stored["up_full"], preferred_element_type=jnp.float32
            )
        ) + group_backward(grad_reduced_up, stored["lower_up_share"])
        grad_middle = grad_stream + back_share(
            grad_normed_two, stored["scaled_two"], stored["inverse_two"], second_gain[layer_index]
        )
        grad_branch = grad_middle.astype(jnp.bfloat16)
        outer_raise_proj = group_outer(stored["reduced_proj"], grad_branch, seq_count)
        grad_whole = spread_grads(grad_branch)
        grad_reduced_proj = group_backward(grad_whole, stored["raise_proj_full"]).astype(
            jnp.bfloat16
        )
        outer_lower_proj = group_outer(stored["attended_rows"], grad_reduced_proj, seq_count)
        grad_attended = (
            jnp.einsum(
                "rd,ed->re", grad_whole, stored["proj_full"], preferred_element_type=jnp.float32
            )
            + group_backward(grad_reduced_proj, stored["lower_proj"])
        ).astype(jnp.bfloat16)
        grad_packed = lax.map(
            attend_back,
            (
                stored["packed"],
                stored["sums_log"],
                grad_attended.reshape(seq_count, LEN, head_count, HD),
            ),
        )
        grad_mixed = grad_packed.reshape(row_count, 3 * share_width)
        outer_raise_qkv = group_outer(stored["reduced"], grad_mixed, seq_count)
        grad_reduced = column_sums(group_backward(grad_mixed, stored["raise_qkv"])).astype(
            jnp.bfloat16
        )
        outer_lower_qkv = group_outer(stored["normed_low"], grad_reduced, seq_count)
        grad_normed = column_parts(
            jnp.einsum(
                "rc,dc->rd", grad_mixed, stored["qkv_flat"], preferred_element_type=jnp.float32
            )
        ) + group_backward(grad_reduced, stored["lower_qkv_share"])
        grad_stream = grad_middle + back_share(
            grad_normed, stored["scaled_one"], stored["inverse_one"], first_gain[layer_index]
        )
        layer_terms = (
            spread_table(onehots[0], outer_lower_qkv),
            spread_table(onehots[0], outer_raise_qkv).reshape(ADAPTERS, RANK, 3, share_width),
            spread_table(onehots[1], outer_lower_proj),
            spread_table(onehots[1], outer_raise_proj),
            spread_table(onehots[2], outer_lower_up),
            spread_table(onehots[2], outer_raise_up),
            spread_table(onehots[3], outer_lower_down),
            spread_table(onehots[3], outer_raise_down),
        )
        layer_grads[layer_index] = layer_terms
    stacked = tuple(
        (
            jnp.stack([layer_grads[layer_number][number] for layer_number in range(LAYERS)])
            for number in range(8)
        )
    )
    stacked = jax.tree.map(
        lambda part: part.astype(jnp.float32), lax.psum(shortened(stacked), "row")
    )
    return (stream, grad_stream) + tuple(stacked)


def solution(mesh):
    return jax.shard_map(
        shards,
        mesh=mesh,
        in_specs=(
            P("row", "col"),
            P("row", "col"),
            P("row", None),
            P(None, "row", None, "col"),
            P(None, None, "col"),
            P(None, "col", "row"),
            P(None, "col"),
            P(None, "row", "col"),
            P(None, "col"),
            P(None, "col", "row"),
            P(None, "col"),
            P(None, "col"),
            P(None, "col"),
            P(None, "col"),
            P(None, "col"),
            P(),
            P(),
            P(),
            P(),
            P(),
            P(),
            P(),
            P(),
        ),
        out_specs=(
            P("row", "col"),
            P("row", "col"),
            P(None, None, "col", None),
            P(None, None, None, None, "col"),
            P(None, None, "col", None),
            P(None, None, None, "col"),
            P(None, None, "col", None),
            P(None, None, None, "col"),
            P(None, None, "col", None),
            P(None, None, None, "col"),
        ),
        check_vma=False,
    )
```

profile of v0, /device:TPU:0, one launch (start us, length us, event | category | flops | bytes accessed | tf_op | source)
XLA Modules:
  0.0 1939.9 jit_solution(16572887018076139531)
XLA Ops:
  9.4 25.5 %all-reduce.7 = (f32[4096]{0:T(1024)S(1)}, f32[4096]{0:T(1024)S(1)}) all-reduce(f32[4096]{0:T(1024)S(1)} %get-tuple-element.357, f32[4096]{0:T(1024)S(1)} %get-tuple-element.356), channel_id=1, replica_groups=mesh['row'=4,'col'=8] {'col'}, use_global_device_ids=true, to_apply=%region_3.0 | all-reduce | flops 8192 | bytes 65536 | tf_op jit(solution)/shard_map/psum | solution.py:25
  52.5 14.7 all-gather.1
  68.0 18.1 all-gather
  114.5 13.6 copy.198
  129.2 32.7 %while.52 = (s32[]{:T(128)}, bf16[4,1024,2,64]{1,3,2,0:T(8,128)(2,1)}, f32[4,2,1024]{2,1,0:T(2,128)S(1)}, bf16[4,1024,3,2,64]{1,4,3,2,0:T(8,128)(2,1)S(1)}, s32[]{:T(128)}) while((s32[]{:T(128)}, bf16[4,1024,2,64]{1,3,2,0:T(8,128)(2,1)}, f32[4,2,1024]{2,1,0:T(2,128)S(1)}, bf16[4,1024,3,2,64]{1,4,3,2,0:T(8,128)(2,1)S(1)}, s32[]{:T(128)}) %tuple.171), condition=%wide.region_7.8_spmd, body=%wide.region_4.7_spmd.sunk | while | flops 563222528 | bytes 32055876 | solution.py:228
  189.3 27.5 %all-reduce.20 = bf16[4096,16]{0,1:T(8,128)(2,1)S(1)} all-reduce(f32[4096,16]{0,1:T(8,128)S(1)} %bitcast.919), channel_id=1, replica_groups=mesh['row'=4,'col'=8] {'col'}, use_global_device_ids=true, to_apply=%region_9.10 | all-reduce | flops 65536 | bytes 393216 | tf_op jit(solution)/shard_map/psum | solution.py:25
  218.7 35.9 %reduce-scatter.25.cloned.1.call-done = bf16[128,4096]{1,0:T(8,128)(2,1)} async-done(((bf16[1024,4096]{1,0:T(8,128)(2,1)}), bf16[128,4096]{1,0:T(8,128)(2,1)}) %reduce-scatter.25.cloned.1.call-update) | async-done | bytes 1048592
  259.9 23.3 %all-reduce.6 = (f32[4096]{0:T(1024)S(1)}, f32[4096]{0:T(1024)S(1)}) all-reduce(f32[4096]{0:T(1024)S(1)} %get-tuple-element.355, f32[4096]{0:T(1024)S(1)} %get-tuple-element.354), channel_id=1, replica_groups=mesh['row'=4,'col'=8] {'col'}, use_global_device_ids=true, to_apply=%region_13.14 | all-reduce | flops 8192 | bytes 65536 | tf_op jit(solution)/shard_map/psum | solution.py:25
  305.0 38.0 %all-gather.23.cloned.1.call-done = bf16[4096,1024]{1,0:T(8,128)(2,1)} async-done(((bf16[4096,128]{1,0:T(8,128)(2,1)}), bf16[4096,1024]{1,0:T(8,128)(2,1)}) %all-gather.23.cloned.1.call-update) | async-done | bytes 8388624 | tf_op jit(solution)/shard_map/all_gather | solution.py:29
  353.9 19.1 all-gather.37.cloned.1.call-done
  373.0 13.7 multiply_convert_fusion.3
  386.7 17.5 all-gather.39.cloned.1.call-done
  414.5 11.3 copy.334
  438.5 29.9 %all-reduce.21 = bf16[4096,16]{0,1:T(8,128)(2,1)S(1)} all-reduce(f32[4096,16]{0,1:T(8,128)S(1)} %bitcast.921), channel_id=1, replica_groups=mesh['row'=4,'col'=8] {'col'}, use_global_device_ids=true, to_apply=%region_15.16 | all-reduce | flops 65536 | bytes 393216 | tf_op jit(solution)/shard_map/psum | solution.py:25
  470.3 27.4 %reduce-scatter.27.cloned.1.call-done = bf16[128,4096]{1,0:T(8,128)(2,1)} async-done(((bf16[1024,4096]{1,0:T(8,128)(2,1)}), bf16[128,4096]{1,0:T(8,128)(2,1)}) %reduce-scatter.27.cloned.1.call-update) | async-done | bytes 1048592
  503.5 23.1 %all-reduce.5 = (f32[4096]{0:T(1024)S(1)}, f32[4096]{0:T(1024)S(1)}) all-reduce(f32[4096]{0:T(1024)} %get-tuple-element.353, f32[4096]{0:T(1024)S(1)} %get-tuple-element.352), channel_id=1, replica_groups=mesh['row'=4,'col'=8] {'col'}, use_global_device_ids=true, to_apply=%region_19.20 | all-reduce | flops 8192 | bytes 65536 | tf_op jit(solution)/shard_map/psum | solution.py:25
  538.6 14.4 all-gather.5
  553.2 18.2 all-gather.4
  571.3 17.2 all-gather.25.cloned.1.call-done
  606.6 13.6 copy.216
  621.9 34.9 %while.53 = (s32[]{:T(128)}, bf16[4,1024,2,64]{1,3,2,0:T(8,128)(2,1)}, f32[4,2,1024]{2,1,0:T(2,128)}, bf16[4,1024,3,2,64]{1,4,3,2,0:T(8,128)(2,1)S(1)}, s32[]{:T(128)}) while((s32[]{:T(128)}, bf16[4,1024,2,64]{1,3,2,0:T(8,128)(2,1)}, f32[4,2,1024]{2,1,0:T(2,128)}, bf16[4,1024,3,2,64]{1,4,3,2,0:T(8,128)(2,1)S(1)}, s32[]{:T(128)}) %tuple.174), condition=%wide.region_23.24_spmd, body=%wide.region_20.23_spmd.sunk | while | flops 563222528 | bytes 32056384 | solution.py:228
  681.5 27.1 %all-reduce.22 = bf16[4096,16]{0,1:T(8,128)(2,1)S(1)} all-reduce(f32[4096,16]{0,1:T(8,128)S(1)} %bitcast.923), channel_id=1, replica_groups=mesh['row'=4,'col'=8] {'col'}, use_global_device_ids=true, to_apply=%region_25.26 | all-reduce | flops 65536 | bytes 393216 | tf_op jit(solution)/shard_map/psum | solution.py:25
  710.4 38.7 %reduce-scatter.29.cloned.1.call-done = bf16[128,4096]{1,0:T(8,128)(2,1)} async-done(((bf16[1024,4096]{1,0:T(8,128)(2,1)}), bf16[128,4096]{1,0:T(8,128)(2,1)}) %reduce-scatter.29.cloned.1.call-update) | async-done | bytes 1048592
  754.7 23.7 %all-reduce.4 = (f32[4096]{0:T(1024)S(1)}, f32[4096]{0:T(1024)S(1)}) all-reduce(f32[4096]{0:T(1024)} %get-tuple-element.351, f32[4096]{0:T(1024)S(1)} %get-tuple-element.350), channel_id=1, replica_groups=mesh['row'=4,'col'=8] {'col'}, use_global_device_ids=true, to_apply=%region_29.30 | all-reduce | flops 8192 | bytes 65536 | tf_op jit(solution)/shard_map/psum | solution.py:25
  818.6 46.6 %all-gather.27.cloned.1.call-done = bf16[4096,1024]{1,0:T(8,128)(2,1)} async-done(((bf16[4096,128]{1,0:T(8,128)(2,1)}), bf16[4096,1024]{1,0:T(8,128)(2,1)}) %all-gather.27.cloned.1.call-update) | async-done | bytes 8388624 | tf_op jit(solution)/shard_map/all_gather | solution.py:29
  876.3 18.5 all-gather.41.cloned.1.call-done
  894.8 13.5 multiply_convert_fusion.2
  908.3 17.7 all-gather.43.cloned.1.call-done
  926.0 17.3 fusion.91
  968.0 27.9 %all-reduce.23 = bf16[4096,16]{0,1:T(8,128)(2,1)S(1)} all-reduce(f32[4096,16]{0,1:T(8,128)} %bitcast.925), channel_id=1, replica_groups=mesh['row'=4,'col'=8] {'col'}, use_global_device_ids=true, to_apply=%region_33.34 | all-reduce | flops 65536 | bytes 393216 | tf_op jit(solution)/shard_map/psum | solution.py:25
  997.8 36.0 %reduce-scatter.33.cloned.1.call-done = bf16[128,4096]{1,0:T(8,128)(2,1)} async-done(((bf16[1024,4096]{1,0:T(8,128)(2,1)}), bf16[128,4096]{1,0:T(8,128)(2,1)}) %reduce-scatter.33.cloned.1.call-update) | async-done | bytes 1048592
  1040.7 23.8 %all-reduce.3 = (f32[4096]{0:T(1024)S(1)}, f32[4096]{0:T(1024)S(1)}) all-reduce(f32[4096]{0:T(1024)} %get-tuple-element.349, f32[4096]{0:T(1024)} %get-tuple-element.348), channel_id=1, replica_groups=mesh['row'=4,'col'=8] {'col'}, use_global_device_ids=true, to_apply=%region_37.38 | all-reduce | flops 8192 | bytes 65536 | tf_op jit(solution)/shard_map/psum | solution.py:25
  1072.0 56.0 %all-gather.31.cloned.1.call-done = bf16[4096,1024]{1,0:T(8,128)(2,1)} async-done(((bf16[4096,128]{1,0:T(8,128)(2,1)}), bf16[4096,1024]{1,0:T(8,128)(2,1)}) %all-gather.31.cloned.1.call-update) | async-done | bytes 8388624 | tf_op jit(solution)/shard_map/all_gather | solution.py:33
  1142.1 57.8 %while.54 = (s32[]{:T(128)}, bf16[4,1024,3,2,64]{1,4,3,2,0:T(8,128)(2,1)S(1)}, bf16[4,1024,3,2,64]{1,4,3,2,0:T(8,128)(2,1)}, f32[4,2,1024]{2,1,0:T(2,128)}, bf16[4,1024,2,64]{1,3,2,0:T(8,128)(2,1)}, /*index=5*/s32[]{:T(128)}) while((s32[]{:T(128)}, bf16[4,1024,3,2,64]{1,4,3,2,0:T(8,128)(2,1)S(1)}, bf16[4,1024,3,2,64]{1,4,3,2,0:T(8,128)(2,1)}, ...), condition=%wide.region_40.41_spmd, body=%wide.region_38.40_spmd.sunk | while | flops 1377703936 | bytes 77135992 | solution.py:317
  1225.3 26.9 %all-reduce.24 = bf16[4096,16]{0,1:T(8,128)(2,1)S(1)} all-reduce(f32[4096,16]{0,1:T(8,128)S(1)} %bitcast.926), channel_id=1, replica_groups=mesh['row'=4,'col'=8] {'col'}, use_global_device_ids=true, to_apply=%region_42.43 | all-reduce | flops 65536 | bytes 393216 | tf_op jit(solution)/shard_map/psum | solution.py:25
  1255.1 38.5 %reduce-scatter.35.cloned.1.call-done = bf16[128,4096]{1,0:T(8,128)(2,1)} async-done(((bf16[1024,4096]{1,0:T(8,128)(2,1)}), bf16[128,4096]{1,0:T(8,128)(2,1)}) %reduce-scatter.35.cloned.1.call-update) | async-done | bytes 1048592
  1299.1 23.1 %all-reduce.2 = (f32[4096]{0:T(1024)S(1)}, f32[4096]{0:T(1024)S(1)}) all-reduce(f32[4096]{0:T(1024)S(1)} %get-tuple-element.347, f32[4096]{0:T(1024)S(1)} %get-tuple-element.346), channel_id=1, replica_groups=mesh['row'=4,'col'=8] {'col'}, use_global_device_ids=true, to_apply=%region_46.47 | all-reduce | flops 8192 | bytes 65536 | tf_op jit(solution)/shard_map/psum | solution.py:25
  1329.2 55.8 %all-gather.33.cloned.1.call-done = bf16[4096,1024]{1,0:T(8,128)(2,1)} async-done(((bf16[4096,128]{1,0:T(8,128)(2,1)}), bf16[4096,1024]{1,0:T(8,128)(2,1)}) %all-gather.33.cloned.1.call-update) | async-done | bytes 8388624 | tf_op jit(solution)/shard_map/all_gather | solution.py:33
  1395.5 12.7 fusion.84
  1432.6 27.0 %all-reduce.25 = bf16[4096,16]{0,1:T(8,128)(2,1)S(1)} all-reduce(f32[4096,16]{0,1:T(8,128)S(1)} %bitcast.927), channel_id=1, replica_groups=mesh['row'=4,'col'=8] {'col'}, use_global_device_ids=true, to_apply=%region_48.49 | all-reduce | flops 65536 | bytes 393216 | tf_op jit(solution)/shard_map/psum | solution.py:25
  1462.6 37.8 %reduce-scatter.37.cloned.1.call-done = bf16[128,4096]{1,0:T(8,128)(2,1)} async-done(((bf16[1024,4096]{1,0:T(8,128)(2,1)}), bf16[128,4096]{1,0:T(8,128)(2,1)}) %reduce-scatter.37.cloned.1.call-update) | async-done | bytes 1048592
  1505.8 23.6 %all-reduce.1 = (f32[4096]{0:T(1024)S(1)}, f32[4096]{0:T(1024)S(1)}) all-reduce(f32[4096]{0:T(1024)S(1)} %get-tuple-element.345, f32[4096]{0:T(1024)S(1)} %get-tuple-element.344), channel_id=1, replica_groups=mesh['row'=4,'col'=8] {'col'}, use_global_device_ids=true, to_apply=%region_52.53 | all-reduce | flops 8192 | bytes 65536 | tf_op jit(solution)/shard_map/psum | solution.py:25
  1546.7 11.4 copy.338
  1558.1 34.2 %all-gather.35.cloned.1.call-done = bf16[4096,1024]{1,0:T(8,128)(2,1)} async-done(((bf16[4096,128]{1,0:T(8,128)(2,1)}), bf16[4096,1024]{1,0:T(8,128)(2,1)}) %all-gather.35.cloned.1.call-update) | async-done | bytes 8388624 | tf_op jit(solution)/shard_map/all_gather | solution.py:33
  1606.2 58.2 %while.55 = (s32[]{:T(128)}, bf16[4,1024,3,2,64]{1,4,3,2,0:T(8,128)(2,1)S(1)}, bf16[4,1024,3,2,64]{1,4,3,2,0:T(8,128)(2,1)}, f32[4,2,1024]{2,1,0:T(2,128)}, bf16[4,1024,2,64]{1,3,2,0:T(8,128)(2,1)}, /*index=5*/s32[]{:T(128)}) while((s32[]{:T(128)}, bf16[4,1024,3,2,64]{1,4,3,2,0:T(8,128)(2,1)S(1)}, bf16[4,1024,3,2,64]{1,4,3,2,0:T(8,128)(2,1)}, ...), condition=%wide.region_55.56_spmd, body=%wide.region_53.55_spmd.sunk | while | flops 1377703936 | bytes 77135992 | solution.py:317
  1775.0 26.0 %all-reduce.26 = bf16[4096,16]{0,1:T(8,128)(2,1)S(1)} all-reduce(f32[4096,16]{0,1:T(8,128)} %bitcast.917), channel_id=1, replica_groups=mesh['row'=4,'col'=8] {'col'}, use_global_device_ids=true, to_apply=%region_57.58 | all-reduce | flops 65536 | bytes 393216 | tf_op jit(solution)/shard_map/psum | solution.py:25
  1822.1 25.5 %all-reduce.27 = (bf16[4096,16]{0,1:T(8,128)(2,1)S(1)}, f32[4096]{0:T(1024)}, f32[4096]{0:T(1024)}) all-reduce(f32[4096,16]{0,1:T(8,128)S(1)} %bitcast.916, f32[4096]{0:T(1024)} %get-tuple-element.343, f32[4096]{0:T(1024)} %get-tuple-element.342), channel_id=1, replica_groups=mesh['row'=4,'col'=8] {'col'}, use_global_device_ids=true, to_apply=%region_31.32 | all-reduce | flops 73728 | bytes 458752 | tf_op jit(solution)/shard_map/psum | solution.py:25
  1866.5 53.4 %all-reduce.19.cloned.1.call-done = (bf16[2,8,128,16]{2,1,3,0:T(8,128)(2,1)}, bf16[2,8,16,3,128]{4,1,3,2,0:T(8,128)(2,1)}, bf16[2,8,128,16]{2,1,3,0:T(8,128)(2,1...) async-done(((bf16[2,8,128,16]{2,1,3,0:T(8,128)(2,1)}, ...) | async-done | bytes 1048592 | tf_op jit(solution)/shard_map/psum | solution.py:357
  (755 shorter events, 777.7 us)
Async XLA Ops:
  7.2 89.0 %all-gather.21.cloned.1.call-start = ((), (), s32[]{:S(2)}) async-start(), calls=%async_computation.8 | async-start | bytes 9437184 | tf_op jit(solution)/shard_map/all_gather | solution.py:29
  40.7 213.9 %reduce-scatter.25.cloned.1.call-start = ((), (), s32[]{:S(2)}) async-start(), calls=%async_computation.20 | async-start | bytes 9437184
  47.1 138.6 %copy-start.121 = (s32[4]{0:T(128)}, s32[4]{0:T(128)S(1)}, u32[]{:S(2)}) copy-start(s32[4]{0:T(128)S(1)} %get-tuple-element.359) | copy-start | bytes 52
  47.1 257.0 %copy-start.117 = (s32[4]{0:T(128)}, s32[4]{0:T(128)S(1)}, u32[]{:S(2)}) copy-start(s32[4]{0:T(128)S(1)} %get-tuple-element.361) | copy-start | bytes 52
  48.2 53.8 %copy-start.23 = (bf16[4,1024,16]{2,1,0:T(8,128)(2,1)}, bf16[4,1024,16]{2,1,0:T(8,128)(2,1)S(1)}, u32[]{:S(2)}) copy-start(bf16[4,1024,16]{2,1,0:T(8,128)(2,1)S(1)} %reshape.930) | copy-start | bytes 393220
  67.2 98.0 %copy-start.29 = (bf16[1,128,1024]{2,1,0:T(8,128)(2,1)}, bf16[1,128,1024]{2,1,0:T(8,128)(2,1)S(1)}, u32[]{:S(2)}) copy-start(bf16[1,128,1024]{2,1,0:T(8,128)(2,1)S(1)} %all-gather.1) | copy-start | bytes 786436
  182.2 160.7 %all-gather.23.cloned.1.call-start = ((), (), s32[]{:S(2)}) async-start(), calls=%async_computation.9 | async-start | bytes 9437184 | tf_op jit(solution)/shard_map/all_gather | solution.py:29
  185.5 71.4 %copy-start.10 = (bf16[4096,128]{1,0:T(8,128)(2,1)S(1)}, bf16[4096,128]{1,0:T(8,128)(2,1)}, u32[]{:S(2)}) copy-start(bf16[4096,128]{1,0:T(8,128)(2,1)} %param.31) | copy-start | bytes 3145732
  187.7 95.6 %copy-start.128 = (f32[128]{0:T(128)}, f32[128]{0:T(128)S(1)}, u32[]{:S(2)}) copy-start(f32[128]{0:T(128)S(1)} %get-tuple-element.498) | copy-start | bytes 1540
  259.9 239.4 %copy-start.2 = (f32[4096,128]{1,0:T(8,128)}, f32[4096,128]{1,0:T(8,128)S(1)}, u32[]{:S(2)}) copy-start(f32[4096,128]{1,0:T(8,128)S(1)} %get-tuple-element.433) | copy-start | bytes 6291460
  286.9 86.1 %all-gather.37.cloned.1.call-start = ((), (), s32[]{:S(2)}) async-start(), calls=%async_computation.16 | async-start | bytes 1310720 | tf_op jit(solution)/shard_map/all_gather | solution.py:197
  287.8 116.4 %all-gather.39.cloned.1.call-start = ((), (), s32[]{:S(2)}) async-start(), calls=%async_computation.17 | async-start | bytes 1310720 | tf_op jit(solution)/shard_map/all_gather | solution.py:199
  288.8 208.9 %reduce-scatter.27.cloned.1.call-start = ((), (), s32[]{:S(2)}) async-start(), calls=%async_computation.21 | async-start | bytes 9437184
  298.9 49.7 %copy-start.24 = (bf16[4,1024,16]{2,1,0:T(8,128)(2,1)}, bf16[4,1024,16]{2,1,0:T(8,128)(2,1)S(1)}, u32[]{:S(2)}) copy-start(bf16[4,1024,16]{2,1,0:T(8,128)(2,1)S(1)} %reshape.942) | copy-start | bytes 393220
  304.4 44.3 %copy-start.75 = (bf16[4,8192]{1,0:T(4,128)(2,1)}, bf16[4,8192]{1,0:T(4,128)(2,1)S(1)}, u32[]{:S(2)}) copy-start(bf16[4,8192]{1,0:T(4,128)(2,1)S(1)} %convolution_convert_fusion.11) | copy-start | bytes 196612
  425.9 162.6 %all-gather.25.cloned.1.call-start = ((), (), s32[]{:S(2)}) async-start(), calls=%async_computation.10 | async-start | bytes 9437184 | tf_op jit(solution)/shard_map/all_gather | solution.py:29
  531.8 217.3 %reduce-scatter.29.cloned.1.call-start = ((), (), s32[]{:S(2)}) async-start(), calls=%async_computation.22 | async-start | bytes 9437184
  538.2 56.1 %copy-start.25 = (bf16[4,1024,16]{2,1,0:T(8,128)(2,1)}, bf16[4,1024,16]{2,1,0:T(8,128)(2,1)S(1)}, u32[]{:S(2)}) copy-start(bf16[4,1024,16]{2,1,0:T(8,128)(2,1)S(1)} %reshape.955) | copy-start | bytes 393220
  553.1 41.2 %copy-start.89 = (bf16[4,6144]{1,0:T(4,128)(2,1)}, bf16[4,6144]{1,0:T(4,128)(2,1)S(1)}, u32[]{:S(2)}) copy-start(bf16[4,6144]{1,0:T(4,128)(2,1)S(1)} %convolution_convert_fusion.20) | copy-start | bytes 147460
  677.1 130.2 %all-gather.29.cloned.1.call-start = ((), (), s32[]{:S(2)}) async-start(), calls=%async_computation.12 | async-start | bytes 9437184 | tf_op jit(solution)/shard_map/all_gather | solution.py:33
  677.8 187.4 %all-gather.27.cloned.1.call-start = ((), (), s32[]{:S(2)}) async-start(), calls=%async_computation.11 | async-start | bytes 9437184 | tf_op jit(solution)/shard_map/all_gather | solution.py:29
  708.6 42.2 %copy-start.55 = (bf16[4096,16]{0,1:T(8,128)(2,1)}, bf16[4096,16]{0,1:T(8,128)(2,1)S(1)}, u32[]{:S(2)}) copy-start(bf16[4096,16]{0,1:T(8,128)(2,1)S(1)} %all-reduce.22) | copy-start | bytes 393220
  754.7 309.7 %copy-start = (f32[4096,128]{1,0:T(8,128)}, f32[4096,128]{1,0:T(8,128)S(1)}, u32[]{:S(2)}) copy-start(f32[4096,128]{1,0:T(8,128)S(1)} %get-tuple-element.431) | copy-start | bytes 6291460
  782.2 112.6 %all-gather.41.cloned.1.call-start = ((), (), s32[]{:S(2)}) async-start(), calls=%async_computation.18 | async-start | bytes 1310720 | tf_op jit(solution)/shard_map/all_gather | solution.py:197
  782.9 143.1 %all-gather.43.cloned.1.call-start = ((), (), s32[]{:S(2)}) async-start(), calls=%async_computation.19 | async-start | bytes 1310720 | tf_op jit(solution)/shard_map/all_gather | solution.py:199
  783.5 250.3 %reduce-scatter.33.cloned.1.call-start = ((), (), s32[]{:S(2)}) async-start(), calls=%async_computation.24 | async-start | bytes 9437184
  963.7 164.3 %all-gather.31.cloned.1.call-start = ((), (), s32[]{:S(2)}) async-start(), calls=%async_computation.13 | async-start | bytes 9437184 | tf_op jit(solution)/shard_map/all_gather | solution.py:33
  996.0 44.7 %copy-start.57 = (bf16[4096,16]{0,1:T(8,128)(2,1)}, bf16[4096,16]{0,1:T(8,128)(2,1)S(1)}, u32[]{:S(2)}) copy-start(bf16[4096,16]{0,1:T(8,128)(2,1)S(1)} %all-reduce.23) | copy-start | bytes 393220
  997.8 66.7 %copy-start.17 = (bf16[4096,128]{1,0:T(8,128)(2,1)S(1)}, bf16[4096,128]{1,0:T(8,128)(2,1)}, u32[]{:S(2)}) copy-start(bf16[4096,128]{1,0:T(8,128)(2,1)} %param.32) | copy-start | bytes 3145732
  1064.5 63.4 %copy-start.50 = (bf16[4,16384]{1,0:T(4,128)(2,1)S(1)}, bf16[4,16384]{1,0:T(4,128)(2,1)}, u32[]{:S(2)}) copy-start(bf16[4,16384]{1,0:T(4,128)(2,1)} %copy-done.49) | copy-start | bytes 393220
  1071.9 221.7 %reduce-scatter.35.cloned.1.call-start = ((), (), s32[]{:S(2)}) async-start(), calls=%async_computation.25 | async-start | bytes 9437184
  1221.9 163.1 %all-gather.33.cloned.1.call-start = ((), (), s32[]{:S(2)}) async-start(), calls=%async_computation.14 | async-start | bytes 9437184 | tf_op jit(solution)/shard_map/all_gather | solution.py:33
  1222.7 72.5 %copy-start.4 = (f32[4096,128]{1,0:T(8,128)S(1)}, f32[4096,128]{1,0:T(8,128)}, u32[]{:S(2)}) copy-start(f32[4096,128]{1,0:T(8,128)} %get-tuple-element.432) | copy-start | bytes 6291460
  1222.7 72.5 %copy-start.103 = (f32[4096]{0:T(1024)S(1)}, f32[4096]{0:T(1024)}, u32[]{:S(2)}) copy-start(f32[4096]{0:T(1024)} %copy-done.102) | copy-start | bytes 49156
  1222.7 72.5 %copy-start.105 = (f32[4096]{0:T(1024)S(1)}, f32[4096]{0:T(1024)}, u32[]{:S(2)}) copy-start(f32[4096]{0:T(1024)} %copy-done.104) | copy-start | bytes 49156
  1222.7 72.5 %copy-start.127 = (f32[128]{0:T(128)S(1)}, f32[128]{0:T(128)}, u32[]{:S(2)}) copy-start(f32[128]{0:T(128)} %get-tuple-element.493) | copy-start | bytes 1540
  1252.2 41.3 %copy-start.59 = (bf16[4096,16]{0,1:T(8,128)(2,1)}, bf16[4096,16]{0,1:T(8,128)(2,1)S(1)}, u32[]{:S(2)}) copy-start(bf16[4096,16]{0,1:T(8,128)(2,1)S(1)} %all-reduce.24) | copy-start | bytes 393220
  1322.2 62.9 %copy-start.46 = (bf16[4,16384]{1,0:T(4,128)(2,1)S(1)}, bf16[4,16384]{1,0:T(4,128)(2,1)}, u32[]{:S(2)}) copy-start(bf16[4,16384]{1,0:T(4,128)(2,1)} %copy-done.45) | copy-start | bytes 393220
  1329.0 171.4 %reduce-scatter.37.cloned.1.call-start = ((), (), s32[]{:S(2)}) async-start(), calls=%async_computation.26 | async-start | bytes 9437184
  1428.3 164.1 %all-gather.35.cloned.1.call-start = ((), (), s32[]{:S(2)}) async-start(), calls=%async_computation.15 | async-start | bytes 9437184 | tf_op jit(solution)/shard_map/all_gather | solution.py:33
  1429.1 72.9 %copy-start.3 = (f32[4096,128]{1,0:T(8,128)S(1)}, f32[4096,128]{1,0:T(8,128)}, u32[]{:S(2)}) copy-start(f32[4096,128]{1,0:T(8,128)} %copy-done.2) | copy-start | bytes 6291460
  1429.1 72.9 %copy-start.99 = (f32[4096]{0:T(1024)S(1)}, f32[4096]{0:T(1024)}, u32[]{:S(2)}) copy-start(f32[4096]{0:T(1024)} %copy-done.98) | copy-start | bytes 49156
  1429.1 72.9 %copy-start.101 = (f32[4096]{0:T(1024)S(1)}, f32[4096]{0:T(1024)}, u32[]{:S(2)}) copy-start(f32[4096]{0:T(1024)} %copy-done.100) | copy-start | bytes 49156
  1429.1 73.0 %copy-start.129 = (f32[128]{0:T(128)S(1)}, f32[128]{0:T(128)}, u32[]{:S(2)}) copy-start(f32[128]{0:T(128)} %copy-done.128) | copy-start | bytes 1540
  1536.3 178.8 %reduce-scatter.31.cloned.1.call-start = ((), (), s32[]{:S(2)}) async-start(), calls=%async_computation.23 | async-start | bytes 9437184
  1558.1 256.7 %reduce-scatter.39.cloned.1.call-start = ((), (), s32[]{:S(2)}) async-start(), calls=%async_computation.27 | async-start | bytes 9437184
  1686.4 233.5 %all-reduce.19.cloned.1.call-start = ((), (), s32[]{:S(2)}) async-start(), calls=%async_computation.28 | async-start | bytes 2097152 | tf_op jit(solution)/shard_map/psum | solution.py:357
  1769.7 40.9 %copy-start.36 = (bf16[4,1024,16]{1,2,0:T(8,128)(2,1)S(1)}, bf16[4,1024,16]{1,2,0:T(8,128)(2,1)}, u32[]{:S(2)}) copy-start(bf16[4,1024,16]{1,2,0:T(8,128)(2,1)} %copy-done.35) | copy-start | bytes 393220
  (122 other events, 1203.3 us)
Sparse Core Ops, SparseCore 0:
  40.8 55.3 all-gather.20
  182.3 72.2 reduce-scatter.24
  287.1 55.8 all-gather.22
  345.0 27.9 all-gather.36
  374.5 29.6 all-gather.38
  426.0 71.6 reduce-scatter.26
  531.9 56.5 all-gather.24
  677.2 71.8 reduce-scatter.28
  751.2 56.1 all-gather.28
  809.2 55.9 all-gather.26
  866.8 27.9 all-gather.40
  896.3 29.6 all-gather.42
  963.8 70.0 reduce-scatter.32
  1072.0 55.8 all-gather.30
  1222.1 71.4 reduce-scatter.34
  1329.1 55.8 all-gather.32
  1428.4 71.9 reduce-scatter.36
  1536.4 55.8 all-gather.34
  1595.8 71.2 reduce-scatter.30
  1686.5 71.4 reduce-scatter.38
  1863.2 56.7 all-reduce.18
where the time goes:
time: 1960 us; the launch traced here: 1940 us
  waiting for transfers between devices  602 us (31%)
  blocking collectives  449 us (23%)
  matrix products  414 us (21%)
  local copies, waits for them, and re-layouts  312 us (16%)
  other arithmetic  144 us (7%)
    psum x15, blocking collectives, column_sums(): return lax.psum(values, 'col')  384 us
    unnamed x29, waiting for transfers between devices  217 us
    all_gather x4, waiting for transfers between devices, spread_grads(): return lax.all_gather(values, 'col', axis=1, tiled=True)  147 us
    unnamed x325, local copies, waits for them, and re-layouts  145 us
    all_gather x4, waiting for transfers between devices, spread_rows(): return lax.all_gather(values, 'col', axis=1, tiled=True)  112 us
    dot_general x16, matrix products, group_forward(): jnp.einsum('slx,sxy->sly', grouped, matrix, preferred_element_type=jnp.fl...  53.6 us
    psum x1, waiting for transfers between devices, shards(): lax.psum(shortened(stacked), 'row')  53.4 us
    dot_general x16, matrix products, group_backward(): jnp.einsum('sly,sxy->slx', grouped, matrix, preferred_element_type=jnp.fl...  52.6 us
  transfers between devices with their start and end apart: 21, of which 19 were waited for; matrix products, arithmetic and copies ran while one was open for 20% of the time, Pallas kernels for 0%

commit v1 on v0

v1 whole, which is shorter than its diff:
```python
import functools

import jax
import jax.numpy as jnp
from jax import lax
from jax.experimental import pallas as pl
from jax.experimental.pallas import tpu as pltpu
from jax.sharding import PartitionSpec as P

HD = 64
LEN = 1024
BLOCK = 256
BLOCKS = LEN // BLOCK
EPSILON = 1e-05
SCALE = HD**-0.5
MESH = pl.DeviceIdType.MESH
F32 = jnp.float32
BF16 = jnp.bfloat16


ORDERS = {
    "qkv": ((0, "z", 1), (1, "z", 0)),
    "proj": ((0, "z", 1), (1, "z", 0)),
    "up": (("z", 0, 1), ("z", 1, 0)),
    "down": (("z", 0, 1), ("z", 1, 0)),
}
KINDS = ("qkv", "proj", "up", "down")
WINDOW = 4


def gather_body(n_row, n_col, layers, *refs):
    shard = dict(zip(KINDS, refs[:4]))
    full = dict(zip(KINDS, refs[4:8]))
    local_sem, send_sem, recv_sem = refs[8:]
    r = lax.axis_index("row")
    c = lax.axis_index("col")
    link_bits = [b for b in (2**k for k in range(1, 8)) if b < n_col]
    depth = shard["up"].shape[1]

    def row_peer(s):
        return (lax.rem(r + s, n_row), c)

    def col_peer(bit):
        return (r, c ^ bit)

    peers = [row_peer(s) for s in range(1, n_row)]
    peers += [col_peer(b) for b in [1] + link_bits]
    barrier = pltpu.get_barrier_semaphore()
    for peer in peers:
        pl.semaphore_signal(barrier, inc=1, device_id=peer, device_id_type=MESH)
    pl.semaphore_wait(barrier, len(peers))

    def own(kind, l, h):
        ref = shard[kind]
        half = ref.shape[1] // 2
        return ref.at[l, pl.ds(h * half, half)]

    def block(kind, l, h, row, col):
        if kind in ("qkv", "up"):
            return full[kind].at[l, col, row, h]
        start = pl.multiple_of(row * depth, depth)
        return full[kind].at[l, col, h, :, pl.ds(start, depth)]

    def strip(kind, l, h, col):
        if kind in ("qkv", "up"):
            return full[kind].at[l, col, :, h]
        return full[kind].at[l, col, h]

    def amount(kind, l, h, strips, rows):
        if kind in ("qkv", "up"):
            return full[kind].at[l, pl.ds(0, strips), pl.ds(0, rows), h]
        return full[kind].at[l, pl.ds(0, strips), h, :, pl.ds(0, rows * depth)]

    chunks = []
    for l in range(layers):
        for kind in KINDS:
            for h in range(2):
                order = []
                for d in ORDERS[kind][h]:
                    if d == "z":
                        order.append("z")
                    elif d < len(link_bits):
                        order.append(link_bits[d])
                order += link_bits[2:]
                chunks.append((kind, l, h, tuple(order)))
    phases = len(link_bits) + 1

    def plan(order):
        masks, whole, steps = [0], False, []
        for d in order:
            steps.append((d, tuple(masks), whole))
            if d == "z":
                whole = True
            else:
                masks = masks + [m ^ d for m in masks]
        steps.append((None, tuple(masks), whole))
        return steps

    def remote(src, dst, k, p, peer):
        return pltpu.make_async_remote_copy(
            src_ref=src, dst_ref=dst, send_sem=send_sem.at[k, p], recv_sem=recv_sem.at[k, p],
            device_id=peer, device_id_type=MESH,
        )

    def local(k):
        kind, l, h, _ = chunks[k]
        return pltpu.make_async_copy(own(kind, l, h), block(kind, l, h, r, c), local_sem.at[k])

    def issue(k, p):
        kind, l, h, order = chunks[k]
        d, masks, whole = plan(order)[p]
        for m in masks:
            if d == "z":
                src = own(kind, l, h) if m == 0 else block(kind, l, h, r, c ^ m)
                for s in range(1, n_row):
                    remote(src, block(kind, l, h, r, c ^ m), k, p, row_peer(s)).start()
            elif whole:
                ref = strip(kind, l, h, c ^ m)
                remote(ref, ref, k, p, col_peer(d)).start()
            else:
                src = own(kind, l, h) if m == 0 else block(kind, l, h, r, c ^ m)
                remote(src, block(kind, l, h, r, c ^ m), k, p, col_peer(d)).start()

    def moved(k, p):
        kind, l, h, order = chunks[k]
        d, masks, whole = plan(order)[p]
        if d == "z":
            rows = n_row - 1
        else:
            rows = n_row if whole else 1
        ref = amount(kind, l, h, len(masks), rows)
        return remote(ref, ref, k, p, col_peer(1))

    def share(k, p):
        kind, l, h, order = chunks[k]
        steps = plan(order)
        (d, masks, _), (_, later, whole) = steps[p], steps[p + 1]
        if not whole:
            return
        fresh = masks if d == "z" else later[len(masks):]
        for m in fresh:
            ref = strip(kind, l, h, c ^ m)
            remote(ref, ref, k, phases, col_peer(1)).start()

    def shared(k):
        kind, l, h, _ = chunks[k]
        ref = amount(kind, l, h, n_col // 2, n_row)
        return remote(ref, ref, k, phases, col_peer(1))

    def finish(k, p):
        moved(k, p).wait_recv()
        if chunks[k][3][p] == "z":
            local(k).wait()
        if p + 1 < phases:
            issue(k, p + 1)
        share(k, p)

    count = len(chunks)
    for k in range(count):
        local(k).start()
    for t in range(count + WINDOW + phases):
        if t < count:
            issue(t, 0)
        for p in range(phases):
            k = t - WINDOW - p
            if 0 <= k < count:
                finish(k, p)
    for k in range(count):
        for p in range(phases):
            moved(k, p).wait_send()
        shared(k).wait_send()
        shared(k).wait_recv()


def gather_weights(n_row, n_col, qkv, proj, up, down):
    layers, depth = up.shape[0], up.shape[1]
    width, units = proj.shape[1], down.shape[1]
    dim = depth * n_row
    shapes = (
        (layers, n_col, n_row, 2, depth // 2, qkv.shape[2]),
        (layers, n_col, 2, width // 2, dim),
        (layers, n_col, n_row, 2, depth // 2, units),
        (layers, n_col, 2, units // 2, dim),
    )
    count = layers * 8
    phases = n_col.bit_length()
    outs = pl.pallas_call(
        functools.partial(gather_body, n_row, n_col, layers),
        out_shape=[jax.ShapeDtypeStruct(s, BF16) for s in shapes],
        in_specs=[pl.BlockSpec(memory_space=pltpu.HBM)] * 4,
        out_specs=[pl.BlockSpec(memory_space=pltpu.HBM)] * 4,
        scratch_shapes=[
            pltpu.SemaphoreType.DMA((count,)),
            pltpu.SemaphoreType.DMA((count, phases)),
            pltpu.SemaphoreType.DMA((count, phases)),
        ],
        compiler_params=pltpu.CompilerParams(collective_id=0, has_side_effects=True),
        name="gather_weights",
    )(qkv, proj, up, down)
    return (
        outs[0].reshape(layers, n_col, dim, qkv.shape[2]),
        outs[1].reshape(layers, dim, dim),
        outs[2].reshape(layers, n_col, dim, units),
        outs[3].reshape(layers, units * n_col, dim),
    )


def dot(a, b, dims=((1,), (0,))):
    return lax.dot_general(a, b, (dims, ((), ())), preferred_element_type=F32)


def norm_forward(stream, gain, shift):
    center = stream - jnp.mean(stream, axis=1, keepdims=True)
    inverse = lax.rsqrt(jnp.mean(center * center, axis=1, keepdims=True) + EPSILON)
    scaled = center * inverse
    return (scaled * gain + shift).astype(BF16), scaled, inverse


def norm_backward(grad, scaled, inverse, gain):
    w = grad * gain
    first = jnp.mean(w, axis=1, keepdims=True)
    second = jnp.mean(w * scaled, axis=1, keepdims=True)
    return inverse * (w - first - scaled * second)


def positions(group):
    if group == 2:
        return ((0, 3), (1, 2))
    per = BLOCKS // group
    return tuple(tuple(range(g * per, (g + 1) * per)) for g in range(group))


def shards(mesh_shape, *args):
    (
        tokens, cotangent, adapter_ids, qkv_weight, qkv_bias, proj_weight, proj_bias,
        up_weight, up_bias, down_weight, down_bias, first_gain, first_shift, second_gain,
        second_shift, qkv_lower, qkv_raise, proj_lower, proj_raise, up_lower, up_raise,
        down_lower, down_raise,
    ) = args
    n_row, n_col = mesh_shape
    layers, adapters, dim, rank = qkv_lower.shape
    rows, width = tokens.shape
    units = up_weight.shape[2]
    seqs = rows // LEN
    group = n_col // seqs
    held = positions(group)
    per = BLOCKS // group
    mine = per * BLOCK
    heads = width // HD
    c = lax.axis_index("col")
    g = lax.rem(c, group)
    seq = c // group

    qkv_full, proj_full, up_full, down_full = gather_weights(
        n_row, n_col, qkv_weight.reshape(layers, -1, 3 * width), proj_weight, up_weight, down_weight
    )

    def vectors(v):
        return lax.all_gather(v, "col", axis=v.ndim - 1, tiled=True).astype(F32)

    qkv_b = lax.all_gather(qkv_bias, "col", axis=0).astype(F32)
    proj_b, up_b, down_b, gain1, shift1, gain2, shift2 = [
        vectors(v)
        for v in (proj_bias, up_bias, down_bias, first_gain, first_shift, second_gain, second_shift)
    ]

    order = [s * BLOCKS + b for s in range(seqs) for q in range(group) for b in held[q]]
    back = [order.index(i) for i in range(len(order))]

    def to_own(x):
        x = x.reshape(seqs * BLOCKS, BLOCK, width)
        x = jnp.concatenate([x[i] for i in order], axis=0)
        return lax.all_to_all(x, "col", split_axis=0, concat_axis=1, tiled=True)

    def to_columns(x):
        x = lax.all_to_all(x.astype(BF16), "col", split_axis=1, concat_axis=0, tiled=True)
        x = x.reshape(seqs * BLOCKS, BLOCK, width)
        return jnp.concatenate([x[i] for i in back], axis=0).astype(F32)

    def peer_values(x, step):
        pairs = [(q, q - q % group + (q + step) % group) for q in range(n_col)]
        return lax.ppermute(x, "col", pairs)

    table = jnp.asarray(held, jnp.int32)
    own_place = table[g]
    key_place = jnp.concatenate([table[lax.rem(g - s + group, group)] for s in range(group)])
    allowed = key_place[None, :] <= own_place[:, None]
    mask = jnp.repeat(jnp.repeat(allowed, BLOCK, axis=0), BLOCK, axis=1)

    ids = lax.dynamic_index_in_dim(adapter_ids, seq, 0, keepdims=False)

    def picked(tab, l, site):
        return lax.dynamic_index_in_dim(tab[l], ids[site], 0, keepdims=False)

    def attend(q, k, v):
        s = jnp.einsum("hqd,hkd->hqk", q, k, preferred_element_type=F32) * SCALE
        s = jnp.where(mask, s, -1e30)
        top = jnp.max(s, axis=2, keepdims=True)
        e = jnp.exp(s - top)
        total = jnp.sum(e, axis=2, keepdims=True)
        out = jnp.einsum("hqk,hkd->hqd", (e / total).astype(BF16), v, preferred_element_type=F32)
        return out.astype(BF16), (top + jnp.log(total))

    def attend_back(q, k, v, lse, grad):
        s = jnp.einsum("hqd,hkd->hqk", q, k, preferred_element_type=F32) * SCALE
        p = jnp.exp(jnp.where(mask, s, -1e30) - lse)
        gp = jnp.einsum("hqd,hkd->hqk", grad, v, preferred_element_type=F32)
        gv = jnp.einsum("hqk,hqd->hkd", p.astype(BF16), grad, preferred_element_type=F32)
        gs = (p * (gp - jnp.sum(p * gp, axis=2, keepdims=True))).astype(BF16)
        gq = jnp.einsum("hqk,hkd->hqd", gs, k, preferred_element_type=F32) * SCALE
        gk = jnp.einsum("hqk,hqd->hkd", gs, q, preferred_element_type=F32) * SCALE
        return gq, gk, gv

    def by_head(x):
        t = x.shape[1]
        return x.reshape(n_col, t, heads, HD).transpose(0, 2, 1, 3).reshape(n_col * heads, t, HD)

    def by_strip(x):
        t = x.shape[1]
        return x.reshape(n_col, heads, t, HD).transpose(0, 2, 1, 3).reshape(n_col, t, width)

    stream = to_own(tokens).astype(F32)
    records = []
    for l in range(layers):
        rec = {}
        a_qkv, b_qkv = picked(qkv_lower, l, 0), picked(qkv_raise, l, 0)
        a_proj, b_proj = picked(proj_lower, l, 1), picked(proj_raise, l, 1)
        a_up, b_up = picked(up_lower, l, 2), picked(up_raise, l, 2)
        a_down, b_down = picked(down_lower, l, 3), picked(down_raise, l, 3)
        b_qkv = b_qkv.reshape(rank, 3, n_col, width).transpose(2, 0, 1, 3).reshape(n_col, rank, 3 * width)
        b_up = b_up.reshape(rank, n_col, units).transpose(1, 0, 2)
        rec["picks"] = (a_qkv, b_qkv, a_proj, b_proj, a_up, b_up, a_down, b_down)
        rec["normed"], rec["n1"], rec["r1"] = norm_forward(stream, gain1[l], shift1[l])
        rec["reduced"] = dot(rec["normed"], a_qkv).astype(BF16)
        mixed = (
            jnp.einsum("tk,ckn->ctn", rec["normed"], qkv_full[l], preferred_element_type=F32)
            + qkv_b[:, l].reshape(n_col, 1, 3 * width)
            + jnp.einsum("tk,ckn->ctn", rec["reduced"], b_qkv, preferred_element_type=F32)
        ).astype(BF16)
        q, kv = mixed[:, :, :width], mixed[:, :, width:]
        kvs = jnp.concatenate([kv] + [peer_values(kv, s) for s in range(1, group)], axis=1)
        rec["q"], rec["k"], rec["v"] = by_head(q), by_head(kvs[:, :, :width]), by_head(kvs[:, :, width:])
        attended, rec["lse"] = attend(rec["q"], rec["k"], rec["v"])
        attended = by_strip(attended).transpose(1, 0, 2).reshape(mine, dim)
        rec["attended"] = attended
        rec["reduced_proj"] = dot(attended, a_proj).astype(BF16)
        middle = stream + dot(attended, proj_full[l]) + proj_b[l] + dot(rec["reduced_proj"], b_proj)
        rec["normed2"], rec["n2"], rec["r2"] = norm_forward(middle, gain2[l], shift2[l])
        rec["reduced_up"] = dot(rec["normed2"], a_up).astype(BF16)
        rec["hidden"] = (
            jnp.einsum("tk,ckn->ctn", rec["normed2"], up_full[l], preferred_element_type=F32)
            + up_b[l].reshape(n_col, 1, units)
            + jnp.einsum("tk,ckn->ctn", rec["reduced_up"], b_up, preferred_element_type=F32)
        )
        rec["active"] = jax.nn.gelu(rec["hidden"], approximate=True).astype(BF16)
        a_down_c = a_down.reshape(n_col, units, rank)
        rec["reduced_down"] = jnp.einsum(
            "ctn,cnk->tk", rec["active"], a_down_c, preferred_element_type=F32
        ).astype(BF16)
        stream = (
            middle
            + jnp.einsum(
                "ctn,cnk->tk", rec["active"], down_full[l].reshape(n_col, units, dim),
                preferred_element_type=F32,
            )
            + down_b[l]
            + dot(rec["reduced_down"], b_down)
        )
        records.append(rec)
    result = to_columns(stream)

    grad = to_own(cotangent).astype(F32)
    grads = [None] * layers
    cross = ((0,), (0,))
    turned = ((1,), (1,))
    for l in reversed(range(layers)):
        rec = records[l]
        a_qkv, b_qkv, a_proj, b_proj, a_up, b_up, a_down, b_down = rec["picks"]
        low = grad.astype(BF16)
        g_red_down = dot(low, b_down, turned).astype(BF16)
        g_b_down = dot(rec["reduced_down"], low, cross)
        g_a_down = jnp.einsum("tk,ctn->ckn", g_red_down, rec["active"], preferred_element_type=F32)
        g_active = jnp.einsum(
            "tk,cnk->ctn", low, down_full[l].reshape(n_col, units, dim), preferred_element_type=F32
        ) + jnp.einsum(
            "tk,cnk->ctn", g_red_down, a_down.reshape(n_col, units, rank), preferred_element_type=F32
        )
        g_hidden = jax.vjp(lambda x: jax.nn.gelu(x, approximate=True), rec["hidden"])[1](g_active)[0]
        g_hidden = g_hidden.astype(BF16)
        g_red_up = jnp.einsum("ctn,ckn->tk", g_hidden, b_up, preferred_element_type=F32).astype(BF16)
        g_b_up = jnp.einsum("tk,ctn->ckn", rec["reduced_up"], g_hidden, preferred_element_type=F32)
        g_a_up = dot(g_red_up, rec["normed2"], cross)
        g_normed2 = jnp.einsum("ctn,ckn->tk", g_hidden, up_full[l], preferred_element_type=F32) + dot(
            g_red_up, a_up, turned
        )
        grad = grad + norm_backward(g_normed2, rec["n2"], rec["r2"], gain2[l])
        low = grad.astype(BF16)
        g_red_proj = dot(low, b_proj, turned).astype(BF16)
        g_b_proj = dot(rec["reduced_proj"], low, cross)
        g_a_proj = dot(g_red_proj, rec["attended"], cross)
        g_att = (dot(low, proj_full[l], turned) + dot(g_red_proj, a_proj, turned)).astype(BF16)
        g_att = by_head(g_att.reshape(mine, n_col, width).transpose(1, 0, 2))
        gq, gk, gv = attend_back(rec["q"], rec["k"], rec["v"], rec["lse"], g_att)
        gkv = jnp.concatenate([by_strip(gk), by_strip(gv)], axis=2)
        total = gkv[:, :mine]
        for s in range(1, group):
            part = gkv[:, s * mine : (s + 1) * mine].astype(BF16)
            total = total + peer_values(part, group - s).astype(F32)
        g_mixed = jnp.concatenate([by_strip(gq), total], axis=2).astype(BF16)
        g_red = jnp.einsum("ctn,ckn->tk", g_mixed, b_qkv, preferred_element_type=F32).astype(BF16)
        g_b_qkv = jnp.einsum("tk,ctn->ckn", rec["reduced"], g_mixed, preferred_element_type=F32)
        g_a_qkv = dot(g_red, rec["normed"], cross)
        g_normed = jnp.einsum("ctn,ckn->tk", g_mixed, qkv_full[l], preferred_element_type=F32) + dot(
            g_red, a_qkv, turned
        )
        grad = grad + norm_backward(g_normed, rec["n1"], rec["r1"], gain1[l])

        def strips(x):
            return x.reshape(rank, n_col, -1).transpose(1, 0, 2)

        grads[l] = jnp.concatenate(
            [
                strips(g_a_qkv), g_b_qkv, strips(g_a_proj), strips(g_b_proj),
                strips(g_a_up), g_b_up, g_a_down, strips(g_b_down),
            ],
            axis=2,
        )
    input_grad = to_columns(grad)

    sizes = (width, 3 * width, width, width, width, units, units, width)
    sites = (0, 0, 1, 1, 2, 2, 3, 3)
    parts = jnp.stack(grads, axis=1).astype(BF16)
    parts = lax.all_to_all(parts, "col", split_axis=0, concat_axis=0, tiled=True)
    parts = parts.reshape((seqs, group) + parts.shape[1:]).astype(F32).sum(axis=1)
    onehot = (adapter_ids.T[:, :, None] == jnp.arange(adapters)[None, None, :]).astype(F32)
    placed, at = [], 0
    for size, site in zip(sizes, sites):
        piece = parts[:, :, :, at : at + size]
        at += size
        placed.append(
            jnp.einsum("sa,slrn->larn", onehot[site], piece, precision=lax.Precision.HIGHEST)
        )
    summed = lax.psum([p.astype(BF16) for p in placed], "row")
    outs = []
    for number, p in enumerate(summed):
        p = p.astype(F32)
        if number == 1:
            outs.append(p.reshape(layers, adapters, rank, 3, width))
        elif number in (0, 2, 4, 6):
            outs.append(p.transpose(0, 1, 3, 2))
        else:
            outs.append(p)
    return (result, input_grad) + tuple(outs)


def solution(mesh):
    mesh_shape = (mesh.shape["row"], mesh.shape["col"])
    return jax.shard_map(
        functools.partial(shards, mesh_shape),
        mesh=mesh,
        in_specs=(
            P("row", "col"), P("row", "col"), P("row", None),
            P(None, "row", None, "col"), P(None, None, "col"),
            P(None, "col", "row"), P(None, "col"),
            P(None, "row", "col"), P(None, "col"),
            P(None, "col", "row"), P(None, "col"),
            P(None, "col"), P(None, "col"), P(None, "col"), P(None, "col"),
            P(), P(), P(), P(), P(), P(), P(), P(),
        ),
        out_specs=(
            P("row", "col"), P("row", "col"),
            P(None, None, "col", None), P(None, None, None, None, "col"),
            P(None, None, "col", None), P(None, None, None, "col"),
            P(None, None, "col", None), P(None, None, None, "col"),
            P(None, None, "col", None), P(None, None, None, "col"),
        ),
        check_vma=False,
    )
```

time: 1960 us -> 1180 us (0.60)
  waiting for transfers between devices: 602 us -> 70.2 us
  blocking collectives: 449 us -> 68.2 us
  Pallas kernels: 0 us -> 306 us
  local copies, waits for them, and re-layouts: 312 us -> 191 us
  matrix products: 414 us -> 359 us
  starting transfers between devices: 1.46 us -> 23.5 us
    psum x15 -> x0, blocking collectives: 384 us -> none  [column_sums(): return lax.psum(values, 'col')]
    all_gather x12 -> x0, waiting for transfers between devices: 332 us -> none  [the longest x4 147 us: spread_grads(): return lax.all_gather(values, 'col', axis=1, tiled=True)]
    pallas_call x0 -> x1, Pallas kernels: none -> 306 us  [gather_weights(): pl.pallas_call(functools.partial(gather_body, n_row, n_col, layers), out_...]
    unnamed x29 -> x1, waiting for transfers between devices: 217 us -> 0.02 us
    unnamed x325 -> x385, local copies, waits for them, and re-layouts: 145 us -> 63.7 us
    dot_general x152 -> x84, matrix products: 414 us -> 359 us  [the longest x2 58.6 us: attend_back(): gp = jnp.einsum('hqd,hkd->hqk', grad, v, preferred_element_type=F32)]
    while x24 -> x0, local copies, waits for them, and re-layouts: 44.7 us -> none  [the longest x4 32.8 us: shards(): attended, stored['sums_log'] = lax.map(attend_block, stored['packed'])]
    slice x15 -> x26, local copies, waits for them, and re-layouts: 19.7 us -> 46.8 us  [the longest x1 11.7 us: shards(): up_full[l]]
  transfers between devices with their start and end apart: 21 -> 10, of which waited for: 19 -> 3; matrix products, arithmetic and copies ran while one was open for 20% -> 17% of each run, Pallas kernels for 0% -> 26%
where the time goes in v1:
time: 1180 us; the launch traced here: 1170 us
  matrix products  359 us (30%)
  Pallas kernels  306 us (26%)
  local copies, waits for them, and re-layouts  191 us (16%)
  other arithmetic  127 us (11%)
  waiting for transfers between devices  70.2 us (6%)
  blocking collectives  68.2 us (6%)
  between operations  24.7 us (2%)
  starting transfers between devices  23.5 us (2%)
    pallas_call x1, Pallas kernels, gather_weights(): pl.pallas_call(functools.partial(gather_body, n_row, n_col, layers), out_...  306 us
    unnamed x385, local copies, waits for them, and re-layouts  63.7 us
    all_gather x7, blocking collectives, vectors(): return lax.all_gather(v, 'col', axis=v.ndim - 1, tiled=True).astype(F32)  59.4 us
    dot_general x2, matrix products, attend_back(): gp = jnp.einsum('hqd,hkd->hqk', grad, v, preferred_element_type=F32)  58.6 us
    convert_element_type x2, other arithmetic, attend_back(): gs = (p * (gp - jnp.sum(p * gp, axis=2, keepdims=True))).astype(BF16)  55.7 us
    psum x1, waiting for transfers between devices, shards(): summed = lax.psum([p.astype(BF16) for p in placed], 'row')  53.9 us
    dot_general x34, matrix products, dot(): return lax.dot_general(a, b, (dims, ((), ())), preferred_element_type=F32)  37.9 us
    dot_general x2, matrix products, attend(): s = jnp.einsum('hqd,hkd->hqk', q, k, preferred_element_type=F32) * SCALE  33.5 us
  transfers between devices with their start and end apart: 10, of which 3 were waited for; matrix products, arithmetic and copies ran while one was open for 17% of the time, Pallas kernels for 26%

profile of v1, /device:TPU:0, one launch (start us, length us, event | category | flops | bytes accessed | tf_op | source)
XLA Modules:
  0.0 1170.0 jit_solution(13944891708945323779)
XLA Ops:
  25.3 5.2 all-to-all-start
  38.2 10.7 all_gather.28
  49.5 7.8 all_gather.27
  57.9 8.8 all-gather
  75.8 7.8 all_gather.31
  84.2 8.7 all_gather.33
  93.5 7.8 all_gather.32
  105.8 306.0 %gather_weights.1 = (bf16[2,8,4,2,128,384]{5,4,3,2,1,0:T(8,128)(2,1)}, bf16[2,8,2,64,1024]{4,3,2,1,0:T(8,128)(2,1)}, bf16[2,8,4,2,128,512]{5,4,3,2,1,0:T(8,128)(2,1)}, bf16[2,8,2,256,1024]{4,3,2,1,0:T(8,128)(2,1)}) custom-call(bf16[2,256,384]{2,1,0:T(8,128)(2,1)} %copy.336.refs_0_, bf16[2,128,256]{2,1,0:T(8,128)(2,1)} %refs_1_.1, ...), custom_call_target="tpu_custom_call" | custom-call | tf_op jit(solution)/shard_map/gather_weights/pallas_call | solution.py:187
  411.9 11.7 fusion.263
  423.5 8.0 all_gather.34
  437.1 8.7 all_gather.35
  462.7 10.7 fusion.264
  473.4 4.8 all-to-all-start.2
  479.7 5.8 fusion.293
  489.4 6.6 fusion.262
  522.8 16.7 %fusion.288 = (f32[16,512]{1,0:T(8,128)S(1)}, f32[16,512,1024]{2,1,0:T(8,128)}) fusion(bf16[16,1024,64]{1,0,2:T(8,128)(2,1)S(1)} %reshape.508, bf16[16,512,64]{1,0,2:T(8,128)(2,1)S(1)} %copy-done.19, pred[512,1024]{1,0:T(8,128)(4,1)} %bitcast.801), kind=kOutput, calls=%fused_computation.550 | convolution fusion | flops 1098899456 | bytes 37257216 | tf_op jit(solution)/shard_map/hqd,hkd->hqk/dot_general | solution.py:296
  539.5 14.4 %fusion = f32[16,512]{1,0:T(8,128)S(1)} fusion(f32[16,512,1024]{2,1,0:T(8,128)} %get-tuple-element.155, f32[16,512]{1,0:T(8,128)S(1)} %get-tuple-element.154), kind=kLoop, calls=%fused_computation.12 | loop fusion | flops 16769024 | bytes 33619968 | tf_op jit(solution)/shard_map/reduce_sum | solution.py:300
  554.0 13.8 %fusion.70 = bf16[16,512,64]{1,2,0:T(8,128)(2,1)S(1)} fusion(bf16[16,1024,64]{1,0,2:T(8,128)(2,1)S(1)} %copy-done.31, f32[16,512,1024]{2,1,0:T(8,128)} %get-tuple-element.155, f32[16,512]{1,0:T(8,128)S(1)} %fusion, f32[16,512]{1,0:T(8,128)S(1)} %get-tuple-element.154), kind=kOutput, calls=%fused_computation.153 | convolution fusion | flops 1099431936 | bytes 36765696 | tf_op jit(solution)/shard_map/hqk,hkd->hqd/dot_general | solution.py:301
  574.6 4.6 fusion.141
  579.3 6.0 fusion.33
  607.3 11.6 fusion.298
  638.2 16.7 %fusion.291 = (f32[16,512]{1,0:T(8,128)S(1)}, f32[16,512,1024]{2,1,0:T(8,128)}) fusion(bf16[16,1024,64]{1,0,2:T(8,128)(2,1)S(1)} %reshape.518, bf16[16,512,64]{1,0,2:T(8,128)(2,1)S(1)} %reshape.517, pred[512,1024]{1,0:T(8,128)(4,1)} %bitcast.802), kind=kOutput, calls=%fused_computation.553 | convolution fusion | flops 1098899456 | bytes 37257216 | tf_op jit(solution)/shard_map/hqd,hkd->hqk/dot_general | solution.py:296
  654.9 14.4 %fusion.1 = f32[16,512]{1,0:T(8,128)S(1)} fusion(f32[16,512,1024]{2,1,0:T(8,128)} %get-tuple-element.163, f32[16,512]{1,0:T(8,128)S(1)} %get-tuple-element.162), kind=kLoop, calls=%fused_computation.13 | loop fusion | flops 16769024 | bytes 33619968 | tf_op jit(solution)/shard_map/reduce_sum | solution.py:300
  669.4 13.6 %fusion.67 = bf16[16,512,64]{1,2,0:T(8,128)(2,1)S(1)} fusion(bf16[16,1024,64]{1,0,2:T(8,128)(2,1)S(1)} %copy-done.32, f32[16,512,1024]{2,1,0:T(8,128)} %get-tuple-element.163, f32[16,512]{1,0:T(8,128)S(1)} %fusion.1, f32[16,512]{1,0:T(8,128)S(1)} %get-tuple-element.162), kind=kOutput, calls=%fused_computation.152 | convolution fusion | flops 1099431936 | bytes 36765696 | tf_op jit(solution)/shard_map/hqk,hkd->hqd/dot_general | solution.py:301
  689.8 7.5 fusion.137
  697.3 7.9 fusion.32
  705.2 5.8 fusion.297
  711.7 10.2 fusion.25
  740.5 29.3 %multiply_reduce_fusion.1 = (f32[16,512]{1,0:T(8,128)S(1)}, f32[16,512,1024]{2,1,0:T(8,128)}) fusion(f32[16,512,1024]{2,1,0:T(8,128)} %get-tuple-element.163, f32[16,512]{1,0:T(8,128)S(1)} %log_add_fusion.1, bf16[16,1024,64]{1,0,2:T(8,128)(2,1)} %reshape.519, bf16[16,512,64]{1,0,2:T(8,128)(2,1)S(1)} %reshape.527), kind=kOutput, calls=%fused_computation.4 | convolution fusion | flops 1098899456 | bytes 70320128 | tf_op jit(solution)/shard_map/hqd,hkd->hqk/dot_general | solution.py:307
  769.8 15.5 %fusion.6 = f32[16,1024,64]{1,2,0:T(8,128)} fusion(f32[16,512,1024]{2,1,0:T(8,128)} %get-tuple-element.163, f32[16,512]{1,0:T(8,128)S(1)} %log_add_fusion.1, bf16[16,512,64]{1,0,2:T(8,128)(2,1)S(1)} %reshape.527), kind=kOutput, calls=%fused_computation.17 | convolution fusion | flops 1090519040 | bytes 38830080 | tf_op jit(solution)/shard_map/hqk,hqd->hkd/dot_general | solution.py:308
  793.6 27.9 %multiply_convert_fusion.1 = bf16[16,512,1024]{2,1,0:T(8,128)(2,1)} fusion(f32[16,512,1024]{2,1,0:T(8,128)} %get-tuple-element.170, f32[16,512,1024]{2,1,0:T(8,128)} %get-tuple-element.163, f32[16,512]{1,0:T(8,128)S(1)} %get-tuple-element.169, f32[16,512]{1,0:T(8,128)S(1)} %log_add_fusion.1), kind=kLoop, calls=%fused_computation.3 | loop fusion | flops 33554432 | bytes 83951616 | tf_op jit(solution)/shard_map/convert_element_type | solution.py:309
  821.5 11.2 convolution_multiply_fusion.1
  832.7 5.3 copy.379
  838.0 5.3 copy.380
  847.8 8.5 multiply_convert_fusion.3
  865.7 6.8 fusion.260
  873.2 7.7 fusion.135
  882.1 8.7 fusion.18
  909.3 29.3 %multiply_reduce_fusion = (f32[16,512]{1,0:T(8,128)S(1)}, f32[16,512,1024]{2,1,0:T(8,128)}) fusion(f32[16,512,1024]{2,1,0:T(8,128)} %get-tuple-element.155, f32[16,512]{1,0:T(8,128)S(1)} %copy-done.54, bf16[16,1024,64]{1,0,2:T(8,128)(2,1)} %reshape.509, bf16[16,512,64]{1,0,2:T(8,128)(2,1)S(1)} %reshape.535), kind=kOutput, calls=%fused_computation.1 | convolution fusion | flops 1098899456 | bytes 70320128 | tf_op jit(solution)/shard_map/hqd,hkd->hqk/dot_general | solution.py:307
  938.5 15.4 %fusion.4 = f32[16,1024,64]{1,2,0:T(8,128)} fusion(f32[16,512,1024]{2,1,0:T(8,128)} %get-tuple-element.155, f32[16,512]{1,0:T(8,128)S(1)} %copy-done.54, bf16[16,512,64]{1,0,2:T(8,128)(2,1)S(1)} %reshape.535), kind=kOutput, calls=%fused_computation.16 | convolution fusion | flops 1090519040 | bytes 38830080 | tf_op jit(solution)/shard_map/hqk,hqd->hkd/dot_general | solution.py:308
  954.0 27.8 %multiply_convert_fusion = bf16[16,512,1024]{2,1,0:T(8,128)(2,1)} fusion(f32[16,512,1024]{2,1,0:T(8,128)} %get-tuple-element.174, f32[16,512,1024]{2,1,0:T(8,128)} %get-tuple-element.155, f32[16,512]{1,0:T(8,128)S(1)} %get-tuple-element.173, f32[16,512]{1,0:T(8,128)S(1)} %copy-done.54), kind=kLoop, calls=%fused_computation | loop fusion | flops 33554432 | bytes 83951616 | tf_op jit(solution)/shard_map/convert_element_type | solution.py:309
  981.8 11.3 convolution_multiply_fusion
  993.2 9.8 multiply_convert_fusion.2
  1003.9 5.3 copy.391
  1009.3 5.3 copy.392
  1060.4 6.9 all-to-all-done.4
  1076.9 9.4 all-to-all-done.3
  1096.1 53.9 %all-reduce.3.cloned.1.call-done = (bf16[2,8,128,16]{2,1,3,0:T(8,128)(2,1)}, bf16[2,8,128,16]{2,1,3,0:T(8,128)(2,1)}, bf16[2,8,16,128]{3,1,2,0:T(8,128)(2,1)}, b...) async-done(((bf16[2,8,128,16]{2,1,3,0:T(8,128)(2,1)}, ...) | async-done | bytes 1048592 | tf_op jit(solution)/shard_map/psum | solution.py:443
  (604 shorter events, 282.2 us)
Async XLA Ops:
  7.2 29.9 %copy-start.74 = (bf16[2,256,3,128]{3,1,2,0:T(8,128)(2,1)S(1)}, bf16[2,256,3,128]{3,1,2,0:T(8,128)(2,1)}, u32[]{:S(2)}) copy-start(bf16[2,256,3,128]{3,1,2,0:T(8,128)(2,1)} %param.27) | copy-start | bytes 1179652
  7.2 31.0 %copy-start.128 = (bf16[2,128]{1,0:T(2,128)(2,1)S(1)}, bf16[2,128]{1,0:T(2,128)(2,1)}, u32[]{:S(2)}) copy-start(bf16[2,128]{1,0:T(2,128)(2,1)} %param.36) | copy-start | bytes 1540
  7.2 42.3 %copy-start.129 = (bf16[2,128]{1,0:T(2,128)(2,1)S(1)}, bf16[2,128]{1,0:T(2,128)(2,1)}, u32[]{:S(2)}) copy-start(bf16[2,128]{1,0:T(2,128)(2,1)} %param.35) | copy-start | bytes 1540
  7.2 50.7 %copy-start.127 = (bf16[2,3,128]{2,0,1:T(2,128)(2,1)S(1)}, bf16[2,3,128]{2,0,1:T(2,128)(2,1)}, u32[]{:S(2)}) copy-start(bf16[2,3,128]{2,0,1:T(2,128)(2,1)} %param.28) | copy-start | bytes 4612
  25.3 448.1 %all-to-all-start = ((bf16[8,512,128]{2,1,0:T(8,128)(2,1)}), bf16[8,512,128]{2,1,0:T(8,128)(2,1)S(1)}, u32[]{:S(2)}, u32[]{:S(2)}) async-start(bf16[8,512,128]{2,1,0:T(8,128)(2,1)} %bitcast), calls=%async_computation | async-start | bytes 2097152 | tf_op jit(solution)/shard_map/all_to_all | solution.py:273
  30.5 39.9 %copy-start.66 = (bf16[2,8,1024,16]{2,3,1,0:T(8,128)(2,1)S(1)}, bf16[2,8,1024,16]{2,3,1,0:T(8,128)(2,1)}, u32[]{:S(2)}) copy-start(bf16[2,8,1024,16]{2,3,1,0:T(8,128)(2,1)} %param.39) | copy-start | bytes 1572868
  37.2 34.0 %copy-start.125 = (s32[2,2]{1,0:T(2,128)S(1)}, s32[2,2]{1,0:T(2,128)}, u32[]{:S(2)}) copy-start(s32[2,2]{1,0:T(2,128)} %constant.136.clone) | copy-start | bytes 52
  49.5 429.8 %copy-start.96 = (f32[1,1024]{1,0:T(1,128)}, f32[1,1024]{1,0:T(1,128)S(1)}, u32[]{:S(2)}) copy-start(f32[1,1024]{1,0:T(1,128)S(1)} %get-tuple-element.146) | copy-start | bytes 12292
  57.9 421.4 %copy-start.98 = (f32[1,1024]{1,0:T(1,128)}, f32[1,1024]{1,0:T(1,128)S(1)}, u32[]{:S(2)}) copy-start(f32[1,1024]{1,0:T(1,128)S(1)} %get-tuple-element.144) | copy-start | bytes 12292
  68.9 15.4 %copy-start.131 = (bf16[2,128]{1,0:T(2,128)(2,1)S(1)}, bf16[2,128]{1,0:T(2,128)(2,1)}, u32[]{:S(2)}) copy-start(bf16[2,128]{1,0:T(2,128)(2,1)} %param.38) | copy-start | bytes 1540
  68.9 24.6 %copy-start.132 = (bf16[2,128]{1,0:T(2,128)(2,1)S(1)}, bf16[2,128]{1,0:T(2,128)(2,1)}, u32[]{:S(2)}) copy-start(bf16[2,128]{1,0:T(2,128)(2,1)} %param.37) | copy-start | bytes 1540
  70.4 416.1 %copy-start.70 = (bf16[8,16,384]{2,1,0:T(8,128)(2,1)}, bf16[8,16,384]{2,1,0:T(8,128)(2,1)S(1)}, u32[]{:S(2)}) copy-start(bf16[8,16,384]{2,1,0:T(8,128)(2,1)S(1)} %reshape.506) | copy-start | bytes 294916
  71.3 30.6 %copy-start.69 = (bf16[2,8,1024,16]{2,3,1,0:T(8,128)(2,1)S(1)}, bf16[2,8,1024,16]{2,3,1,0:T(8,128)(2,1)}, u32[]{:S(2)}) copy-start(bf16[2,8,1024,16]{2,3,1,0:T(8,128)(2,1)} %param.43) | copy-start | bytes 1572868
  101.9 471.0 %copy-start.100 = (f32[1,1024]{1,0:T(1,128)}, f32[1,1024]{1,0:T(1,128)S(1)}, u32[]{:S(2)}) copy-start(f32[1,1024]{1,0:T(1,128)S(1)} %get-tuple-element.138) | copy-start | bytes 12292
  411.9 11.7 copy-start.126
  434.6 21.0 %copy-start.55 = (bf16[4096,128]{1,0:T(8,128)(2,1)S(1)}, bf16[4096,128]{1,0:T(8,128)(2,1)}, u32[]{:S(2)}) copy-start(bf16[4096,128]{1,0:T(8,128)(2,1)} %param.25) | copy-start | bytes 3145732
  473.4 32.3 %all-to-all-start.2 = ((bf16[8,512,128]{2,1,0:T(8,128)(2,1)}), bf16[8,512,128]{2,1,0:T(8,128)(2,1)}, u32[]{:S(2)}, u32[]{:S(2)}) async-start(bf16[8,512,128]{2,1,0:T(8,128)(2,1)} %bitcast.108), calls=%async_computation.2 | async-start | bytes 2097152 | tf_op jit(solution)/shard_map/all_to_all | solution.py:273
  488.6 20.3 %collective-permute-start = (bf16[8,512,256]{1,2,0:T(8,128)(2,1)S(1)}, bf16[8,512,256]{1,2,0:T(8,128)(2,1)}, u32[]{:S(2)}, u32[]{:S(2)}) collective-permute-start(bf16[8,512,256]{1,2,0:T(8,128)(2,1)S(1)} %slice.649), channel_id=1, source_target_pairs={{0,1},{1,0},{2,3},{3,2},{4,5},{5,4},{6,7},{7,6},{8,9},{9,8},{10,11... | collective-permute-start | bytes 6291464 | tf_op jit(solution)/shard_map/ppermute | solution.py:282
  522.8 16.8 %copy-start.15 = (bf16[16,1024,64]{1,0,2:T(8,128)(2,1)}, bf16[16,1024,64]{1,0,2:T(8,128)(2,1)S(1)}, u32[]{:S(2)}) copy-start(bf16[16,1024,64]{1,0,2:T(8,128)(2,1)S(1)} %reshape.508) | copy-start | bytes 6291460
  539.5 14.4 %copy-start.31 = (bf16[16,1024,64]{1,0,2:T(8,128)(2,1)S(1)}, bf16[16,1024,64]{1,0,2:T(8,128)(2,1)}, u32[]{:S(2)}) copy-start(bf16[16,1024,64]{1,0,2:T(8,128)(2,1)} %reshape.509) | copy-start | bytes 6291460
  554.0 13.9 %copy-start.43 = (bf16[1,8,2,64,1024]{4,3,2,1,0:T(8,128)(2,1)S(1)}, bf16[1,8,2,64,1024]{4,3,2,1,0:T(8,128)(2,1)}, u32[]{:S(2)}) copy-start(bf16[1,8,2,64,1024]{4,3,2,1,0:T(8,128)(2,1)} %get-tuple-element.93) | copy-start | bytes 6291460
  572.5 18.0 %copy-start = (f32[512,1024]{1,0:T(8,128)}, f32[512,1024]{1,0:T(8,128)S(1)}, u32[]{:S(2)}) copy-start(f32[512,1024]{1,0:T(8,128)S(1)} %get-tuple-element.157) | copy-start | bytes 6291460
  602.0 22.1 %collective-permute-start.1 = (bf16[8,512,256]{1,2,0:T(8,128)(2,1)S(1)}, bf16[8,512,256]{1,2,0:T(8,128)(2,1)}, u32[]{:S(2)}, u32[]{:S(2)}) collective-permute-start(bf16[8,512,256]{1,2,0:T(8,128)(2,1)S(1)} %slice.666), channel_id=1, source_target_pairs={{0,1},{1,0},{2,3},{3,2},{4,5},{5,4},{6,7},{7,6},{8,9},{9,8},{10,11... | collective-permute-start | bytes 6291464 | tf_op jit(solution)/shard_map/ppermute | solution.py:282
  607.3 104.4 %copy-start.114 = (bf16[512,16,1]{0,1,2:T(8,128)(2,1)}, bf16[512,16,1]{0,1,2:T(8,128)(2,1)S(1)}, u32[]{:S(2)}) copy-start(bf16[512,16,1]{0,1,2:T(8,128)(2,1)S(1)} %fusion.123) | copy-start | bytes 49156
  623.3 14.8 %copy-start.21 = (bf16[16,512,64]{1,0,2:T(8,128)(2,1)}, bf16[16,512,64]{1,0,2:T(8,128)(2,1)S(1)}, u32[]{:S(2)}) copy-start(bf16[16,512,64]{1,0,2:T(8,128)(2,1)S(1)} %reshape.517) | copy-start | bytes 3145732
  638.2 16.7 %copy-start.17 = (bf16[16,1024,64]{1,0,2:T(8,128)(2,1)}, bf16[16,1024,64]{1,0,2:T(8,128)(2,1)S(1)}, u32[]{:S(2)}) copy-start(bf16[16,1024,64]{1,0,2:T(8,128)(2,1)S(1)} %reshape.518) | copy-start | bytes 6291460
  654.9 14.4 %copy-start.32 = (bf16[16,1024,64]{1,0,2:T(8,128)(2,1)S(1)}, bf16[16,1024,64]{1,0,2:T(8,128)(2,1)}, u32[]{:S(2)}) copy-start(bf16[16,1024,64]{1,0,2:T(8,128)(2,1)} %reshape.519) | copy-start | bytes 6291460
  669.4 14.9 %copy-start.45 = (bf16[1,8,2,64,1024]{4,3,2,1,0:T(8,128)(2,1)S(1)}, bf16[1,8,2,64,1024]{4,3,2,1,0:T(8,128)(2,1)}, u32[]{:S(2)}) copy-start(bf16[1,8,2,64,1024]{4,3,2,1,0:T(8,128)(2,1)} %get-tuple-element.92) | copy-start | bytes 6291460
  687.1 18.1 %slice-start.14 = ((s8[8388608]{0:T(1024)(128)(4,1)}), s8[4194304]{0:T(1024)(128)(4,1)S(1)}, s32[]{:S(2)}) async-start(s8[8388608]{0:T(1024)(128)(4,1)} %bitcast.831), calls=%async_computation.20 | async-start | bytes 8388608
  689.8 15.4 %slice-start.15 = ((s8[8388608]{0:T(1024)(128)(4,1)}), s8[4194304]{0:T(1024)(128)(4,1)S(1)}, s32[]{:S(2)}) async-start(s8[8388608]{0:T(1024)(128)(4,1)} %bitcast.831), calls=%async_computation.21 | async-start | bytes 8388608
  711.7 74.5 %copy-start.79 = (bf16[512,16]{0,1:T(8,128)(2,1)}, bf16[512,16]{0,1:T(8,128)(2,1)S(1)}, u32[]{:S(2)}) copy-start(bf16[512,16]{0,1:T(8,128)(2,1)S(1)} %fusion.117) | copy-start | bytes 49156
  769.8 15.5 %copy-start.11 = (f32[512,1024]{1,0:T(8,128)S(1)}, f32[512,1024]{1,0:T(8,128)}, u32[]{:S(2)}) copy-start(f32[512,1024]{1,0:T(8,128)} %copy-done.10) | copy-start | bytes 6291460
  769.8 16.4 %copy-start.120 = (f32[1,1024]{1,0:T(1,128)S(1)}, f32[1,1024]{1,0:T(1,128)}, u32[]{:S(2)}) copy-start(f32[1,1024]{1,0:T(1,128)} %get-tuple-element.135) | copy-start | bytes 12292
  789.5 68.4 %all-to-all-start.1 = ((bf16[512,8,128]{2,0,1:T(8,128)(2,1)}), bf16[512,8,128]{2,0,1:T(8,128)(2,1)S(1)}, u32[]{:S(2)}, u32[]{:S(2)}) async-start(bf16[512,8,128]{2,0,1:T(8,128)(2,1)} %bitcast.794), calls=%async_computation.1 | async-start | bytes 2097152 | tf_op jit(solution)/shard_map/all_to_all | solution.py:276
  793.6 27.9 %copy-start.22 = (bf16[16,512,64]{1,0,2:T(8,128)(2,1)S(1)}, bf16[16,512,64]{1,0,2:T(8,128)(2,1)}, u32[]{:S(2)}) copy-start(bf16[16,512,64]{1,0,2:T(8,128)(2,1)} %copy-done.21) | copy-start | bytes 3145732
  847.3 11.9 %collective-permute-start.2 = (bf16[8,512,256]{2,1,0:T(8,128)(2,1)}, bf16[8,512,256]{2,1,0:T(8,128)(2,1)}, u32[]{:S(2)}, u32[]{:S(2)}) collective-permute-start(bf16[8,512,256]{2,1,0:T(8,128)(2,1)} %fusion.41), channel_id=1, source_target_pairs={{0,1},{1,0},{2,3},{3,2},{4,5},{5,4},{6,7},{7,6},{8,9},{9,8},{10,11... | collective-permute-start | bytes 6291464 | tf_op jit(solution)/shard_map/ppermute | solution.py:282
  862.6 10.5 slice-start.10
  873.1 18.3 %slice-start.6 = ((s8[8388608]{0:T(1024)(128)(4,1)}), s8[4194304]{0:T(1024)(128)(4,1)S(1)}, s32[]{:S(2)}) async-start(s8[8388608]{0:T(1024)(128)(4,1)} %bitcast.817), calls=%async_computation.12 | async-start | bytes 8388608
  954.0 27.9 %copy-start.20 = (bf16[16,512,64]{1,0,2:T(8,128)(2,1)S(1)}, bf16[16,512,64]{1,0,2:T(8,128)(2,1)}, u32[]{:S(2)}) copy-start(bf16[16,512,64]{1,0,2:T(8,128)(2,1)} %reshape.507) | copy-start | bytes 3145732
  981.8 11.3 copy-start.16
  993.1 9.8 copy-start.40
  993.1 10.1 copy-start.8
  993.1 10.1 copy-start.76
  1017.2 11.1 collective-permute-start.3
  1047.8 19.5 %all-to-all-start.4 = ((bf16[8,2,16,2048]{3,2,1,0:T(8,128)(2,1)}), bf16[8,2,16,2048]{3,2,1,0:T(8,128)(2,1)S(1)}, u32[]{:S(2)}, u32[]{:S(2)}) async-start(bf16[8,2,16,2048]{3,2,1,0:T(8,128)(2,1)} %copy.407), calls=%async_computation.4 | async-start | bytes 2097152 | tf_op jit(solution)/shard_map/all_to_all | solution.py:433
  1067.3 18.9 %all-to-all-start.3 = ((bf16[512,8,128]{2,0,1:T(8,128)(2,1)}), bf16[512,8,128]{2,0,1:T(8,128)(2,1)S(1)}, u32[]{:S(2)}, u32[]{:S(2)}) async-start(bf16[512,8,128]{2,0,1:T(8,128)(2,1)} %bitcast.793), calls=%async_computation.3 | async-start | bytes 2097152 | tf_op jit(solution)/shard_map/all_to_all | solution.py:276
  1070.9 79.1 %all-reduce.3.cloned.1.call-start = ((), (), s32[]{:S(2)}) async-start(), calls=%async_computation.5 | async-start | bytes 2097152 | tf_op jit(solution)/shard_map/psum | solution.py:443
  1076.6 9.9 copy-start.109
  (117 other events, 510.1 us)
Sparse Core Ops, SparseCore 0:
  1094.6 55.3 all-reduce.2

commit v2 on v1

v2 whole, which is shorter than its diff:
```python
import functools

import jax
import jax.numpy as jnp
from jax import lax
from jax.experimental import pallas as pl
from jax.experimental.pallas import tpu as pltpu
from jax.sharding import PartitionSpec as P

HD = 64
LEN = 1024
BLOCK = 256
BLOCKS = LEN // BLOCK
EPSILON = 1e-05
SCALE = HD**-0.5
ROOT = (2.0 / 3.141592653589793) ** 0.5
MESH = pl.DeviceIdType.MESH
F32 = jnp.float32
BF16 = jnp.bfloat16


ORDERS = {
    "qkv": ((0, "z", 1), (1, "z", 0)),
    "proj": ((0, "z", 1), (1, "z", 0)),
    "up": (("z", 0, 1), ("z", 1, 0)),
    "down": (("z", 0, 1), ("z", 1, 0)),
}
KINDS = ("qkv", "proj", "up", "down")
WINDOW = 4


def place_of(group, g, b):
    if group == 2:
        return g + b * (BLOCKS - 1 - 2 * g)
    return g * (BLOCKS // group) + b


def gather_body(n_row, n_col, layers, group, *refs):
    shard = dict(zip(KINDS, refs[:4]))
    tokens, cotangent, vector = refs[4:7]
    full = dict(zip(KINDS, refs[7:11]))
    own_tokens, own_cotangent, vectors = refs[11:14]
    local_sem, send_sem, recv_sem, near_sem, out_sem, in_sem = refs[14:]
    r = lax.axis_index("row")
    c = lax.axis_index("col")
    link_bits = [b for b in (2**k for k in range(1, 8)) if b < n_col]
    depth = shard["up"].shape[1]

    def row_peer(s):
        return (lax.rem(r + s, n_row), c)

    def col_peer(bit):
        return (r, c ^ bit)

    peers = [row_peer(s) for s in range(1, n_row)]
    peers += [(r, lax.rem(c + d, n_col)) for d in range(1, n_col)]
    barrier = pltpu.get_barrier_semaphore()
    for peer in peers:
        pl.semaphore_signal(barrier, inc=1, device_id=peer, device_id_type=MESH)
    pl.semaphore_wait(barrier, len(peers))

    per, width = BLOCKS // group, tokens.shape[1]

    def own_place(ref, b, col):
        if len(ref.shape) == 2:
            start = pl.multiple_of(col * width, width)
            return ref.at[pl.ds(b * BLOCK, BLOCK), pl.ds(start, width)]
        return ref.at[col, pl.ds(b * BLOCK, BLOCK)]

    def from_place(ref, b, col):
        start = (col // group) * LEN + place_of(group, lax.rem(col, group), b) * BLOCK
        return ref.at[pl.ds(pl.multiple_of(start, BLOCK), BLOCK)]

    exchanged = ((tokens, own_tokens), (cotangent, own_cotangent))

    def near(n, b):
        src, dst = exchanged[n]
        return pltpu.make_async_copy(from_place(src, b, c), own_place(dst, b, c), near_sem.at[n * per + b])

    def near_vector():
        return pltpu.make_async_copy(vector, vectors.at[c], near_sem.at[2 * per])

    def far(src, dst, n, peer):
        return pltpu.make_async_remote_copy(
            src_ref=src, dst_ref=dst, send_sem=out_sem.at[n], recv_sem=in_sem.at[n],
            device_id=peer, device_id_type=MESH,
        )

    def start_exchange(n):
        src, dst = exchanged[n]
        for b in range(per):
            near(n, b).start()
        for d in range(1, n_col):
            to = lax.rem(c + d, n_col)
            for b in range(per):
                far(from_place(src, b, to), own_place(dst, b, c), n, (r, to)).start()

    def wait_exchange(n):
        _, dst = exchanged[n]
        for b in range(per):
            near(n, b).wait()
        if len(dst.shape) == 2:
            ref = dst.at[:, pl.ds(0, (n_col - 1) * width)]
        else:
            ref = dst.at[pl.ds(0, n_col - 1)]
        far(ref, ref, n, col_peer(1)).wait()

    def own(kind, l, h):
        ref = shard[kind]
        half = ref.shape[1] // 2
        return ref.at[l, pl.ds(h * half, half)]

    def block(kind, l, h, row, col):
        if kind in ("qkv", "up"):
            return full[kind].at[l, col, row, h]
        start = pl.multiple_of(row * depth, depth)
        return full[kind].at[l, col, h, :, pl.ds(start, depth)]

    def strip(kind, l, h, col):
        if kind in ("qkv", "up"):
            return full[kind].at[l, col, :, h]
        return full[kind].at[l, col, h]

    def amount(kind, l, h, strips, rows):
        if kind in ("qkv", "up"):
            return full[kind].at[l, pl.ds(0, strips), pl.ds(0, rows), h]
        return full[kind].at[l, pl.ds(0, strips), h, :, pl.ds(0, rows * depth)]

    chunks = []
    for l in range(layers):
        for kind in KINDS:
            for h in range(2):
                order = []
                for d in ORDERS[kind][h]:
                    if d == "z":
                        order.append("z")
                    elif d < len(link_bits):
                        order.append(link_bits[d])
                order += link_bits[2:]
                chunks.append((kind, l, h, tuple(order)))
    phases = len(link_bits) + 1

    def plan(order):
        masks, whole, steps = [0], False, []
        for d in order:
            steps.append((d, tuple(masks), whole))
            if d == "z":
                whole = True
            else:
                masks = masks + [m ^ d for m in masks]
        steps.append((None, tuple(masks), whole))
        return steps

    def remote(src, dst, k, p, peer):
        return pltpu.make_async_remote_copy(
            src_ref=src, dst_ref=dst, send_sem=send_sem.at[k, p], recv_sem=recv_sem.at[k, p],
            device_id=peer, device_id_type=MESH,
        )

    def local(k):
        kind, l, h, _ = chunks[k]
        return pltpu.make_async_copy(own(kind, l, h), block(kind, l, h, r, c), local_sem.at[k])

    def issue(k, p):
        kind, l, h, order = chunks[k]
        d, masks, whole = plan(order)[p]
        for m in masks:
            if d == "z":
                src = own(kind, l, h) if m == 0 else block(kind, l, h, r, c ^ m)
                for s in range(1, n_row):
                    remote(src, block(kind, l, h, r, c ^ m), k, p, row_peer(s)).start()
            elif whole:
                ref = strip(kind, l, h, c ^ m)
                remote(ref, ref, k, p, col_peer(d)).start()
            else:
                src = own(kind, l, h) if m == 0 else block(kind, l, h, r, c ^ m)
                remote(src, block(kind, l, h, r, c ^ m), k, p, col_peer(d)).start()

    def moved(k, p):
        kind, l, h, order = chunks[k]
        d, masks, whole = plan(order)[p]
        if d == "z":
            rows = n_row - 1
        else:
            rows = n_row if whole else 1
        ref = amount(kind, l, h, len(masks), rows)
        return remote(ref, ref, k, p, col_peer(1))

    def share(k, p):
        kind, l, h, order = chunks[k]
        steps = plan(order)
        (d, masks, _), (_, later, whole) = steps[p], steps[p + 1]
        if not whole:
            return
        fresh = masks if d == "z" else later[len(masks):]
        for m in fresh:
            ref = strip(kind, l, h, c ^ m)
            remote(ref, ref, k, phases, col_peer(1)).start()

    def shared(k):
        kind, l, h, _ = chunks[k]
        ref = amount(kind, l, h, n_col // 2, n_row)
        return remote(ref, ref, k, phases, col_peer(1))

    def finish(k, p):
        moved(k, p).wait_recv()
        if chunks[k][3][p] == "z":
            local(k).wait()
        if p + 1 < phases:
            issue(k, p + 1)
        share(k, p)

    count = len(chunks)
    near_vector().start()
    for d in range(1, n_col):
        far(vector, vectors.at[c], 2, (r, lax.rem(c + d, n_col))).start()
    start_exchange(0)
    for k in range(count):
        local(k).start()
    for t in range(count + WINDOW + phases):
        if t < count:
            issue(t, 0)
        if t == count - 1:
            start_exchange(1)
        for p in range(phases):
            k = t - WINDOW - p
            if 0 <= k < count:
                finish(k, p)
    for k in range(count):
        for p in range(phases):
            moved(k, p).wait_send()
        shared(k).wait_send()
        shared(k).wait_recv()
    near_vector().wait()
    rest = vectors.at[pl.ds(0, n_col - 1)]
    far(rest, rest, 2, col_peer(1)).wait()
    wait_exchange(0)
    wait_exchange(1)


def gather_inputs(n_row, n_col, group, qkv, proj, up, down, tokens, cotangent, vector):
    layers, depth = up.shape[0], up.shape[1]
    width, units = proj.shape[1], down.shape[1]
    dim = depth * n_row
    mine = LEN // group
    own = (mine, dim) if width % 128 == 0 else (n_col, mine, width)
    shapes = (
        (layers, n_col, n_row, 2, depth // 2, qkv.shape[2]),
        (layers, n_col, 2, width // 2, dim),
        (layers, n_col, n_row, 2, depth // 2, units),
        (layers, n_col, 2, units // 2, dim),
        own,
        own,
        (n_col,) + vector.shape,
    )
    count = layers * 8
    phases = n_col.bit_length()
    outs = pl.pallas_call(
        functools.partial(gather_body, n_row, n_col, layers, group),
        out_shape=[jax.ShapeDtypeStruct(s, BF16) for s in shapes],
        in_specs=[pl.BlockSpec(memory_space=pltpu.HBM)] * 7,
        out_specs=[pl.BlockSpec(memory_space=pltpu.HBM)] * 7,
        scratch_shapes=[
            pltpu.SemaphoreType.DMA((count,)),
            pltpu.SemaphoreType.DMA((count, phases)),
            pltpu.SemaphoreType.DMA((count, phases)),
            pltpu.SemaphoreType.DMA((2 * (BLOCKS // group) + 1,)),
            pltpu.SemaphoreType.DMA((3,)),
            pltpu.SemaphoreType.DMA((3,)),
        ],
        compiler_params=pltpu.CompilerParams(collective_id=0, has_side_effects=True),
        name="gather_inputs",
    )(qkv, proj, up, down, tokens, cotangent, vector)

    merge = 128 // width
    strips = n_col // merge
    qkv_full = outs[0].reshape(layers, n_col, dim, qkv.shape[2])
    up_full = outs[2].reshape(layers, n_col, dim, units)
    own_rows = outs[4:6]
    if merge > 1:
        qkv_full = qkv_full.reshape(layers, strips, merge, dim, 3, width).transpose(0, 1, 3, 4, 2, 5)
        up_full = up_full.reshape(layers, strips, merge, dim, units).transpose(0, 1, 3, 2, 4)
        own_rows = [x.transpose(1, 0, 2).reshape(mine, dim) for x in own_rows]
    return (
        qkv_full.reshape(layers, strips, dim, 384),
        outs[1].reshape(layers, dim, dim),
        up_full.reshape(layers, strips, dim, units * merge),
        outs[3].reshape(layers, units * n_col, dim),
        own_rows[0],
        own_rows[1],
        outs[6],
    )


PARAMS = pltpu.CompilerParams(vmem_limit_bytes=60 * 2**20)
NARROW = 8
CROSS = ((0,), (0,))
TURNED = ((1,), (1,))


def dot(a, b, dims=((1,), (0,))):
    return lax.dot_general(a, b, (dims, ((), ())), preferred_element_type=F32)


def whole(shape):
    return pl.BlockSpec(shape, lambda i, ids: (0,) * len(shape))


def layer_of(shape, l):
    return pl.BlockSpec((None,) + shape, lambda i, ids: (l,) + (0,) * len(shape))


def chosen(shape, l, site):
    return pl.BlockSpec((None, None) + shape, lambda i, ids: (l, ids[site]) + (0,) * len(shape))


def call(body, ids, steps, operands, outs, scratch, name):
    return pl.pallas_call(
        body,
        grid_spec=pltpu.PrefetchScalarGridSpec(
            num_scalar_prefetch=1,
            grid=(steps,),
            in_specs=[spec for _, spec in operands],
            out_specs=[spec for _, spec in outs],
            scratch_shapes=scratch,
        ),
        out_shape=[shape for shape, _ in outs],
        compiler_params=PARAMS,
        name=name,
    )(ids, *[array for array, _ in operands])


def shape_of(shape, kind):
    return jax.ShapeDtypeStruct(shape, kind)


def stream_spec(tokens, dim, final):
    if final:
        shape = (NARROW, tokens, dim // NARROW)
        return shape_of(shape, BF16), whole(shape)
    return shape_of((tokens, dim), F32), whole((tokens, dim))


def put(ref, value):
    if len(ref.shape) == 2:
        ref[...] = value
    else:
        for i in range(ref.shape[0]):
            ref[i] = value[:, i * 128 : (i + 1) * 128].astype(BF16)


def norm_parts(x):
    center = x - jnp.mean(x, axis=1, keepdims=True)
    inverse = lax.rsqrt(jnp.mean(center * center, axis=1, keepdims=True) + EPSILON)
    return center * inverse, inverse


def norm_grad(grad, scaled, inverse, gain):
    w = grad * gain
    first = jnp.mean(w, axis=1, keepdims=True)
    second = jnp.mean(w * scaled, axis=1, keepdims=True)
    return inverse * (w - first - scaled * second)


def qkv_body(ids, x, gain, shift, w, bias, a, b, q, kv, red, normed):
    @pl.when(pl.program_id(0) == 0)
    def _():
        scaled, _ = norm_parts(x[...])
        normed[...] = (scaled * gain[...] + shift[...]).astype(BF16)
        red[...] = dot(normed[...], a[...]).astype(BF16)

    for j in range(w.shape[0]):
        mixed = (dot(normed[...], w[j]) + bias[j] + dot(red[...], b[j])).astype(BF16)
        q[j] = mixed[:, :128]
        kv[j] = mixed[:, 128:]


def qkv_kernel(l, ids, x, gain, shift, w, bias, a, b):
    tokens, dim = x.shape
    rank = a.shape[-1]
    two = 2

    def strips(shape):
        return pl.BlockSpec((two,) + shape, lambda i, ids: (i, 0, 0))

    return call(
        qkv_body, ids, NARROW // two,
        [
            (x, whole((tokens, dim))),
            (gain, layer_of((1, dim), l)),
            (shift, layer_of((1, dim), l)),
            (w, pl.BlockSpec((None, two, dim, 384), lambda i, ids: (l, i, 0, 0))),
            (bias, pl.BlockSpec((None, two, 1, 384), lambda i, ids: (l, i, 0, 0))),
            (a, chosen((dim, rank), l, 0)),
            (b, pl.BlockSpec((None, two, rank, 384), lambda i, ids: (l, i, 0, 0))),
        ],
        [
            (shape_of((NARROW, tokens, 128), BF16), strips((tokens, 128))),
            (shape_of((NARROW, tokens, 256), BF16), strips((tokens, 256))),
            (shape_of((tokens, rank), BF16), whole((tokens, rank))),
        ],
        [pltpu.VMEM((tokens, dim), BF16)],
        "qkv",
    )


def pair_state(held):
    group, per = len(held), len(held[0])
    state = {}
    for s in range(per):
        for j in range(group):
            for b in range(per):
                seen = {held[(g - j) % group][b] <= held[g][s] for g in range(group)}
                state[s, j, b] = 0 if len(seen) == 2 else (1 if True in seen else -1)
    return state


def head_mask(h):
    lane = lax.broadcasted_iota(jnp.int32, (1, 128), 1)
    return (lane // HD) == h


def attend_body(held, bias, q, *refs):
    group, per = len(held), len(held[0])
    kvs, (out, lse) = refs[:group], refs[group:]
    state = pair_state(held)
    turned = {}
    for s in range(per):
        rows = pl.ds(s * BLOCK, BLOCK)
        queries = q[rows, :] * SCALE
        pieces = []
        for h in range(2):
            query = jnp.where(head_mask(h), queries, 0).astype(BF16)
            scores, values = [], []
            for j in range(group):
                for b in range(per):
                    if state[s, j, b] < 0:
                        continue
                    keys = kvs[j][b * BLOCK : (b + 1) * BLOCK, :128]
                    score = dot(keys, query, TURNED)
                    if state[s, j, b] == 0:
                        score = score + bias[s * group * per + j * per + b].astype(F32)
                    scores.append(score)
                    if (j, b) not in turned:
                        turned[j, b] = kvs[j][b * BLOCK : (b + 1) * BLOCK, 128:].T
                    values.append(turned[j, b][h * HD : (h + 1) * HD])
            top = functools.reduce(jnp.maximum, [jnp.max(x, axis=0, keepdims=True) for x in scores])
            total, made = 0.0, 0.0
            for score, value in zip(scores, values):
                e = jnp.exp(score - top)
                total = total + jnp.sum(e, axis=0, keepdims=True)
                made = made + dot(value, e.astype(BF16))
            pieces.append(made / total)
            lse[h : h + 1, rows] = top + jnp.log(total)
        out[rows, :] = jnp.concatenate(pieces, axis=0).T.astype(BF16)


def attend_kernel(held, bias, q, kvs):
    _, tokens, _ = q.shape

    def strip(shape):
        return pl.BlockSpec((None,) + shape, lambda i, ids: (i, 0, 0))

    return call(
        functools.partial(attend_body, held), bias, NARROW,
        [(q, strip((tokens, 128)))] + [(kv, strip((tokens, 256))) for kv in kvs],
        [
            (shape_of((tokens, NARROW * 128), BF16), pl.BlockSpec((tokens, 128), lambda i, ids: (0, i))),
            (shape_of((NARROW, 8, tokens), F32), strip((8, tokens))),
        ],
        [],
        "attend",
    )


def attend_back_body(held, bias, q, lse, out, grad, *refs):
    group, per = len(held), len(held[0])
    kvs, gq, gkvs = refs[:group], refs[group], refs[group + 1 :]
    state = pair_state(held)
    turned, gk, gv = {}, {}, {}
    for s in range(per):
        rows = pl.ds(s * BLOCK, BLOCK)
        queries = q[rows, :] * SCALE
        up = grad[rows, :]
        product = (up.astype(F32) * out[rows, :].astype(F32)).T
        pieces = []
        for h in range(2):
            query = jnp.where(head_mask(h), queries, 0).astype(BF16)
            given = jnp.where(head_mask(h), up, 0).astype(BF16)
            inner = jnp.sum(product[h * HD : (h + 1) * HD], axis=0, keepdims=True)
            level = lse[h : h + 1, rows]
            made = 0.0
            for j in range(group):
                for b in range(per):
                    if state[s, j, b] < 0:
                        continue
                    keys = kvs[j][b * BLOCK : (b + 1) * BLOCK, :128]
                    values = kvs[j][b * BLOCK : (b + 1) * BLOCK, 128:]
                    score = dot(keys, query, TURNED)
                    if state[s, j, b] == 0:
                        score = score + bias[s * group * per + j * per + b].astype(F32)
                    probs = jnp.exp(score - level)
                    g_probs = dot(values, given, TURNED)
                    g_scores = (probs * (g_probs - inner)).astype(BF16)
                    if (j, b) not in turned:
                        turned[j, b] = keys.T
                        gk[j, b], gv[j, b] = 0.0, 0.0
                    gv[j, b] = gv[j, b] + dot(probs.astype(BF16), given)
                    gk[j, b] = gk[j, b] + dot(g_scores, query)
                    made = made + dot(turned[j, b][h * HD : (h + 1) * HD], g_scores)
            pieces.append(made)
        gq[rows, :] = (jnp.concatenate(pieces, axis=0) * SCALE).T.astype(BF16)
    for j in range(group):
        for b in range(per):
            rows = pl.ds(b * BLOCK, BLOCK)
            gkvs[j][rows, :128] = gk[j, b].astype(BF16)
            gkvs[j][rows, 128:] = gv[j, b].astype(BF16)


def attend_back_kernel(held, bias, q, lse, out, grad, kvs):
    _, tokens, _ = q.shape

    def strip(shape):
        return pl.BlockSpec((None,) + shape, lambda i, ids: (i, 0, 0))

    columns = pl.BlockSpec((tokens, 128), lambda i, ids: (0, i))
    return call(
        functools.partial(attend_back_body, held), bias, NARROW,
        [(q, strip((tokens, 128))), (lse, strip((8, tokens))), (out, columns), (grad, columns)]
        + [(kv, strip((tokens, 256))) for kv in kvs],
        [(shape_of((NARROW, tokens, 128), BF16), strip((tokens, 128)))]
        + [(shape_of((NARROW, tokens, 256), BF16), strip((tokens, 256))) for _ in kvs],
        [],
        "attend_back",
    )


def gelu_parts(x):
    square = x * x
    t = jnp.tanh(ROOT * (x + 0.044715 * (x * square)))
    half = 0.5 * (1.0 + t)
    slope = half + 0.5 * x * (1.0 - t * t) * (ROOT * (1.0 + 3 * 0.044715 * square))
    return x * half, slope


def mlp_body(
    ids, x, att, w_proj, b_proj, low_proj, up_proj, gain, shift, low_up, w_up, b_up, up_up,
    w_down, low_down, up_down, b_down,
    middle, result, hidden, red_proj, red_up, red_down, normed, total, small,
):
    i = pl.program_id(0)

    @pl.when(i == 0)
    def _():
        red_proj[...] = dot(att[...], low_proj[...]).astype(BF16)
        mid = x[...] + (dot(att[...], w_proj[...]) + b_proj[...] + dot(red_proj[...], up_proj[...]))
        middle[...] = mid
        scaled, _ = norm_parts(mid)
        normed[...] = (scaled * gain[...] + shift[...]).astype(BF16)
        red_up[...] = dot(normed[...], low_up[...]).astype(BF16)
        total[...] = jnp.zeros_like(total)
        small[...] = jnp.zeros_like(small)

    value = dot(normed[...], w_up[...]) + b_up[...] + dot(red_up[...], up_up[...])
    hidden[...] = value
    active = (0.5 * value * (1.0 + jnp.tanh(ROOT * (value + 0.044715 * (value * value * value))))).astype(BF16)
    total[...] += dot(active, w_down[...])
    small[...] += dot(active, low_down[...])

    @pl.when(i == pl.num_programs(0) - 1)
    def _():
        red_down[...] = small[...].astype(BF16)
        put(result, middle[...] + (total[...] + b_down[...] + dot(red_down[...], up_down[...])))


def mlp_kernel(l, final, ids, x, att, w_proj, b_proj, low_proj, up_proj, gain, shift, low_up, w_up, b_up, up_up, w_down, low_down, up_down, b_down):
    tokens, dim = x.shape
    rank = low_proj.shape[-1]
    units = w_up.shape[-1]
    return call(
        mlp_body, ids, NARROW,
        [
            (x, whole((tokens, dim))),
            (att, whole((tokens, dim))),
            (w_proj, layer_of((dim, dim), l)),
            (b_proj, layer_of((1, dim), l)),
            (low_proj, chosen((dim, rank), l, 1)),
            (up_proj, chosen((rank, dim), l, 1)),
            (gain, layer_of((1, dim), l)),
            (shift, layer_of((1, dim), l)),
            (low_up, chosen((dim, rank), l, 2)),
            (w_up, pl.BlockSpec((None, None, dim, units), lambda i, ids: (l, i, 0, 0))),
            (b_up, pl.BlockSpec((None, None, 1, units), lambda i, ids: (l, i, 0, 0))),
            (up_up, pl.BlockSpec((None, None, rank, units), lambda i, ids: (l, ids[2], 0, i))),
            (w_down, pl.BlockSpec((None, units, dim), lambda i, ids: (l, i, 0))),
            (low_down, pl.BlockSpec((None, None, units, rank), lambda i, ids: (l, ids[3], i, 0))),
            (up_down, chosen((rank, dim), l, 3)),
            (b_down, layer_of((1, dim), l)),
        ],
        [
            (shape_of((tokens, dim), F32), whole((tokens, dim))),
            stream_spec(tokens, dim, final),
            (shape_of((NARROW, tokens, units), F32), pl.BlockSpec((None, tokens, units), lambda i, ids: (i, 0, 0))),
            (shape_of((tokens, rank), BF16), whole((tokens, rank))),
            (shape_of((tokens, rank), BF16), whole((tokens, rank))),
            (shape_of((tokens, rank), BF16), whole((tokens, rank))),
        ],
        [pltpu.VMEM((tokens, dim), BF16), pltpu.VMEM((tokens, dim), F32), pltpu.VMEM((tokens, rank), F32)],
        "mlp",
    )


def mlp_back_body(
    ids, grad, hidden, mid, att, red_proj, red_up, red_down, w_proj, low_proj, up_proj, gain, shift,
    low_up, w_up, up_up, w_down, low_down, up_down,
    g_mid, g_att, g_low_proj, g_up_proj, g_low_up, g_up_up, g_low_down, g_up_down,
    low, g_red, total, small,
):
    i = pl.program_id(0)

    @pl.when(i == 0)
    def _():
        low[...] = grad[...].astype(BF16)
        g_red[...] = dot(low[...], up_down[...], TURNED).astype(BF16)
        g_up_down[...] = dot(red_down[...], low[...], CROSS).astype(BF16)
        total[...] = jnp.zeros_like(total)
        small[...] = jnp.zeros_like(small)

    active, slope = gelu_parts(hidden[...])
    active = active.astype(BF16)
    g_low_down[...] = dot(g_red[...], active, CROSS).astype(BF16)
    g_active = dot(low[...], w_down[...], TURNED) + dot(g_red[...], low_down[...], TURNED)
    g_hidden = (g_active * slope).astype(BF16)
    g_up_up[...] = dot(red_up[...], g_hidden, CROSS).astype(BF16)
    small[...] += dot(g_hidden, up_up[...], TURNED)
    total[...] += dot(g_hidden, w_up[...], TURNED)

    @pl.when(i == pl.num_programs(0) - 1)
    def _():
        g_red_up = small[...].astype(BF16)
        scaled, inverse = norm_parts(mid[...])
        normed = (scaled * gain[...] + shift[...]).astype(BF16)
        g_low_up[...] = dot(g_red_up, normed, CROSS).astype(BF16)
        g_normed = total[...] + dot(g_red_up, low_up[...], TURNED)
        g = grad[...] + norm_grad(g_normed, scaled, inverse, gain[...])
        g_mid[...] = g
        low[...] = g.astype(BF16)
        g_red_proj = dot(low[...], up_proj[...], TURNED).astype(BF16)
        g_up_proj[...] = dot(red_proj[...], low[...], CROSS).astype(BF16)
        g_low_proj[...] = dot(g_red_proj, att[...], CROSS).astype(BF16)
        g_att[...] = (dot(low[...], w_proj[...], TURNED) + dot(g_red_proj, low_proj[...], TURNED)).astype(BF16)


def mlp_back_kernel(l, ids, grad, hidden, mid, att, red_proj, red_up, red_down, w_proj, low_proj, up_proj, gain, shift, low_up, w_up, up_up, w_down, low_down, up_down):
    tokens, dim = grad.shape
    rank = low_proj.shape[-1]
    units = w_up.shape[-1]
    flat = (shape_of((rank, dim), BF16), whole((rank, dim)))
    cut = (shape_of((rank, NARROW * units), BF16), pl.BlockSpec((rank, units), lambda i, ids: (0, i)))
    return call(
        mlp_back_body, ids, NARROW,
        [
            (grad, whole((tokens, dim))),
            (hidden, pl.BlockSpec((None, tokens, units), lambda i, ids: (i, 0, 0))),
            (mid, whole((tokens, dim))),
            (att, whole((tokens, dim))),
            (red_proj, whole((tokens, rank))),
            (red_up, whole((tokens, rank))),
            (red_down, whole((tokens, rank))),
            (w_proj, layer_of((dim, dim), l)),
            (low_proj, chosen((dim, rank), l, 1)),
            (up_proj, chosen((rank, dim), l, 1)),
            (gain, layer_of((1, dim), l)),
            (shift, layer_of((1, dim), l)),
            (low_up, chosen((dim, rank), l, 2)),
            (w_up, pl.BlockSpec((None, None, dim, units), lambda i, ids: (l, i, 0, 0))),
            (up_up, pl.BlockSpec((None, None, rank, units), lambda i, ids: (l, ids[2], 0, i))),
            (w_down, pl.BlockSpec((None, units, dim), lambda i, ids: (l, i, 0))),
            (low_down, pl.BlockSpec((None, None, units, rank), lambda i, ids: (l, ids[3], i, 0))),
            (up_down, chosen((rank, dim), l, 3)),
        ],
        [
            (shape_of((tokens, dim), F32), whole((tokens, dim))),
            (shape_of((tokens, dim), BF16), whole((tokens, dim))),
            flat, flat, flat, cut, cut, flat,
        ],
        [
            pltpu.VMEM((tokens, dim), BF16), pltpu.VMEM((tokens, rank), BF16),
            pltpu.VMEM((tokens, dim), F32), pltpu.VMEM((tokens, rank), F32),
        ],
        "mlp_back",
    )


def qkv_back_body(group, ids, g_mid, x, gain, shift, red, w, a, b, gq, *refs):
    parts, (g_x, g_low, g_raise, total, small) = refs[:group], refs[group:]
    i = pl.program_id(0)

    @pl.when(i == 0)
    def _():
        total[...] = jnp.zeros_like(total)
        small[...] = jnp.zeros_like(small)

    for j in range(w.shape[0]):
        g_kv = sum(part[j].astype(F32) for part in parts).astype(BF16)
        g_mixed = jnp.concatenate([gq[j], g_kv], axis=1)
        g_raise[j] = dot(red[...], g_mixed, CROSS).astype(BF16)
        small[...] += dot(g_mixed, b[j], TURNED)
        total[...] += dot(g_mixed, w[j], TURNED)

    @pl.when(i == pl.num_programs(0) - 1)
    def _():
        g_red = small[...].astype(BF16)
        scaled, inverse = norm_parts(x[...])
        normed = (scaled * gain[...] + shift[...]).astype(BF16)
        g_low[...] = dot(g_red, normed, CROSS).astype(BF16)
        g_normed = total[...] + dot(g_red, a[...], TURNED)
        put(g_x, g_mid[...] + norm_grad(g_normed, scaled, inverse, gain[...]))


def qkv_back_kernel(l, final, ids, g_mid, x, gain, shift, red, w, a, b, gq, parts):
    tokens, dim = x.shape
    rank = a.shape[-1]
    two = 2

    def strips(shape):
        return pl.BlockSpec((two,) + shape, lambda i, ids: (i, 0, 0))

    return call(
        functools.partial(qkv_back_body, len(parts)), ids, NARROW // two,
        [
            (g_mid, whole((tokens, dim))),
            (x, whole((tokens, dim))),
            (gain, layer_of((1, dim), l)),
            (shift, layer_of((1, dim), l)),
            (red, whole((tokens, rank))),
            (w, pl.BlockSpec((None, two, dim, 384), lambda i, ids: (l, i, 0, 0))),
            (a, chosen((dim, rank), l, 0)),
            (b, pl.BlockSpec((None, two, rank, 384), lambda i, ids: (l, i, 0, 0))),
            (gq, strips((tokens, 128))),
        ]
        + [(part, strips((tokens, 256))) for part in parts],
        [
            stream_spec(tokens, dim, final),
            (shape_of((rank, dim), BF16), whole((rank, dim))),
            (shape_of((NARROW, rank, 384), BF16), strips((rank, 384))),
        ],
        [pltpu.VMEM((tokens, dim), F32), pltpu.VMEM((tokens, rank), F32)],
        "qkv_back",
    )


def to_rows_body(held, x, out):
    n = 0
    for s in range(x.shape[0] // (len(held) * len(held[0]))):
        for g in range(len(held)):
            for place in held[g]:
                start = (s * BLOCKS + place) * BLOCK
                out[start : start + BLOCK, :] = x[n].astype(F32)
                n += 1


def to_rows(held, x):
    blocks, _, width = x.shape
    return pl.pallas_call(
        functools.partial(to_rows_body, held),
        out_shape=shape_of((blocks * BLOCK, width), F32),
        compiler_params=PARAMS,
        name="to_rows",
    )(x)


def positions(group):
    per = BLOCKS // group
    return tuple(tuple(place_of(group, g, b) for b in range(per)) for g in range(group))


def shards(mesh_shape, *args):
    (
        tokens, cotangent, adapter_ids, qkv_weight, qkv_bias, proj_weight, proj_bias,
        up_weight, up_bias, down_weight, down_bias, first_gain, first_shift, second_gain,
        second_shift, qkv_lower, qkv_raise, proj_lower, proj_raise, up_lower, up_raise,
        down_lower, down_raise,
    ) = args
    n_row, n_col = mesh_shape
    layers, adapters, dim, rank = qkv_lower.shape
    rows, width = tokens.shape
    units = up_weight.shape[2]
    seqs = rows // LEN
    group = n_col // seqs
    held = positions(group)
    per = BLOCKS // group
    mine = per * BLOCK
    merge = 128 // width
    c = lax.axis_index("col")
    g = lax.rem(c, group)
    ids = lax.dynamic_index_in_dim(adapter_ids, c // group, 0, keepdims=False)

    vector = jnp.concatenate(
        [qkv_bias.reshape(layers, 3 * width), proj_bias, up_bias, down_bias]
        + [first_gain, first_shift, second_gain, second_shift],
        axis=1,
    ).reshape(-1)
    cells = vector.shape[0]
    lanes = -(-cells // 2048) * 128
    vector = jnp.pad(vector, (0, 16 * lanes - cells)).reshape(16, lanes)

    qkv_full, proj_full, up_full, down_full, x, grad, vectors = gather_inputs(
        n_row, n_col, group, qkv_weight.reshape(layers, -1, 3 * width), proj_weight, up_weight,
        down_weight, tokens, cotangent, vector
    )
    x, grad = x.astype(F32), grad.astype(F32)
    vectors = vectors.reshape(n_col, -1)[:, :cells].reshape(n_col, layers, -1).astype(F32)
    vectors = vectors.transpose(1, 0, 2)
    at = 0
    cut = []
    for size in (3 * width, width, units, width, width, width, width, width):
        cut.append(vectors[:, :, at : at + size])
        at += size
    qkv_b = cut[0].reshape(layers, NARROW, merge, 3, width).transpose(0, 1, 3, 2, 4)
    qkv_b = qkv_b.reshape(layers, NARROW, 1, 384)
    up_b = cut[2].reshape(layers, NARROW, 1, -1)
    proj_b, down_b, gain1, shift1, gain2, shift2 = [
        cut[i].reshape(layers, 1, dim) for i in (1, 3, 4, 5, 6, 7)
    ]
    raise_qkv = lax.dynamic_index_in_dim(qkv_raise, ids[0], 1, keepdims=False)
    raise_qkv = raise_qkv.reshape(layers, rank, 3, NARROW, 128).transpose(0, 3, 1, 2, 4)
    raise_qkv = raise_qkv.reshape(layers, NARROW, rank, 384)

    def peer_values(x, step):
        pairs = [(q, q - q % group + (q + step) % group) for q in range(n_col)]
        return lax.ppermute(x, "col", pairs)

    def to_columns(x):
        if merge > 1:
            x = x.reshape(NARROW, mine, merge, width).transpose(0, 2, 1, 3).reshape(n_col, mine, width)
        x = lax.all_to_all(x, "col", split_axis=0, concat_axis=0, tiled=True)
        return to_rows(held, x.reshape(n_col * per, BLOCK, width))

    table = jnp.asarray(held, jnp.int32)
    own_place = table[g]
    key_place = jnp.concatenate([table[lax.rem(g - s + group, group)] for s in range(group)])
    bias = jnp.where(key_place[None, :] <= own_place[:, None], 0, -(2**30)).astype(jnp.int32).reshape(-1)

    records = []
    for l in range(layers):
        rec = {"x": x}
        rec["q"], kv, rec["red"] = qkv_kernel(l, ids, x, gain1, shift1, qkv_full, qkv_b, qkv_lower, raise_qkv)
        rec["kvs"] = [kv] + [peer_values(kv, s) for s in range(1, group)]
        rec["att"], rec["lse"] = attend_kernel(held, bias, rec["q"], rec["kvs"])
        rec["mid"], x, rec["hidden"], rec["red_proj"], rec["red_up"], rec["red_down"] = mlp_kernel(
            l, l == layers - 1, ids, x, rec["att"], proj_full, proj_b, proj_lower, proj_raise,
            gain2, shift2, up_lower, up_full, up_b, up_raise, down_full, down_lower, down_raise, down_b
        )
        records.append(rec)
    result = to_columns(x)

    onehot = (adapter_ids.T[:, :, None] == jnp.arange(adapters)[None, None, :]).astype(BF16)

    def all_rows(x):
        pairs = [[(q, (q + s) % n_row) for q in range(n_row)] for s in range(1, n_row)]
        return [x] + [lax.ppermute(x, "row", pair) for pair in pairs]

    onehots = jnp.concatenate(all_rows(onehot), axis=1)

    def collect(named):
        parts = jnp.concatenate([part for _, part in named], axis=2)
        parts = lax.all_to_all(parts, "col", split_axis=0, concat_axis=0, tiled=True)
        parts = parts.reshape((seqs, group) + parts.shape[1:]).astype(F32).sum(axis=1).astype(BF16)
        parts = jnp.concatenate(all_rows(parts), axis=0)
        outs, at = [], 0
        for site, part in named:
            piece = parts[:, :, at : at + part.shape[2]]
            at += part.shape[2]
            outs.append(jnp.einsum("sa,srn->arn", onehots[site], piece, preferred_element_type=F32))
        return outs

    def strips(x):
        return x.reshape(rank, n_col, -1).transpose(1, 0, 2)

    grads = [None] * layers
    for l in reversed(range(layers)):
        rec = records[l]
        g_mid, g_att, g_low_proj, g_up_proj, g_low_up, g_up_up, g_low_down, g_up_down = mlp_back_kernel(
            l, ids, grad, rec["hidden"], rec["mid"], rec["att"], rec["red_proj"], rec["red_up"],
            rec["red_down"], proj_full, proj_lower, proj_raise, gain2, shift2, up_lower, up_full,
            up_raise, down_full, down_lower, down_raise
        )
        done = collect(
            [(1, strips(g_low_proj)), (1, strips(g_up_proj)), (2, strips(g_low_up))]
            + [(2, strips(g_up_up)), (3, strips(g_low_down)), (3, strips(g_up_down))]
        )
        gq, *gkvs = attend_back_kernel(held, bias, rec["q"], rec["lse"], rec["att"], g_att, rec["kvs"])
        parts = [gkvs[0]] + [peer_values(gkvs[s], group - s) for s in range(1, group)]
        grad, g_low, g_raise = qkv_back_kernel(
            l, l == 0, ids, g_mid, rec["x"], gain1, shift1, rec["red"], qkv_full, qkv_lower, raise_qkv, gq, parts
        )
        g_raise = g_raise.reshape(NARROW, rank, 3, merge, width).transpose(0, 3, 1, 2, 4)
        first = collect([(0, strips(g_low)), (0, g_raise.reshape(n_col, rank, 3 * width))])
        grads[l] = first + done
    input_grad = to_columns(grad)

    outs = []
    for number in range(8):
        p = jnp.stack([grads[l][number] for l in range(layers)])
        if number == 1:
            p = p.reshape(layers, adapters, rank, 3, width)
        elif number % 2 == 0:
            p = p.transpose(0, 1, 3, 2)
        outs.append(p)
    return (result, input_grad) + tuple(outs)


def solution(mesh):
    mesh_shape = (mesh.shape["row"], mesh.shape["col"])
    return jax.shard_map(
        functools.partial(shards, mesh_shape),
        mesh=mesh,
        in_specs=(
            P("row", "col"), P("row", "col"), P("row", None),
            P(None, "row", None, "col"), P(None, None, "col"),
            P(None, "col", "row"), P(None, "col"),
            P(None, "row", "col"), P(None, "col"),
            P(None, "col", "row"), P(None, "col"),
            P(None, "col"), P(None, "col"), P(None, "col"), P(None, "col"),
            P(), P(), P(), P(), P(), P(), P(), P(),
        ),
        out_specs=(
            P("row", "col"), P("row", "col"),
            P(None, None, "col", None), P(None, None, None, None, "col"),
            P(None, None, "col", None), P(None, None, None, "col"),
            P(None, None, "col", None), P(None, None, None, "col"),
            P(None, None, "col", None), P(None, None, None, "col"),
        ),
        check_vma=False,
    )
```

time: 1180 us -> 761 us (0.64)
  matrix products: 359 us -> 5.17 us
  Pallas kernels: 306 us -> 570 us
  local copies, waits for them, and re-layouts: 191 us -> 57.7 us
  other arithmetic: 127 us -> 6.86 us
  blocking collectives: 68.2 us -> 0 us
  starting transfers between devices: 23.5 us -> 58.6 us
  between operations: 24.7 us -> 1.54 us
  waiting for transfers between devices: 70.2 us -> 55.7 us
    dot_general x84 -> x16, matrix products: 359 us -> 5.17 us  [collect(): jnp.einsum('sa,srn->arn', onehots[site], piece, preferred_element_type=F32)]
    pallas_call x1 -> x15, Pallas kernels: 306 us -> 570 us  [the longest x1 315 us: gather_inputs(): pl.pallas_call(functools.partial(gather_body, n_row, n_col, layers, group...]
    all_gather x8 -> x0, blocking collectives: 68.2 us -> none  [the longest x7 59.4 us: vectors(): return lax.all_gather(v, 'col', axis=v.ndim - 1, tiled=True).astype(F32)]
    convert_element_type x10 -> x3, other arithmetic: 63.1 us -> 3.16 us  [the longest x2 3.15 us: shards(): x, grad = (x.astype(F32), grad.astype(F32))]
    psum x1 -> x0, waiting for transfers between devices: 53.9 us -> none  [shards(): summed = lax.psum([p.astype(BF16) for p in placed], 'row')]
    slice x26 -> x3, local copies, waits for them, and re-layouts: 46.8 us -> 0.65 us  [the longest x2 0.65 us: shards(): cut.append(vectors[:, :, at:at + size])]
    reshape x19 -> x4, local copies, waits for them, and re-layouts: 45.4 us -> 2.12 us  [the longest x1 0.85 us: shards(): raise_qkv = raise_qkv.reshape(layers, NARROW, rank, 384)]
    ppermute x0 -> x15, starting transfers between devices: none -> 35.5 us  [all_rows(): return [x] + [lax.ppermute(x, 'row', pair) for pair in pairs]]
  transfers between devices with their start and end apart: 10 -> 25, of which waited for: 3 -> 15; matrix products, arithmetic and copies ran while one was open for 17% -> 6% of each run, Pallas kernels for 26% -> 10%
where the time goes in v2:
time: 761 us; the launch traced here: 755 us
  Pallas kernels  570 us (75%)
  starting transfers between devices  58.6 us (8%)
  local copies, waits for them, and re-layouts  57.7 us (8%)
  waiting for transfers between devices  55.7 us (7%)
    pallas_call x1, Pallas kernels, gather_inputs(): pl.pallas_call(functools.partial(gather_body, n_row, n_col, layers, group...  315 us
    pallas_call x12, Pallas kernels, call(): pl.pallas_call(body, grid_spec=pltpu.PrefetchScalarGridSpec(num_scalar_pr...  249 us
    unnamed x96, local copies, waits for them, and re-layouts  47.3 us
    ppermute x15, starting transfers between devices, all_rows(): return [x] + [lax.ppermute(x, 'row', pair) for pair in pairs]  35.5 us
    ppermute x15, waiting for transfers between devices, all_rows(): return [x] + [lax.ppermute(x, 'row', pair) for pair in pairs]  33.7 us
    all_to_all x4, waiting for transfers between devices, collect(): lax.all_to_all(parts, 'col', split_axis=0, concat_axis=0, tiled=True)  18.4 us
  transfers between devices with their start and end apart: 25, of which 15 were waited for; matrix products, arithmetic and copies ran while one was open for 6% of the time, Pallas kernels for 10%

profile of v2, /device:TPU:0, one launch (start us, length us, event | category | flops | bytes accessed | tf_op | source)
XLA Modules:
  0.0 755.1 jit_solution(2045023382872045391)
XLA Ops:
  10.8 314.8 %gather_inputs.1 = (bf16[2,8,4,2,128,384]{5,4,3,2,1,0:T(8,128)(2,1)}, bf16[2,8,2,64,1024]{4,3,2,1,0:T(8,128)(2,1)}, bf16[2,8,4,2,128,512]{5,4,3,2,1,0:T(8,128)(2...) custom-call(bf16[2,256,384]{2,1,0:T(8,128)(2,1)} %copy.159.refs_0_, ...), custom_call_target="tpu_custom_call" | custom-call | tf_op jit(solution)/shard_map/gather_inputs/pallas_call | solution.py:258
  329.1 1.6 convert_element_type.11.x
  330.7 3.2 copy.162.a
  333.9 10.9 %qkv.2 = (bf16[8,512,128]{2,1,0:T(8,128)(2,1)}, bf16[8,512,256]{2,1,0:T(8,128)(2,1)}, bf16[512,16]{1,0:T(8,128)(2,1)}) custom-call(s32[4]{0:T(128)} %fusion.107.ids, f32[512,1024]{1,0:T(8,128)} %convert_element_type.11.x, f32[2,1,1024]{2,1,0:T(1,128)} %bitcast.308, f32[2,1,1024]{2,1,0:T(1,128)} %bitcast.304, bf16[2,8,1024,384]{3,2,1,0:T(8,128)(2,1)} %bitcast.289, ...), custom_call_target="tpu_custom_call" | custom-call | tf_op jit(solution)/shard_map/qkv/pallas_call | solution.py:318
  346.6 12.9 %copy.166.low_down = bf16[2,8,4096,16]{3,2,1,0:T(8,128)(2,1)} copy(bf16[2,8,4096,16]{2,3,1,0:T(8,128)(2,1)} %param.45) | data formatting | bytes 4194304 | tf_op args[21]
  359.5 3.1 copy.164.low_proj
  362.6 3.2 copy.165.low_up
  367.2 19.2 %attend.2 = (bf16[512,1024]{1,0:T(8,128)(2,1)}, f32[8,8,512]{2,1,0:T(8,128)}) custom-call(s32[8]{0:T(128)} %select_n.36.bias, bf16[8,512,128]{2,1,0:T(8,128)(2,1)} %get-tuple-element.70.q, bf16[8,512,256]{2,1,0:T(8,128)(2,1)} %get-tuple-element.71.refs_0_, bf16[8,512,256]{2,1,0:T(8,128)(2,1)} %copy-done.2), custom_call_target="tpu_custom_call" | custom-call | tf_op jit(solution)/shard_map/attend/pallas_call | solution.py:318
  386.4 24.7 %mlp.2 = (f32[512,1024]{1,0:T(8,128)}, f32[512,1024]{1,0:T(8,128)}, f32[8,512,512]{2,1,0:T(8,128)}, bf16[512,16]{1,0:T(8,128)(2,1)}, bf16[512,16]{1,0:T(8,128)(2,1)}, /*index=5*/bf16[512,16]{1,0:T(8,128)(2,1)}) custom-call(s32[4]{0:T(128)} %fusion.107.ids, f32[512,1024]{1,0:T(8,128)} %convert_element_type.11.x, bf16[512,1024]{1,0:T(8,128)(2,1)} %get-tuple-element.72.att.out, ...), custom_call_target="tpu_custom_call" | custom-call | tf_op jit(solution)/shard_map/mlp/pallas_call | solution.py:318
  411.1 10.9 %qkv.3 = (bf16[8,512,128]{2,1,0:T(8,128)(2,1)}, bf16[8,512,256]{2,1,0:T(8,128)(2,1)}, bf16[512,16]{1,0:T(8,128)(2,1)}) custom-call(s32[4]{0:T(128)} %fusion.107.ids, f32[512,1024]{1,0:T(8,128)} %get-tuple-element.76.x, f32[2,1,1024]{2,1,0:T(1,128)} %bitcast.309, f32[2,1,1024]{2,1,0:T(1,128)} %bitcast.305, bf16[2,8,1024,384]{3,2,1,0:T(8,128)(2,1)} %bitcast.290, ...), custom_call_target="tpu_custom_call" | custom-call | tf_op jit(solution)/shard_map/qkv/pallas_call | solution.py:318
  422.1 1.6 convert_element_type.13.grad
  423.7 2.7 collective-permute-done.1.refs_1_
  427.7 19.6 %attend.3 = (bf16[512,1024]{1,0:T(8,128)(2,1)}, f32[8,8,512]{2,1,0:T(8,128)}) custom-call(s32[8]{0:T(128)} %select_n.36.bias, bf16[8,512,128]{2,1,0:T(8,128)(2,1)} %get-tuple-element.77.q, bf16[8,512,256]{2,1,0:T(8,128)(2,1)} %get-tuple-element.78.refs_0_, bf16[8,512,256]{2,1,0:T(8,128)(2,1)} %copy-done.3), custom_call_target="tpu_custom_call" | custom-call | tf_op jit(solution)/shard_map/attend/pallas_call | solution.py:318
  447.3 24.4 %mlp.3 = (f32[512,1024]{1,0:T(8,128)}, bf16[8,512,128]{2,1,0:T(8,128)(2,1)}, f32[8,512,512]{2,1,0:T(8,128)}, bf16[512,16]{1,0:T(8,128)(2,1)}, bf16[512,16]{1,0:T(8,128)(2,1)}, /*index=5*/bf16[512,16]{1,0:T(8,128)(2,1)}) custom-call(s32[4]{0:T(128)} %fusion.107.ids, f32[512,1024]{1,0:T(8,128)} %get-tuple-element.76.x, ...), custom_call_target="tpu_custom_call" | custom-call | tf_op jit(solution)/shard_map/mlp/pallas_call | solution.py:318
  471.7 30.3 %mlp_back.2 = (f32[512,1024]{1,0:T(8,128)}, bf16[512,1024]{1,0:T(8,128)(2,1)}, bf16[16,1024]{1,0:T(8,128)(2,1)}, bf16[16,1024]{1,0:T(8,128)(2,1)}, bf16[16,1024]...) custom-call(s32[4]{0:T(128)} %fusion.107.ids, ...), custom_call_target="tpu_custom_call" | custom-call | tf_op jit(solution)/shard_map/mlp_back/pallas_call | solution.py:318
  502.1 26.0 %attend_back.2 = (bf16[8,512,128]{2,1,0:T(8,128)(2,1)}, bf16[8,512,256]{2,1,0:T(8,128)(2,1)}, bf16[8,512,256]{2,1,0:T(8,128)(2,1)}) custom-call(s32[8]{0:T(128)} %select_n.36.bias, bf16[8,512,128]{2,1,0:T(8,128)(2,1)} %get-tuple-element.77.q, f32[8,8,512]{2,1,0:T(8,128)} %get-tuple-element.89.lse, bf16[512,1024]{1,0:T(8,128)(2,1)} %get-tuple-element.79.att.out, ...), custom_call_target="tpu_custom_call" | custom-call | tf_op jit(solution)/shard_map/attend_back/pallas_call | solution.py:318
  532.1 3.5 all-to-all-start.5
  535.7 8.2 %all-to-all-done.5 = bf16[8,16,1536]{2,1,0:T(8,128)(2,1)S(1)} async-done(((bf16[8,16,1536]{2,1,0:T(8,128)(2,1)}), bf16[8,16,1536]{2,1,0:T(8,128)(2,1)S(1)}, u32[]{:S(2)}, u32[]{:S(2)}) %all-to-all-start.5) | async-done | bytes 393248 | tf_op jit(solution)/shard_map/all_to_all | solution.py:868
  544.1 2.7 collective-permute-start.16
  546.8 13.8 %collective-permute-start.17 = (bf16[4,16,1536]{2,0,1:T(4,128)(2,1)S(1)}, bf16[4,16,1536]{2,0,1:T(4,128)(2,1)S(1)}, u32[]{:S(2)}, u32[]{:S(2)}) collective-permute-start(bf16[4,16,1536]{2,0,1:T(4,128)(2,1)S(1)} %copy.213), channel_id=1, source_target_pairs={{0,16},{8,24},{16,0},{24,8},{1,17},{9,25},{17,1},{25,9},{2,18},{10... | collective-permute-start | bytes 589832 | tf_op jit(solution)/shard_map/ppermute | solution.py:862
  560.6 2.0 collective-permute-start.4
  562.6 9.4 %collective-permute-done.4 = bf16[4,4,8]{1,2,0:T(8,128)(2,1)S(1)} collective-permute-done((bf16[4,4,8]{1,2,0:T(8,128)(2,1)S(1)}, bf16[4,4,8]{1,2,0:T(8,128)(2,1)S(1)}, u32[]{:S(2)}, u32[]{:S(2)}) %collective-permute-start.4) | collective-permute-done | bytes 288 | tf_op jit(solution)/shard_map/ppermute | solution.py:862
  572.0 1.9 collective-permute-start.5
  573.9 2.7 collective-permute-done.5
  576.6 3.6 collective-permute-done.6
  580.3 3.6 all-to-all-start
  586.9 13.6 %qkv_back.2 = (f32[512,1024]{1,0:T(8,128)}, bf16[16,1024]{1,0:T(8,128)(2,1)}, bf16[8,16,384]{2,1,0:T(8,128)(2,1)}) custom-call(s32[4]{0:T(128)} %fusion.107.ids, f32[512,1024]{1,0:T(8,128)} %get-tuple-element.87.g_mid, f32[512,1024]{1,0:T(8,128)} %get-tuple-element.76.x, f32[2,1,1024]{2,1,0:T(1,128)} %bitcast.310, f32[2,1,1024]{2,1,0:T(1,128)} %bitcast.306, ...), custom_call_target="tpu_custom_call" | custom-call | tf_op jit(solution)/shard_map/qkv_back/pallas_call | solution.py:318
  600.5 30.4 %mlp_back.3 = (f32[512,1024]{1,0:T(8,128)}, bf16[512,1024]{1,0:T(8,128)(2,1)}, bf16[16,1024]{1,0:T(8,128)(2,1)}, bf16[16,1024]{1,0:T(8,128)(2,1)}, bf16[16,1024]...) custom-call(s32[4]{0:T(128)} %fusion.107.ids, ...), custom_call_target="tpu_custom_call" | custom-call | tf_op jit(solution)/shard_map/mlp_back/pallas_call | solution.py:318
  632.3 26.1 %attend_back.3 = (bf16[8,512,128]{2,1,0:T(8,128)(2,1)}, bf16[8,512,256]{2,1,0:T(8,128)(2,1)}, bf16[8,512,256]{2,1,0:T(8,128)(2,1)}) custom-call(s32[8]{0:T(128)} %select_n.36.bias, bf16[8,512,128]{2,1,0:T(8,128)(2,1)} %get-tuple-element.70.q, f32[8,8,512]{2,1,0:T(8,128)} %get-tuple-element.102.lse, bf16[512,1024]{1,0:T(8,128)(2,1)} %get-tuple-element.72.att.out, ...), custom_call_target="tpu_custom_call" | custom-call | tf_op jit(solution)/shard_map/attend_back/pallas_call | solution.py:318
  662.2 3.9 all-to-all-start.3
  666.7 4.9 all-to-all-done.3
  672.2 3.5 all-to-all-start.4
  676.6 2.7 to_rows.2
  679.9 2.0 collective-permute-start.11
  681.9 2.4 collective-permute-start.12
  684.6 1.7 collective-permute-done.10
  688.4 2.6 collective-permute-start.15
  691.3 2.9 collective-permute-done.13
  694.2 8.1 %collective-permute-done.14 = bf16[4,16,1536]{2,0,1:T(4,128)(2,1)S(1)} collective-permute-done((bf16[4,16,1536]{2,0,1:T(4,128)(2,1)S(1)}, bf16[4,16,1536]{2,0,1:T(4,128)(2,1)S(1)}, u32[]{:S(2)}, u32[]{:S(2)}) %collective-permute-start.14) | collective-permute-done | bytes 196640 | tf_op jit(solution)/shard_map/ppermute | solution.py:862
  707.1 13.3 %qkv_back.3 = (bf16[8,512,128]{2,1,0:T(8,128)(2,1)}, bf16[16,1024]{1,0:T(8,128)(2,1)}, bf16[8,16,384]{2,1,0:T(8,128)(2,1)}) custom-call(s32[4]{0:T(128)} %fusion.107.ids, f32[512,1024]{1,0:T(8,128)} %get-tuple-element.100.g_mid, f32[512,1024]{1,0:T(8,128)} %convert_element_type.11.x, f32[2,1,1024]{2,1,0:T(1,128)} %bitcast.311, f32[2,1,1024]{2,1,0:T(1,128)} %bitcast.307, ...), custom_call_target="tpu_custom_call" | custom-call | tf_op jit(solution)/shard_map/qkv_back/pallas_call | solution.py:318
  721.2 1.6 pad_maximum_fusion.10
  722.8 4.0 all-to-all-start.2
  726.9 5.4 all-to-all-done.2
  732.3 3.6 all-to-all-start.1
  736.8 4.2 collective-permute-start.7
  741.1 1.8 collective-permute-start.8
  745.3 2.6 collective-permute-done.8
  752.2 2.7 to_rows.3
  (179 shorter events, 49.6 us)
Async XLA Ops:
  0.6 326.7 %copy-start = (bf16[2,8,16,3,1024]{4,2,3,1,0:T(8,128)(2,1)S(1)}, bf16[2,8,16,3,1024]{4,2,3,1,0:T(8,128)(2,1)}, u32[]{:S(2)}) copy-start(bf16[2,8,16,3,1024]{4,2,3,1,0:T(8,128)(2,1)} %param.40) | copy-start | bytes 4718596
  333.9 11.3 %copy-start.30 = (s32[2,2]{1,0:T(2,128)S(1)}, s32[2,2]{1,0:T(2,128)}, u32[]{:S(2)}) copy-start(s32[2,2]{1,0:T(2,128)} %constant.48.clone) | copy-start | bytes 52
  344.7 21.1 %collective-permute-start = (bf16[8,512,256]{2,1,0:T(8,128)(2,1)}, bf16[8,512,256]{2,1,0:T(8,128)(2,1)S(1)}, u32[]{:S(2)}, u32[]{:S(2)}) collective-permute-start(bf16[8,512,256]{2,1,0:T(8,128)(2,1)} %get-tuple-element.71.refs_0_), channel_id=1, source_target_pairs={{0,1},{1,0},{2,3},{3,2},{4,5},{5,4},{6,7},{7,6},{8,9},{9,8},{10,11... | collective-permute-start | bytes 6291464 | tf_op jit(solution)/shard_map/ppermute | solution.py:832
  346.6 12.9 %copy-start.9 = (bf16[2,8,1024,16]{2,3,1,0:T(8,128)(2,1)S(1)}, bf16[2,8,1024,16]{2,3,1,0:T(8,128)(2,1)}, u32[]{:S(2)}) copy-start(bf16[2,8,1024,16]{2,3,1,0:T(8,128)(2,1)} %param.41) | copy-start | bytes 1572868
  411.1 11.0 %copy-start.6 = (bf16[512,1024]{1,0:T(8,128)(2,1)S(1)}, bf16[512,1024]{1,0:T(8,128)(2,1)}, u32[]{:S(2)}) copy-start(bf16[512,1024]{1,0:T(8,128)(2,1)} %get-tuple-element.81) | copy-start | bytes 3145732
  422.0 4.4 collective-permute-start.1
  502.1 26.2 %copy-start.29 = (bf16[16,1024]{1,0:T(8,128)(2,1)S(1)}, bf16[16,1024]{1,0:T(8,128)(2,1)}, u32[]{:S(2)}) copy-start(bf16[16,1024]{1,0:T(8,128)(2,1)} %get-tuple-element.118) | copy-start | bytes 98308
  502.1 26.9 %copy-start.28 = (bf16[16,1024]{1,0:T(8,128)(2,1)S(1)}, bf16[16,1024]{1,0:T(8,128)(2,1)}, u32[]{:S(2)}) copy-start(bf16[16,1024]{1,0:T(8,128)(2,1)} %get-tuple-element.119) | copy-start | bytes 98308
  502.1 27.5 %copy-start.27 = (bf16[16,1024]{1,0:T(8,128)(2,1)S(1)}, bf16[16,1024]{1,0:T(8,128)(2,1)}, u32[]{:S(2)}) copy-start(bf16[16,1024]{1,0:T(8,128)(2,1)} %get-tuple-element.120) | copy-start | bytes 98308
  502.1 28.1 %copy-start.20 = (bf16[16,4096]{1,0:T(8,128)(2,1)S(1)}, bf16[16,4096]{1,0:T(8,128)(2,1)}, u32[]{:S(2)}) copy-start(bf16[16,4096]{1,0:T(8,128)(2,1)} %get-tuple-element.121) | copy-start | bytes 393220
  502.1 28.7 %copy-start.19 = (bf16[16,4096]{1,0:T(8,128)(2,1)S(1)}, bf16[16,4096]{1,0:T(8,128)(2,1)}, u32[]{:S(2)}) copy-start(bf16[16,4096]{1,0:T(8,128)(2,1)} %get-tuple-element.122) | copy-start | bytes 393220
  502.1 29.4 %copy-start.26 = (bf16[16,1024]{1,0:T(8,128)(2,1)S(1)}, bf16[16,1024]{1,0:T(8,128)(2,1)}, u32[]{:S(2)}) copy-start(bf16[16,1024]{1,0:T(8,128)(2,1)} %get-tuple-element.123) | copy-start | bytes 98308
  502.1 33.5 %copy-start.31 = (s32[4,4]{1,0:T(4,128)S(1)}, s32[4,4]{1,0:T(4,128)}, u32[]{:S(2)}) copy-start(s32[4,4]{1,0:T(4,128)} %param.26) | copy-start | bytes 196
  528.1 58.8 %collective-permute-start.2 = (bf16[8,512,256]{2,1,0:T(8,128)(2,1)}, bf16[8,512,256]{2,1,0:T(8,128)(2,1)}, u32[]{:S(2)}, u32[]{:S(2)}) collective-permute-start(bf16[8,512,256]{2,1,0:T(8,128)(2,1)} %get-tuple-element.93), channel_id=1, source_target_pairs={{0,1},{1,0},{2,3},{3,2},{4,5},{5,4},{6,7},{7,6},{8,9},{9,8},{10,11... | collective-permute-start | bytes 6291464 | tf_op jit(solution)/shard_map/ppermute | solution.py:832
  532.1 11.7 %all-to-all-start.5 = ((bf16[8,16,1536]{2,1,0:T(8,128)(2,1)}), bf16[8,16,1536]{2,1,0:T(8,128)(2,1)S(1)}, u32[]{:S(2)}, u32[]{:S(2)}) async-start(bf16[8,16,1536]{2,1,0:T(8,128)(2,1)} %constant_dynamic-update-slice_fusion.12), calls=%async_computation.5 | async-start | bytes 786432 | tf_op jit(solution)/shard_map/all_to_all | solution.py:868
  544.1 39.8 %collective-permute-start.16 = (bf16[4,16,1536]{2,0,1:T(4,128)(2,1)S(1)}, bf16[4,16,1536]{2,0,1:T(4,128)(2,1)S(1)}, u32[]{:S(2)}, u32[]{:S(2)}) collective-permute-start(bf16[4,16,1536]{2,0,1:T(4,128)(2,1)S(1)} %copy.213), channel_id=1, source_target_pairs={{0,8},{8,16},{16,24},{24,0},{1,9},{9,17},{17,25},{25,1},{2,10},{10... | collective-permute-start | bytes 589832 | tf_op jit(solution)/shard_map/ppermute | solution.py:862
  546.8 37.1 %collective-permute-start.17 = (bf16[4,16,1536]{2,0,1:T(4,128)(2,1)S(1)}, bf16[4,16,1536]{2,0,1:T(4,128)(2,1)S(1)}, u32[]{:S(2)}, u32[]{:S(2)}) collective-permute-start(bf16[4,16,1536]{2,0,1:T(4,128)(2,1)S(1)} %copy.213), channel_id=1, source_target_pairs={{0,16},{8,24},{16,0},{24,8},{1,17},{9,25},{17,1},{25,9},{2,18},{10... | collective-permute-start | bytes 589832 | tf_op jit(solution)/shard_map/ppermute | solution.py:862
  560.6 23.3 %collective-permute-start.18 = (bf16[4,16,1536]{2,0,1:T(4,128)(2,1)S(1)}, bf16[4,16,1536]{2,0,1:T(4,128)(2,1)S(1)}, u32[]{:S(2)}, u32[]{:S(2)}) collective-permute-start(bf16[4,16,1536]{2,0,1:T(4,128)(2,1)S(1)} %copy.213), channel_id=1, source_target_pairs={{0,24},{8,0},{16,8},{24,16},{1,25},{9,1},{17,9},{25,17},{2,26},{10... | collective-permute-start | bytes 589832 | tf_op jit(solution)/shard_map/ppermute | solution.py:862
  560.6 11.4 %collective-permute-start.4 = (bf16[4,4,8]{1,2,0:T(8,128)(2,1)S(1)}, bf16[4,4,8]{1,2,0:T(8,128)(2,1)S(1)}, u32[]{:S(2)}, u32[]{:S(2)}) collective-permute-start(bf16[4,4,8]{1,2,0:T(8,128)(2,1)S(1)} %fusion.84), channel_id=1, source_target_pairs={{0,8},{8,16},{16,24},{24,0},{1,9},{9,17},{17,25},{25,1},{2,10},{10... | collective-permute-start | bytes 776 | tf_op jit(solution)/shard_map/ppermute | solution.py:862
  572.0 4.5 collective-permute-start.5
  576.6 3.7 collective-permute-start.6
  580.3 81.9 %all-to-all-start = ((bf16[8,512,128]{2,1,0:T(8,128)(2,1)}), bf16[8,512,128]{2,1,0:T(8,128)(2,1)S(1)}, u32[]{:S(2)}, u32[]{:S(2)}) async-start(bf16[8,512,128]{2,1,0:T(8,128)(2,1)} %get-tuple-element.80), calls=%async_computation | async-start | bytes 2097152 | tf_op jit(solution)/shard_map/all_to_all | solution.py:837
  632.3 26.6 %copy-start.23 = (bf16[16,1024]{1,0:T(8,128)(2,1)S(1)}, bf16[16,1024]{1,0:T(8,128)(2,1)}, u32[]{:S(2)}) copy-start(bf16[16,1024]{1,0:T(8,128)(2,1)} %get-tuple-element.110) | copy-start | bytes 98308
  632.3 26.6 %copy-start.21 = (bf16[8,16,384]{2,1,0:T(8,128)(2,1)S(1)}, bf16[8,16,384]{2,1,0:T(8,128)(2,1)}, u32[]{:S(2)}) copy-start(bf16[8,16,384]{2,1,0:T(8,128)(2,1)} %get-tuple-element.111) | copy-start | bytes 294916
  632.3 27.3 %copy-start.25 = (bf16[16,1024]{1,0:T(8,128)(2,1)S(1)}, bf16[16,1024]{1,0:T(8,128)(2,1)}, u32[]{:S(2)}) copy-start(bf16[16,1024]{1,0:T(8,128)(2,1)} %get-tuple-element.113) | copy-start | bytes 98308
  632.3 27.9 %copy-start.24 = (bf16[16,1024]{1,0:T(8,128)(2,1)S(1)}, bf16[16,1024]{1,0:T(8,128)(2,1)}, u32[]{:S(2)}) copy-start(bf16[16,1024]{1,0:T(8,128)(2,1)} %get-tuple-element.114) | copy-start | bytes 98308
  632.3 28.6 %copy-start.18 = (bf16[16,4096]{1,0:T(8,128)(2,1)S(1)}, bf16[16,4096]{1,0:T(8,128)(2,1)}, u32[]{:S(2)}) copy-start(bf16[16,4096]{1,0:T(8,128)(2,1)} %get-tuple-element.115) | copy-start | bytes 393220
  632.3 29.2 %copy-start.17 = (bf16[16,4096]{1,0:T(8,128)(2,1)S(1)}, bf16[16,4096]{1,0:T(8,128)(2,1)}, u32[]{:S(2)}) copy-start(bf16[16,4096]{1,0:T(8,128)(2,1)} %get-tuple-element.116) | copy-start | bytes 393220
  632.3 33.7 %copy-start.22 = (bf16[16,1024]{1,0:T(8,128)(2,1)S(1)}, bf16[16,1024]{1,0:T(8,128)(2,1)}, u32[]{:S(2)}) copy-start(bf16[16,1024]{1,0:T(8,128)(2,1)} %get-tuple-element.117) | copy-start | bytes 98308
  658.4 48.7 %collective-permute-start.3 = (bf16[8,512,256]{2,1,0:T(8,128)(2,1)}, bf16[8,512,256]{2,1,0:T(8,128)(2,1)}, u32[]{:S(2)}, u32[]{:S(2)}) collective-permute-start(bf16[8,512,256]{2,1,0:T(8,128)(2,1)} %get-tuple-element.106), channel_id=1, source_target_pairs={{0,1},{1,0},{2,3},{3,2},{4,5},{5,4},{6,7},{7,6},{8,9},{9,8},{10,11... | collective-permute-start | bytes 6291464 | tf_op jit(solution)/shard_map/ppermute | solution.py:832
  662.2 14.5 %copy-start.4 = (bf16[8,512,128]{2,1,0:T(8,128)(2,1)}, bf16[8,512,128]{2,1,0:T(8,128)(2,1)S(1)}, u32[]{:S(2)}) copy-start(bf16[8,512,128]{2,1,0:T(8,128)(2,1)S(1)} %all-to-all-done) | copy-start | bytes 3145732
  662.2 9.4 %all-to-all-start.3 = ((bf16[8,16,512]{2,1,0:T(8,128)(2,1)}), bf16[8,16,512]{2,1,0:T(8,128)(2,1)S(1)}, u32[]{:S(2)}, u32[]{:S(2)}) async-start(bf16[8,16,512]{2,1,0:T(8,128)(2,1)} %pad_maximum_fusion.11), calls=%async_computation.3 | async-start | bytes 262144 | tf_op jit(solution)/shard_map/all_to_all | solution.py:868
  672.2 12.0 %all-to-all-start.4 = ((bf16[8,16,1536]{2,1,0:T(8,128)(2,1)}), bf16[8,16,1536]{2,1,0:T(8,128)(2,1)S(1)}, u32[]{:S(2)}, u32[]{:S(2)}) async-start(bf16[8,16,1536]{2,1,0:T(8,128)(2,1)} %constant_dynamic-update-slice_fusion.8), calls=%async_computation.4 | async-start | bytes 786432 | tf_op jit(solution)/shard_map/all_to_all | solution.py:868
  679.3 23.1 %copy-start.15 = (f32[1,8,16,128]{3,1,2,0:T(8,128)S(1)}, f32[1,8,16,128]{3,1,2,0:T(8,128)}, u32[]{:S(2)}) copy-start(f32[1,8,16,128]{3,1,2,0:T(8,128)} %convolution_bitcast_fusion.6) | copy-start | bytes 196612
  679.4 6.9 collective-permute-start.10
  679.9 8.5 %collective-permute-start.11 = (bf16[4,16,512]{2,0,1:T(4,128)(2,1)S(1)}, bf16[4,16,512]{2,0,1:T(4,128)(2,1)S(1)}, u32[]{:S(2)}, u32[]{:S(2)}) collective-permute-start(bf16[4,16,512]{2,0,1:T(4,128)(2,1)S(1)} %copy.191), channel_id=1, source_target_pairs={{0,16},{8,24},{16,0},{24,8},{1,17},{9,25},{17,1},{25,9},{2,18},{10... | collective-permute-start | bytes 196616 | tf_op jit(solution)/shard_map/ppermute | solution.py:862
  681.9 9.1 %collective-permute-start.12 = (bf16[4,16,512]{2,0,1:T(4,128)(2,1)S(1)}, bf16[4,16,512]{2,0,1:T(4,128)(2,1)S(1)}, u32[]{:S(2)}, u32[]{:S(2)}) collective-permute-start(bf16[4,16,512]{2,0,1:T(4,128)(2,1)S(1)} %copy.191), channel_id=1, source_target_pairs={{0,24},{8,0},{16,8},{24,16},{1,25},{9,1},{17,9},{25,17},{2,26},{10... | collective-permute-start | bytes 196616 | tf_op jit(solution)/shard_map/ppermute | solution.py:862
  684.5 9.7 %collective-permute-start.13 = (bf16[4,16,1536]{2,0,1:T(4,128)(2,1)S(1)}, bf16[4,16,1536]{2,0,1:T(4,128)(2,1)S(1)}, u32[]{:S(2)}, u32[]{:S(2)}) collective-permute-start(bf16[4,16,1536]{2,0,1:T(4,128)(2,1)S(1)} %copy.203), channel_id=1, source_target_pairs={{0,8},{8,16},{16,24},{24,0},{1,9},{9,17},{17,25},{25,1},{2,10},{10... | collective-permute-start | bytes 589832 | tf_op jit(solution)/shard_map/ppermute | solution.py:862
  686.3 16.0 %collective-permute-start.14 = (bf16[4,16,1536]{2,0,1:T(4,128)(2,1)S(1)}, bf16[4,16,1536]{2,0,1:T(4,128)(2,1)S(1)}, u32[]{:S(2)}, u32[]{:S(2)}) collective-permute-start(bf16[4,16,1536]{2,0,1:T(4,128)(2,1)S(1)} %copy.203), channel_id=1, source_target_pairs={{0,16},{8,24},{16,0},{24,8},{1,17},{9,25},{17,1},{25,9},{2,18},{10... | collective-permute-start | bytes 589832 | tf_op jit(solution)/shard_map/ppermute | solution.py:862
  688.4 13.9 %collective-permute-start.15 = (bf16[4,16,1536]{2,0,1:T(4,128)(2,1)S(1)}, bf16[4,16,1536]{2,0,1:T(4,128)(2,1)S(1)}, u32[]{:S(2)}, u32[]{:S(2)}) collective-permute-start(bf16[4,16,1536]{2,0,1:T(4,128)(2,1)S(1)} %copy.203), channel_id=1, source_target_pairs={{0,24},{8,0},{16,8},{24,16},{1,25},{9,1},{17,9},{25,17},{2,26},{10... | collective-permute-start | bytes 589832 | tf_op jit(solution)/shard_map/ppermute | solution.py:862
  720.4 15.5 %copy-start.13 = (f32[1,8,16,128]{3,1,2,0:T(8,128)S(1)}, f32[1,8,16,128]{3,1,2,0:T(8,128)}, u32[]{:S(2)}) copy-start(f32[1,8,16,128]{3,1,2,0:T(8,128)} %convolution_bitcast_fusion.10) | copy-start | bytes 196612
  722.8 9.5 %all-to-all-start.2 = ((bf16[8,16,512]{2,1,0:T(8,128)(2,1)}), bf16[8,16,512]{2,1,0:T(8,128)(2,1)S(1)}, u32[]{:S(2)}, u32[]{:S(2)}) async-start(bf16[8,16,512]{2,1,0:T(8,128)(2,1)} %pad_maximum_fusion.10), calls=%async_computation.2 | async-start | bytes 262144 | tf_op jit(solution)/shard_map/all_to_all | solution.py:868
  726.9 16.6 %copy-start.16 = (f32[1,8,16,128]{3,1,2,0:T(8,128)S(1)}, f32[1,8,16,128]{3,1,2,0:T(8,128)}, u32[]{:S(2)}) copy-start(f32[1,8,16,128]{3,1,2,0:T(8,128)} %convolution_bitcast_fusion.12) | copy-start | bytes 196612
  732.3 18.9 %all-to-all-start.1 = ((bf16[8,512,128]{2,1,0:T(8,128)(2,1)}), bf16[8,512,128]{2,1,0:T(8,128)(2,1)S(1)}, u32[]{:S(2)}, u32[]{:S(2)}) async-start(bf16[8,512,128]{2,1,0:T(8,128)(2,1)} %get-tuple-element.107), calls=%async_computation.1 | async-start | bytes 2097152 | tf_op jit(solution)/shard_map/all_to_all | solution.py:837
  736.8 8.5 %collective-permute-start.7 = (bf16[4,16,512]{2,0,1:T(4,128)(2,1)S(1)}, bf16[4,16,512]{2,0,1:T(4,128)(2,1)S(1)}, u32[]{:S(2)}, u32[]{:S(2)}) collective-permute-start(bf16[4,16,512]{2,0,1:T(4,128)(2,1)S(1)} %copy.186), channel_id=1, source_target_pairs={{0,8},{8,16},{16,24},{24,0},{1,9},{9,17},{17,25},{25,1},{2,10},{10... | collective-permute-start | bytes 196616 | tf_op jit(solution)/shard_map/ppermute | solution.py:862
  741.1 6.8 collective-permute-start.8
  742.9 5.5 collective-permute-start.9
  748.6 6.3 copy-start.1
  (9 other events, 20.4 us)

commit v3 on v1

v3 whole, which is shorter than its diff:
```python
import functools

import jax
import jax.numpy as jnp
from jax import lax
from jax.experimental import pallas as pl
from jax.experimental.pallas import tpu as pltpu
from jax.sharding import PartitionSpec as P

HD = 64
LEN = 1024
BLOCK = 256
BLOCKS = LEN // BLOCK
EPSILON = 1e-05
SCALE = HD**-0.5
ROOT = (2.0 / 3.141592653589793) ** 0.5
MESH = pl.DeviceIdType.MESH
F32 = jnp.float32
BF16 = jnp.bfloat16


ROW_FIRST = (("z", 0, 1), ("z", 1, 0))
ROW_SECOND = ((0, "z", 1), (1, "z", 0))
ORDERS = {"qkv": (ROW_SECOND,), "proj": (ROW_SECOND,), "up": (ROW_FIRST,) * 2, "down": (ROW_FIRST,) * 2}
KINDS = ("qkv", "proj", "up", "down")
DEPTH = 4
FUSED = True
LINK = 90e3


def transfer_plan(order):
    masks, rows, steps = [0], False, []
    for d in order:
        steps.append((d, tuple(masks), rows))
        if d == "z":
            rows = True
        else:
            masks = masks + [m ^ d for m in masks]
    steps.append((None, tuple(masks), rows))
    return steps


def transfer_schedule(pieces, n_row, tasks):
    cost, parts = {}, {}
    for k, (name, order, size) in enumerate(pieces):
        parts.setdefault(name, set()).add(k)
        for p, (d, masks, rows) in enumerate(transfer_plan(order)[:-1]):
            load = (n_row // 2) * (n_row - n_row // 2) if d == "z" else (n_row if rows else 1)
            cost[k, p] = (d, 2 * len(masks) * load * size / LINK)
    ready = {d: [] for d, _ in cost.values()}
    free = dict.fromkeys(ready, 0.0)
    flight = {d: [] for d in ready}
    for k in range(len(pieces)):
        ready[cost[k, 0][0]].append((k, 0))
    tasks, left = list(tasks), {}
    for task in tasks:
        left[task[4]] = left.get(task[4], 0) + 1
    landed, staged, now, ops = {}, {}, 0.0, []

    def stage(name):
        kind, l = name
        if name in landed and name not in staged and landed[name] <= now and not left.get((kind, l - 1)):
            staged[name] = now + 3.0
            ops.append(("stage", kind, l))

    while tasks or any(ready.values()) or any(flight.values()):
        for d in ready:
            while ready[d] and len(flight[d]) < DEPTH:
                k, p = ready[d].pop(0)
                free[d] = max(now, free[d]) + cost[k, p][1]
                flight[d].append((free[d], k, p))
                ops.append(("start", k, p))
        if tasks:
            for name in list(landed):
                stage(name)
        events = [f for line in flight.values() for f in line]
        event = min(events) if events else None
        due = None
        if tasks:
            need = tasks[0][4]
            due = now if need is None else staged.get(need)
            if due is None and need in landed and not left.get((need[0], need[1] - 1)):
                due = landed[need]
        if due is not None and (event is None or max(due, now) < event[0]):
            now = max(due, now)
            need = tasks[0][4]
            if need is not None and need not in staged:
                continue
            name, l, part, micros, _ = tasks.pop(0)
            left[need] -= 1
            now += micros
            ops.append(("task", name, (l, part)))
            continue
        now, k, p = max(now, event[0]), event[1], event[2]
        d = cost[k, p][0]
        flight[d].remove(event)
        ops.append(("wait", k, p))
        if (k, p + 1) in cost:
            later = ready[cost[k, p + 1][0]]
            later.append((k, p + 1))
            later.sort()
        else:
            name = pieces[k][0]
            parts[name].discard(k)
            if not parts[name]:
                landed[name] = now + 4.0
    return ops


def place_of(group, g, b):
    if group == 2:
        return g + b * (BLOCKS - 1 - 2 * g)
    return g * (BLOCKS // group) + b


def positions(group):
    per = BLOCKS // group
    return tuple(tuple(place_of(group, g, b) for b in range(per)) for g in range(group))


NARROW = 8
CROSS = ((0,), (0,))
TURNED = ((1,), (1,))


def dot(a, b, dims=((1,), (0,))):
    return lax.dot_general(a, b, (dims, ((), ())), preferred_element_type=F32)


def columns(i, size=128):
    if isinstance(i, int):
        return pl.ds(i * size, size)
    return pl.ds(pl.multiple_of(i * size, size), size)


def norm_parts(x):
    center = x - jnp.mean(x, axis=1, keepdims=True)
    inverse = lax.rsqrt(jnp.mean(center * center, axis=1, keepdims=True) + EPSILON)
    return center * inverse, inverse


def norm_grad(grad, scaled, inverse, gain):
    w = grad * gain
    first = jnp.mean(w, axis=1, keepdims=True)
    second = jnp.mean(w * scaled, axis=1, keepdims=True)
    return inverse * (w - first - scaled * second)


def norm_low(x, gain, shift):
    return (norm_parts(x)[0] * gain + shift).astype(BF16)


def pair_state(held):
    group, per = len(held), len(held[0])
    state = {}
    for s in range(per):
        for j in range(group):
            for b in range(per):
                seen = {held[(g - j) % group][b] <= held[g][s] for g in range(group)}
                state[s, j, b] = 0 if len(seen) == 2 else (1 if True in seen else -1)
    return state


def pair_bias(held, g):
    group = len(held)
    bias = {}
    for (s, j, b), state in pair_state(held).items():
        if state == 0:
            keys = place_of(group, lax.rem(g - j + group, group), b)
            bias[s, j, b] = jnp.where(keys <= place_of(group, g, s), 0.0, -1e9).astype(F32)
    return bias


def head_mask(h):
    lane = lax.broadcasted_iota(jnp.int32, (1, 128), 1)
    return (lane // HD) == h


def attend_strip(held, bias, i, q, kvs, out, lse):
    group, per = len(held), len(held[0])
    state = pair_state(held)
    turned = {}
    for s in range(per):
        rows = pl.ds(s * BLOCK, BLOCK)
        queries = q[i, rows, :] * SCALE
        pieces = []
        for h in range(2):
            query = jnp.where(head_mask(h), queries, 0).astype(BF16)
            scores, values = [], []
            for j in range(group):
                for b in range(per):
                    if state[s, j, b] < 0:
                        continue
                    keys = kvs[j][i, b * BLOCK : (b + 1) * BLOCK, :128]
                    score = dot(keys, query, TURNED)
                    if state[s, j, b] == 0:
                        score = score + bias[s, j, b]
                    scores.append(score)
                    if (j, b) not in turned:
                        turned[j, b] = kvs[j][i, b * BLOCK : (b + 1) * BLOCK, 128:].T
                    values.append(turned[j, b][h * HD : (h + 1) * HD])
            top = functools.reduce(jnp.maximum, [jnp.max(x, axis=0, keepdims=True) for x in scores])
            total, made = 0.0, 0.0
            for score, value in zip(scores, values):
                e = jnp.exp(score - top)
                total = total + jnp.sum(e, axis=0, keepdims=True)
                made = made + dot(value, e.astype(BF16))
            pieces.append(made / total)
            lse[i, h : h + 1, rows] = top + jnp.log(total)
        out[rows, columns(i)] = jnp.concatenate(pieces, axis=0).T.astype(BF16)


def attend_back_strip(held, bias, i, q, lse, out, grad, kvs, gq, gkvs):
    group, per = len(held), len(held[0])
    state = pair_state(held)
    turned, gk, gv = {}, {}, {}
    for s in range(per):
        rows = pl.ds(s * BLOCK, BLOCK)
        queries = q[i, rows, :] * SCALE
        up = grad[rows, columns(i)]
        product = (up.astype(F32) * out[rows, columns(i)].astype(F32)).T
        pieces = []
        for h in range(2):
            query = jnp.where(head_mask(h), queries, 0).astype(BF16)
            given = jnp.where(head_mask(h), up, 0).astype(BF16)
            inner = jnp.sum(product[h * HD : (h + 1) * HD], axis=0, keepdims=True)
            level = lse[i, h : h + 1, rows]
            made = 0.0
            for j in range(group):
                for b in range(per):
                    if state[s, j, b] < 0:
                        continue
                    keys = kvs[j][i, b * BLOCK : (b + 1) * BLOCK, :128]
                    values = kvs[j][i, b * BLOCK : (b + 1) * BLOCK, 128:]
                    score = dot(keys, query, TURNED)
                    if state[s, j, b] == 0:
                        score = score + bias[s, j, b]
                    probs = jnp.exp(score - level)
                    g_probs = dot(values, given, TURNED)
                    g_scores = (probs * (g_probs - inner)).astype(BF16)
                    if (j, b) not in turned:
                        turned[j, b] = keys.T
                        gk[j, b], gv[j, b] = 0.0, 0.0
                    gv[j, b] = gv[j, b] + dot(probs.astype(BF16), given)
                    gk[j, b] = gk[j, b] + dot(g_scores, query)
                    made = made + dot(turned[j, b][h * HD : (h + 1) * HD], g_scores)
            pieces.append(made)
        gq[i, rows, :] = (jnp.concatenate(pieces, axis=0) * SCALE).T.astype(BF16)
    for j in range(group):
        for b in range(per):
            rows = pl.ds(b * BLOCK, BLOCK)
            gkvs[j][i, rows, :128] = gk[j, b].astype(BF16)
            gkvs[j][i, rows, 128:] = gv[j, b].astype(BF16)


def by_rows(count, body, size=128):
    each(count // size, lambda n: body(pl.ds(pl.multiple_of(n * size, size), size)))


def keep(value, red, red_out):
    red[...] = value.astype(BF16)
    red_out[...] = value.T.astype(BF16)


def each(count, body):
    def step(i, carry):
        body(i)
        return carry

    lax.fori_loop(0, count, step, 0)


def qkv_stage(x, gain, shift, w, bias, low, up, q, kv, red, red_out, normed):
    def norm(rows):
        normed[rows, :] = norm_low(x[rows, :], gain, shift)

    by_rows(x.shape[0], norm)
    keep(dot(normed[...], low[...], TURNED), red, red_out)

    def pair(j):
        made = dot(normed[...], w[j])
        for n in range(2):
            i = 2 * j + n
            mixed = made[:, n * 384 : (n + 1) * 384] + (bias[i] + dot(red[...], up[i]))
            q[i] = mixed[:, :128].astype(BF16)
            kv[i] = mixed[:, 128:].astype(BF16)

    each(NARROW // 2, pair)


def proj_stage(x, att, w, bias, low, up, gain, shift, low_up, mid, normed, red, red_out, red_up, red_up_out):
    keep(dot(att[...], low[...], TURNED), red, red_out)

    def part(rows):
        value = x[rows, :] + (dot(att[rows, :], w[...]) + bias + dot(red[rows, :], up[...]))
        mid[rows, :] = value
        normed[rows, :] = norm_low(value, gain, shift)

    by_rows(x.shape[0], part, 256)
    keep(dot(normed[...], low_up[...], TURNED), red_up, red_up_out)


def up_strip(i, normed, w, bias, red_up, up, hidden, active):
    units = w.shape[2]
    cols = columns(i, units)
    value = dot(normed[...], w[i]) + (bias[i] + dot(red_up[...], up[:, cols]))
    hidden[:, cols] = value.astype(BF16)
    inner = ROOT * (value + 0.044715 * (value * value * value))
    active[:, cols] = (0.5 * value * (1.0 + jnp.tanh(inner))).astype(BF16)


def down_stage(mid, active, w, bias, low, up, red, red_out, put):
    keep(dot(active[...], low[...], TURNED), red, red_out)

    for n in range(mid.shape[1] // 256):
        cols = slice(n * 256, (n + 1) * 256)
        put(n, mid[:, cols] + (dot(active[...], w[:, cols]) + bias[:, cols] + dot(red[...], up[:, cols])))


def gelu_parts(x):
    square = x * x
    t = jnp.tanh(ROOT * (x + 0.044715 * (x * square)))
    half = 0.5 * (1.0 + t)
    slope = half + 0.5 * x * (1.0 - t * t) * (ROOT * (1.0 + 3 * 0.044715 * square))
    return x * half, slope


class Vectors:
    def __init__(self, ref, l):
        self.ref, self.l = ref, l

    def qkv(self, i):
        return self.ref[i, pl.ds(4 * self.l, 1), :384]

    def up(self, i):
        return self.ref[i, pl.ds(4 * self.l + 1, 1), :]

    def row(self, name):
        at = ("proj", "down", "gain1", "shift1", "gain2", "shift2").index(name)
        row, lane = 4 * self.l + 2 + at // 4, at % 4 * 128
        return jnp.concatenate([self.ref[i, row : row + 1, lane : lane + 128] for i in range(NARROW)], axis=1)


class Strips:
    def __init__(self, read):
        self.read = read

    def __getitem__(self, i):
        return self.read(i)


TABLES = ("low_qkv", "up_qkv", "low_proj", "up_proj", "low_up", "up_up", "low_down", "up_down")
SAVED = ("q", "kv", "peer", "att", "lse", "mid", "hidden", "x")


def task_list(layers):
    tasks = [("load", 0, 0, 3.0, None)]
    for l in range(layers):
        tasks.append(("qkv", l, 0, 7.0, ("qkv", l)))
        tasks += [("attend", l, n, 5.0, None) for n in range(4)]
        tasks.append(("proj", l, 0, 4.0, ("proj", l)))
        tasks += [("up", l, n, 5.0, ("up", l)) for n in range(2)]
        tasks.append(("down", l, 0, 6.0, ("down", l)))
    return tasks


class ForwardWork:
    def __init__(self, n_col, group, refs):
        self.__dict__.update(refs)
        self.group = group
        self.held = positions(group)
        self.r, self.c = lax.axis_index("row"), lax.axis_index("col")
        self.g = lax.rem(self.c, group)
        self.bias = pair_bias(self.held, self.g)
        self.layers = self.low_qkv.shape[0]

    def stage_copies(self, kind, l):
        full = self.full[kind]
        if kind == "qkv":
            pieces = []
            for i in range(NARROW):
                src = full.at[l, i]
                pieces.append((src, self.wq.at[i // 2, :, :, :, pl.ds(i % 2 * 384, 384)]))
            return pieces, self.wq
        if kind == "up":
            return [(full.at[l, i], self.wu.at[i]) for i in range(NARROW)], self.wu
        target = self.wp if kind == "proj" else self.wd
        return [(full.at[l, i], target.at[i]) for i in range(NARROW)], target

    def stage(self, kind, l):
        for src, dst in self.stage_copies(kind, l)[0]:
            pltpu.make_async_copy(src, dst, self.stage_sem.at[KINDS.index(kind)]).start()

    def staged(self, kind, l):
        target = self.stage_copies(kind, l)[1]
        pltpu.make_async_copy(target, target, self.stage_sem.at[KINDS.index(kind)]).wait()

    def save_copy(self, name, l):
        src = {
            "q": self.q, "kv": self.kv, "peer": self.peer.at[l], "att": self.att, "lse": self.lse,
            "mid": self.mid, "hidden": self.hidden, "x": self.x,
        }[name]
        return pltpu.make_async_copy(src, self.saved[name].at[l], self.save_sem.at[l, SAVED.index(name)])

    def save(self, *names, l):
        for name in names:
            self.save_copy(name, l).start()

    def settled(self, *names, l):
        if l >= 0:
            for name in names:
                self.save_copy(name, l).wait()

    def exchange(self, l, s):
        to = self.c - self.g + lax.rem(self.g + s, self.group)
        return pltpu.make_async_remote_copy(
            src_ref=self.kv, dst_ref=self.peer.at[l, s - 1],
            send_sem=self.kv_send.at[l, s - 1], recv_sem=self.kv_recv.at[l, s - 1],
            device_id=(self.r, to), device_id_type=MESH,
        )

    def run(self, name, l, part):
        vec = Vectors(self.vec, l)
        if name == "load":
            self.arrive_tokens()
            self.x[...] = self.tokens_v[...].astype(F32)
        elif name == "qkv":
            self.staged("qkv", l)
            self.settled("q", "kv", l=l - 1)
            if l > 0:
                for s in range(1, self.group):
                    self.exchange(l - 1, s).wait_send()
            w = self.wq.reshape(NARROW // 2, -1, 768)
            qkv_stage(
                self.x, vec.row("gain1"), vec.row("shift1"), w, Strips(vec.qkv), self.low_qkv.at[l],
                self.up_qkv.at[l], self.q, self.kv, self.red, self.reds.at[l, 0], self.normed,
            )
            for s in range(1, self.group):
                self.exchange(l, s).start()
            self.save("q", "kv", l=l)
        elif name == "attend":
            if part == 0:
                for s in range(1, self.group):
                    self.exchange(l, s).wait_recv()
                self.save("peer", l=l)
                self.settled("att", "lse", l=l - 1)
            kvs = [self.kv] + [self.peer.at[l, s - 1] for s in range(1, self.group)]
            size = NARROW // 4
            each(size, lambda n: attend_strip(self.held, self.bias, part * size + n, self.q, kvs, self.att, self.lse))
            if part == 3:
                self.save("att", "lse", l=l)
        elif name == "proj":
            self.staged("proj", l)
            self.settled("mid", l=l - 1)
            dim = self.att.shape[1]
            proj_stage(
                self.x, self.att, self.wp.reshape(dim, dim), vec.row("proj"), self.low_proj.at[l],
                self.up_proj.at[l], vec.row("gain2"), vec.row("shift2"), self.low_up.at[l],
                self.mid, self.normed, self.red, self.reds.at[l, 1], self.red_up, self.reds.at[l, 2],
            )
            self.save("mid", l=l)
        elif name == "up":
            if part == 0:
                self.staged("up", l)
                self.settled("hidden", l=l - 1)
            w = self.wu.reshape(NARROW, self.x.shape[1], -1)
            size = NARROW // 2
            each(size, lambda n: up_strip(
                part * size + n, self.normed, w, Strips(vec.up), self.red_up, self.up_up.at[l],
                self.hidden, self.active,
            ))
            if part == 1:
                self.save("hidden", l=l)
        elif name == "down":
            self.staged("down", l)
            self.settled("x", l=l - 1)
            dim = self.x.shape[1]

            def put(n, value):
                if l < self.layers - 1:
                    self.x[:, columns(n, 256)] = value
                else:
                    for m in range(2):
                        self.result[2 * n + m] = value[:, m * 128 : (m + 1) * 128].astype(BF16)

            down_stage(
                self.mid, self.active, self.wd.reshape(-1, dim), vec.row("down"), self.low_down.at[l],
                self.up_down.at[l], self.red, self.reds.at[l, 3], put,
            )
            if l < self.layers - 1:
                self.save("x", l=l)

    def close(self):
        last = self.layers - 1
        self.settled(*[name for name in SAVED if name not in ("x", "peer")], l=last)
        for l in range(self.layers):
            self.settled("peer", l=l)
        for s in range(1, self.group):
            self.exchange(last, s).wait_send()
        if last > 0:
            pass


def gather_body(n_row, n_col, layers, group, names, *refs):
    refs = dict(zip(names, refs))
    shard = {kind: refs["shard_" + kind] for kind in KINDS}
    full = {kind: refs["full_" + kind] for kind in KINDS}
    tokens, cotangent, vector = refs["tokens"], refs["cotangent"], refs["vector"]
    own_tokens, own_cotangent, vectors = refs["own_tokens"], refs["own_cotangent"], refs["vectors"]
    local_sem, send_sem, recv_sem = refs["local_sem"], refs["send_sem"], refs["recv_sem"]
    near_sem, out_sem, in_sem = refs["near_sem"], refs["out_sem"], refs["in_sem"]
    r = lax.axis_index("row")
    c = lax.axis_index("col")
    link_bits = [b for b in (2**k for k in range(1, 8)) if b < n_col]
    depth = shard["up"].shape[1]

    def row_peer(s):
        return (lax.rem(r + s, n_row), c)

    def col_peer(bit):
        return (r, c ^ bit)

    peers = [row_peer(s) for s in range(1, n_row)]
    peers += [(r, lax.rem(c + d, n_col)) for d in range(1, n_col)]
    barrier = pltpu.get_barrier_semaphore()
    for peer in peers:
        pl.semaphore_signal(barrier, inc=1, device_id=peer, device_id_type=MESH)
    pl.semaphore_wait(barrier, len(peers))

    per, width = BLOCKS // group, tokens.shape[1]

    def own_place(ref, b, col):
        if len(ref.shape) == 2:
            start = pl.multiple_of(col * width, width)
            return ref.at[pl.ds(b * BLOCK, BLOCK), pl.ds(start, width)]
        return ref.at[col, pl.ds(b * BLOCK, BLOCK)]

    def from_place(ref, b, col):
        start = (col // group) * LEN + place_of(group, lax.rem(col, group), b) * BLOCK
        return ref.at[pl.ds(pl.multiple_of(start, BLOCK), BLOCK)]

    exchanged = ((tokens, own_tokens), (cotangent, own_cotangent))

    def near(n, b):
        src, dst = exchanged[n]
        return pltpu.make_async_copy(from_place(src, b, c), own_place(dst, b, c), near_sem.at[n * per + b])

    def near_vector():
        return pltpu.make_async_copy(vector, vectors.at[c], near_sem.at[2 * per])

    def far(src, dst, n, peer):
        return pltpu.make_async_remote_copy(
            src_ref=src, dst_ref=dst, send_sem=out_sem.at[n], recv_sem=in_sem.at[n],
            device_id=peer, device_id_type=MESH,
        )

    def start_exchange(n):
        src, dst = exchanged[n]
        for b in range(per):
            near(n, b).start()
        for d in range(1, n_col):
            to = lax.rem(c + d, n_col)
            for b in range(per):
                far(from_place(src, b, to), own_place(dst, b, c), n, (r, to)).start()

    def wait_exchange(n):
        _, dst = exchanged[n]
        for b in range(per):
            near(n, b).wait()
        if len(dst.shape) == 2:
            ref = dst.at[:, pl.ds(0, (n_col - 1) * width)]
        else:
            ref = dst.at[pl.ds(0, n_col - 1)]
        far(ref, ref, n, col_peer(1)).wait()

    def own(kind, l, h):
        ref = shard[kind]
        size = ref.shape[1] // (2 * len(ORDERS[kind]))
        return ref.at[l, pl.ds(h * size, size)]

    def block(kind, l, h, row, col):
        if kind in ("qkv", "up"):
            return full[kind].at[l, col, row, h]
        start = pl.multiple_of(row * depth, depth)
        return full[kind].at[l, col, h, :, pl.ds(start, depth)]

    def strip(kind, l, h, col):
        if kind in ("qkv", "up"):
            return full[kind].at[l, col, :, h]
        return full[kind].at[l, col, h]

    def amount(kind, l, h, strips, rows):
        if kind in ("qkv", "up"):
            return full[kind].at[l, pl.ds(0, strips), pl.ds(0, rows), h]
        return full[kind].at[l, pl.ds(0, strips), h, :, pl.ds(0, rows * depth)]

    chunks = []
    for l in range(layers):
        for kind in KINDS:
            for h in range(2 * len(ORDERS[kind])):
                order = []
                for d in ORDERS[kind][h // 2][h % 2]:
                    if d == "z":
                        order.append("z")
                    elif d < len(link_bits):
                        order.append(link_bits[d])
                order += link_bits[2:]
                chunks.append((kind, l, h, tuple(order)))
    phases = len(link_bits) + 1

    def remote(src, dst, k, p, peer):
        return pltpu.make_async_remote_copy(
            src_ref=src, dst_ref=dst, send_sem=send_sem.at[k, p], recv_sem=recv_sem.at[k, p],
            device_id=peer, device_id_type=MESH,
        )

    def local(k):
        kind, l, h, _ = chunks[k]
        return pltpu.make_async_copy(own(kind, l, h), block(kind, l, h, r, c), local_sem.at[k])

    def issue(k, p):
        kind, l, h, order = chunks[k]
        d, masks, whole = transfer_plan(order)[p]
        for m in masks:
            if d == "z":
                src = own(kind, l, h) if m == 0 else block(kind, l, h, r, c ^ m)
                for s in range(1, n_row):
                    remote(src, block(kind, l, h, r, c ^ m), k, p, row_peer(s)).start()
            elif whole:
                ref = strip(kind, l, h, c ^ m)
                remote(ref, ref, k, p, col_peer(d)).start()
            else:
                src = own(kind, l, h) if m == 0 else block(kind, l, h, r, c ^ m)
                remote(src, block(kind, l, h, r, c ^ m), k, p, col_peer(d)).start()

    def moved(k, p):
        kind, l, h, order = chunks[k]
        d, masks, whole = transfer_plan(order)[p]
        if d == "z":
            rows = n_row - 1
        else:
            rows = n_row if whole else 1
        ref = amount(kind, l, h, len(masks), rows)
        return remote(ref, ref, k, p, col_peer(1))

    def share(k, p):
        kind, l, h, order = chunks[k]
        steps = transfer_plan(order)
        (d, masks, _), (_, later, whole) = steps[p], steps[p + 1]
        if not whole:
            return
        fresh = masks if d == "z" else later[len(masks):]
        for m in fresh:
            ref = strip(kind, l, h, c ^ m)
            remote(ref, ref, k, phases, col_peer(1)).start()

    def shared(k):
        kind, l, h, _ = chunks[k]
        ref = amount(kind, l, h, n_col // 2, n_row)
        return remote(ref, ref, k, phases, col_peer(1))

    def finish(k, p):
        moved(k, p).wait_recv()
        if chunks[k][3][p] == "z":
            local(k).wait()
        share(k, p)

    count = len(chunks)
    near_vector().start()
    for d in range(1, n_col):
        far(vector, vectors.at[c], 2, (r, lax.rem(c + d, n_col))).start()
    start_exchange(0)
    for k in range(count):
        local(k).start()
    def vectors_arrive():
        near_vector().wait()
        rest = vectors.at[pl.ds(0, n_col - 1)]
        far(rest, rest, 2, col_peer(1)).wait()

    work = None
    if "x" in refs:
        refs.update(full=full, saved={name: refs["saved_" + name] for name in SAVED})

        def arrive_tokens():
            vectors_arrive()
            wait_exchange(0)
            load_sem = refs["load_sem"]
            loads = [(own_tokens, refs["tokens_v"]), (vectors, refs["vec"])]
            copies = [pltpu.make_async_copy(s, d, load_sem.at[n]) for n, (s, d) in enumerate(loads)]
            for copy in copies:
                copy.start()
            for copy in copies:
                copy.wait()

        refs.update(arrive_tokens=arrive_tokens)
        work = ForwardWork(n_col, group, refs)

    pieces = []
    for kind, l, h, order in chunks:
        size = 2 * shard[kind].shape[1] * shard[kind].shape[2] // (2 * len(ORDERS[kind]))
        pieces.append(((kind, l), order, size))
    for op, k, p in transfer_schedule(pieces, n_row, task_list(layers) if work else []):
        if op == "start":
            issue(k, p)
        elif op == "wait":
            finish(k, p)
        elif op == "stage":
            for n, (kind, l, _, _) in enumerate(chunks):
                if (kind, l) == (k, p):
                    shared(n).wait_recv()
            work.stage(k, p)
        else:
            work.run(k, *p)
    start_exchange(1)
    for k in range(count):
        for p in range(phases):
            moved(k, p).wait_send()
        shared(k).wait_send()
        if not work:
            shared(k).wait_recv()
    if work:
        work.close()
    else:
        vectors_arrive()
        wait_exchange(0)
    wait_exchange(1)


def gather_inputs(n_row, n_col, group, qkv, proj, up, down, tokens, cotangent, vector, tables=None):
    layers, depth = up.shape[0], up.shape[1]
    width, units = proj.shape[1], down.shape[1]
    dim, hidden = depth * n_row, units * n_col
    mine = LEN // group
    cuts = [2 * len(ORDERS[kind]) for kind in KINDS]
    own = (mine, dim) if width % 128 == 0 else (n_col, mine, width)
    hbm = pl.BlockSpec(memory_space=pltpu.HBM)
    vmem = pl.BlockSpec(memory_space=pltpu.VMEM)
    dma = pltpu.SemaphoreType.DMA
    count = layers * sum(cuts)
    phases = n_col.bit_length()
    inputs = [("shard_" + kind, array, hbm) for kind, array in zip(KINDS, (qkv, proj, up, down))]
    inputs += [("tokens", tokens, hbm), ("cotangent", cotangent, hbm), ("vector", vector, hbm)]
    outputs = [
        ("full_qkv", (layers, n_col, n_row, cuts[0], depth // cuts[0], qkv.shape[2]), BF16, hbm),
        ("full_proj", (layers, n_col, cuts[1], width // cuts[1], dim), BF16, hbm),
        ("full_up", (layers, n_col, n_row, cuts[2], depth // cuts[2], units), BF16, hbm),
        ("full_down", (layers, n_col, cuts[3], units // cuts[3], dim), BF16, hbm),
        ("own_tokens", own, BF16, hbm),
        ("own_cotangent", own, BF16, hbm),
        ("vectors", (n_col,) + vector.shape, F32, hbm),
    ]
    scratch = [
        ("local_sem", dma((count,))),
        ("send_sem", dma((count, phases))),
        ("recv_sem", dma((count, phases))),
        ("near_sem", dma((2 * (BLOCKS // group) + 1,))),
        ("out_sem", dma((3,))),
        ("in_sem", dma((3,))),
    ]
    if tables is not None:
        rank = tables[0].shape[1]
        inputs += [(name, table, vmem) for name, table in zip(TABLES, tables)]
        strip = (NARROW, mine)
        kept = {
            "q": (strip + (128,), BF16), "kv": (strip + (256,), BF16), "att": ((mine, dim), BF16),
            "lse": ((NARROW, 8, mine), F32), "mid": ((mine, dim), F32), "hidden": ((mine, hidden), BF16),
            "x": ((mine, dim), F32), "peer": ((group - 1,) + strip + (256,), BF16),
        }
        outputs += [("saved_" + name, (layers,) + kept[name][0], kept[name][1], hbm) for name in SAVED]
        outputs += [
            ("reds", (layers, 4, rank, mine), BF16, vmem),
            ("result", (NARROW, mine, 128), BF16, vmem),
        ]
        scratch += [
            (name, pltpu.VMEM(((layers,) if name == "peer" else ()) + kept[name][0], kept[name][1]))
            for name in SAVED
        ]
        scratch += [
            ("wq", pltpu.VMEM((NARROW // 2, n_row, cuts[0], depth // cuts[0], 768), BF16)),
            ("wp", pltpu.VMEM((NARROW, cuts[1], width // cuts[1], dim), BF16)),
            ("wu", pltpu.VMEM((NARROW, n_row, cuts[2], depth // cuts[2], units), BF16)),
            ("wd", pltpu.VMEM((NARROW, cuts[3], units // cuts[3], dim), BF16)),
            ("tokens_v", pltpu.VMEM((mine, dim), BF16)),
            ("normed", pltpu.VMEM((mine, dim), BF16)),
            ("active", pltpu.VMEM((mine, hidden), BF16)),
            ("red", pltpu.VMEM((mine, rank), BF16)),
            ("red_up", pltpu.VMEM((mine, rank), BF16)),
            ("vec", pltpu.VMEM((n_col,) + vector.shape, F32)),
            ("stage_sem", dma((4,))),
            ("save_sem", dma((layers, len(SAVED)))),
            ("kv_send", dma((layers, group - 1))),
            ("kv_recv", dma((layers, group - 1))),
            ("load_sem", dma((2,))),
        ]
    names = [x[0] for x in inputs] + [x[0] for x in outputs] + [x[0] for x in scratch]
    outs = pl.pallas_call(
        functools.partial(gather_body, n_row, n_col, layers, group, tuple(names)),
        out_shape=[jax.ShapeDtypeStruct(shape, kind) for _, shape, kind, _ in outputs],
        in_specs=[spec for _, _, spec in inputs],
        out_specs=[spec for _, _, _, spec in outputs],
        scratch_shapes=[shape for _, shape in scratch],
        compiler_params=pltpu.CompilerParams(
            collective_id=0, has_side_effects=True, vmem_limit_bytes=60 * 2**20
        ),
        name="gather_inputs",
    )(*[array for _, array, _ in inputs])
    outs = dict(zip([x[0] for x in outputs], outs))

    merge = 128 // width
    strips = n_col // merge
    qkv_full = outs["full_qkv"].reshape(layers, n_col, dim, qkv.shape[2])
    up_full = outs["full_up"].reshape(layers, n_col, dim, units)
    rows, vec = [outs["own_tokens"], outs["own_cotangent"]], outs["vectors"]
    if merge > 1:
        qkv_full = qkv_full.reshape(layers, strips, merge, dim, 3, width).transpose(0, 1, 3, 4, 2, 5)
        up_full = up_full.reshape(layers, strips, merge, dim, units).transpose(0, 1, 3, 2, 4)
        rows = [x.transpose(1, 0, 2).reshape(mine, dim) for x in rows]
        vec = vec.reshape(strips, merge, layers, 4, 4 * 128)
        first = vec[:, :, :, 0, : 3 * width].reshape(strips, merge, layers, 3, width).transpose(0, 2, 3, 1, 4)
        first = jnp.pad(first.reshape(strips, layers, 384), ((0, 0), (0, 0), (0, 128)))
        second = vec[:, :, :, 1, :units].transpose(0, 2, 1, 3).reshape(strips, layers, 512)
        rest = vec[:, :, :, 2:, : 4 * width].reshape(strips, merge, layers, 2, 4, width)
        rest = rest.transpose(0, 2, 3, 4, 1, 5).reshape(strips, layers, 2, 512)
        vec = jnp.concatenate([first[:, :, None], second[:, :, None], rest], axis=2)
        vec = vec.reshape(strips, layers * 4, 512)
    outs.update(
        qkv=qkv_full.reshape(layers, strips, dim, 384),
        proj=outs["full_proj"].reshape(layers, dim, dim),
        up=up_full.reshape(layers, strips, dim, units * merge),
        down=outs["full_down"].reshape(layers, hidden, dim),
        tokens=rows[0], cotangent=rows[1], vec=vec,
    )
    return outs


PARAMS = pltpu.CompilerParams(vmem_limit_bytes=60 * 2**20)


def shape_of(shape, kind):
    return jax.ShapeDtypeStruct(shape, kind)


def kernel(body, name, inputs, outputs, scratch=()):
    spaces = (pl.BlockSpec(memory_space=pltpu.VMEM), pl.BlockSpec(memory_space=pltpu.HBM))
    return pl.pallas_call(
        body,
        out_shape=[shape_of(shape, kind) for shape, kind, _ in outputs],
        in_specs=[spaces[far] for _, far in inputs],
        out_specs=[spaces[far] for _, _, far in outputs],
        scratch_shapes=list(scratch),
        compiler_params=PARAMS,
        name=name,
    )(*[array for array, _ in inputs])


def own_group(group):
    return lax.rem(lax.axis_index("col"), group)


def qkv_body(l, x, vec, w, low, up, q, kv, red_out, red, normed, buf, sem):
    copies = []
    for i in range(NARROW):
        copies.append(pltpu.make_async_copy(w.at[l, i], buf.at[i // 2, :, columns(i % 2, 384)], sem.at[i]))
        copies[-1].start()
    for copy in copies:
        copy.wait()
    v = Vectors(vec, l)
    qkv_stage(x, v.row("gain1"), v.row("shift1"), buf, Strips(v.qkv), low.at[l], up.at[l], q, kv, red, red_out, normed)


def qkv_kernel(l, x, vec, w, low, up):
    tokens, dim = x.shape
    return kernel(
        functools.partial(qkv_body, l), "qkv",
        [(x, False), (vec, False), (w, True), (low, False), (up, False)],
        [((NARROW, tokens, 128), BF16, False), ((NARROW, tokens, 256), BF16, False), ((low.shape[1], tokens), BF16, False)],
        [pltpu.VMEM((tokens, low.shape[1]), BF16), pltpu.VMEM((tokens, dim), BF16), pltpu.VMEM((NARROW // 2, dim, 768), BF16), pltpu.SemaphoreType.DMA((NARROW,))],
    )


def attend_body(group, g_ref, q, *refs):
    held = positions(group)
    kvs, (out, lse) = refs[:group], refs[group:]
    bias = pair_bias(held, g_ref[0])
    each(NARROW, lambda i: attend_strip(held, bias, i, q, kvs, out, lse))


def attend_kernel(group, g, q, kvs):
    tokens = q.shape[1]
    return pl.pallas_call(
        functools.partial(attend_body, group),
        out_shape=[shape_of((tokens, NARROW * 128), BF16), shape_of((NARROW, 8, tokens), F32)],
        in_specs=[pl.BlockSpec(memory_space=pltpu.SMEM)] + [pl.BlockSpec(memory_space=pltpu.VMEM)] * (group + 1),
        out_specs=[pl.BlockSpec(memory_space=pltpu.VMEM)] * 2,
        compiler_params=PARAMS,
        name="attend",
    )(g, q, *kvs)


def mlp_body(l, x, att, vec, wp, wu, wd, *refs):
    low_proj, up_proj, low_up, up_up, low_down, up_down = [ref.at[l] for ref in refs[:6]]
    mid, result, hidden, reds, red, red_up, normed, active, bp, bu, bd, sem = refs[6:]
    copies = []
    for n, (src, dst) in enumerate(((wp.at[l], bp), (wu.at[l], bu), (wd.at[l], bd))):
        copies.append(pltpu.make_async_copy(src, dst, sem.at[n]))
        copies[-1].start()
    v = Vectors(vec, l)
    copies[0].wait()
    proj_stage(
        x, att, bp, v.row("proj"), low_proj, up_proj, v.row("gain2"), v.row("shift2"), low_up,
        mid, normed, red, reds.at[0], red_up, reds.at[1],
    )
    copies[1].wait()
    each(NARROW, lambda i: up_strip(i, normed, bu, Strips(v.up), red_up, up_up, hidden, active))
    copies[2].wait()

    def put(n, value):
        if len(result.shape) == 2:
            result[:, columns(n, 256)] = value
        else:
            for m in range(2):
                result[2 * n + m] = value[:, m * 128 : (m + 1) * 128].astype(BF16)

    down_stage(mid, active, bd, v.row("down"), low_down, up_down, red, reds.at[2], put)


def mlp_kernel(l, final, x, att, vec, wp, wu, wd, tables):
    tokens, dim = x.shape
    hidden = wd.shape[1]
    rank = tables[0].shape[1]
    result = ((NARROW, tokens, 128), BF16, False) if final else ((tokens, dim), F32, False)
    return kernel(
        functools.partial(mlp_body, l), "mlp",
        [(x, False), (att, False), (vec, False), (wp, True), (wu, True), (wd, True)] + [(t, False) for t in tables],
        [((tokens, dim), F32, False), result, ((tokens, hidden), BF16, False), ((3, rank, tokens), BF16, False)],
        [
            pltpu.VMEM((tokens, rank), BF16), pltpu.VMEM((tokens, rank), BF16),
            pltpu.VMEM((tokens, dim), BF16), pltpu.VMEM((tokens, hidden), BF16), pltpu.VMEM(wp.shape[1:], BF16),
            pltpu.VMEM(wu.shape[1:], BF16), pltpu.VMEM(wd.shape[1:], BF16), pltpu.SemaphoreType.DMA((3,)),
        ],
    )


def mlp_back_stage(vec, grad, hidden, g_hid, mid, att, low, total, wp, wu, wd, reds, t, grads, g_mid, waits):
    low[...] = grad[...].astype(BF16)
    g_red = dot(low[...], t["up_down"], TURNED).astype(BF16)
    rank = g_red.shape[1]
    waits("hidden")
    waits("down")
    waits("up")
    units = wu.shape[2]
    total[...] = jnp.zeros_like(total)

    def strip(i):
        cols = columns(i, units)
        active, slope = gelu_parts(hidden[:, cols].astype(F32))
        hidden[:, cols] = active.astype(BF16)
        g_active = dot(low[...], wd[cols, :], TURNED) + dot(g_red, t["low_down"][:, cols])
        g_hid[:, cols] = (g_active * slope).astype(BF16)
        total[...] += dot(g_hid[:, cols], wu[i], TURNED)

    each(NARROW, strip)

    def give(at, value):
        size = value.shape[1] // NARROW
        for i in range(NARROW):
            grads[i, :, at : at + size] = value[:, i * size : (i + 1) * size].astype(BF16)

    give(384 + 2 * units, dot(reds[3], low[...]))
    give(384 + units, dot(g_red, hidden[...], CROSS))
    give(384, dot(reds[2], g_hid[...]))
    g_hid[:, :rank] = dot(g_hid[...], t["up_up"][...], TURNED).astype(BF16)
    waits("mid")
    gain, shift = vec.row("gain2"), vec.row("shift2")
    dim = mid.shape[1]

    def norm(rows):
        scaled, inverse = norm_parts(mid[rows, :])
        hidden[rows, :dim] = (scaled * gain + shift).astype(BF16)
        g_normed = total[rows, :] + dot(g_hid[rows, :rank], t["low_up"])
        value = grad[rows, :] + norm_grad(g_normed, scaled, inverse, gain)
        g_mid[rows, :] = value
        low[rows, :] = value.astype(BF16)

    by_rows(mid.shape[0], norm)
    give(256, dot(g_hid[:, :rank], hidden[:, :dim], CROSS))
    give(128, dot(reds[1], low[...]))
    g_red_proj = dot(low[...], t["up_proj"], TURNED).astype(BF16)
    waits("att")
    waits("proj")
    give(0, dot(g_red_proj, att[...], CROSS))
    low[...] = (dot(low[...], wp[...], TURNED) + dot(g_red_proj, t["low_proj"])).astype(BF16)


def qkv_back_stage(vec, x, g_mid, gq, parts, total, g_red, normed, wq, red, low, up, grads, put, waits):
    total[...] = jnp.zeros_like(total)
    waits("gq")
    waits("qkv")

    def pair(j, small):
        pieces = []
        for i in (2 * j, 2 * j + 1):
            g_kv = sum(part[i].astype(F32) for part in parts).astype(BF16)
            g_mixed = jnp.concatenate([gq[i], g_kv], axis=1)
            grads[i, :, 128:512] = dot(red[...], g_mixed).astype(BF16)
            small = small + dot(g_mixed, up[i], TURNED)
            pieces.append(g_mixed)
        total[...] += dot(jnp.concatenate(pieces, axis=1), wq[j], TURNED)
        return small

    rank, tokens = red.shape
    small = lax.fori_loop(0, NARROW // 2, pair, jnp.zeros((tokens, rank), F32))
    g_low_rank = small.astype(BF16)
    g_red[...] = g_low_rank
    waits("x")
    waits("g_mid")
    gain, shift = vec.row("gain1"), vec.row("shift1")

    def norm(rows):
        scaled, inverse = norm_parts(x[rows, :].astype(F32))
        normed[rows, :] = (scaled * gain + shift).astype(BF16)
        g_normed = total[rows, :] + dot(g_red[rows, :], low[...])
        put(rows, g_mid[rows, :] + norm_grad(g_normed, scaled, inverse, gain))

    by_rows(tokens, norm)
    g_low = dot(g_low_rank, normed[...], CROSS).astype(BF16)
    for i in range(NARROW):
        grads[i, :, :128] = g_low[:, i * 128 : (i + 1) * 128]


def back_body(lq, lm, group, names, *refs):
    R = dict(zip(names, refs))
    held = positions(group)
    sem, started = R["sem"], {}

    def waits(name):
        for copy in started.pop(name, ()):
            copy.wait()

    count = [0]

    def begin(name, *copies):
        started[name] = []
        for src, dst in copies:
            copy = pltpu.make_async_copy(src, dst, sem.at[count[0]])
            count[0] += 1
            copy.start()
            started[name].append(copy)

    if lq is not None:
        begin("gq", (R["in_gq"], R["gq"]), *[(R["in_part%d" % j], R["part%d" % j]) for j in range(group)])
        begin("qkv", *[
            (R["w_qkv"].at[lq, i], R["wq"].at[i // 2, :, columns(i % 2, 384)]) for i in range(NARROW)
        ])
        begin("x", (R["in_x"], R["x"]))
        begin("g_mid", (R["in_g_mid"], R["total2"]))
    else:
        begin("cotangent", (R["cotangent"], R["low"]))
    if lm is not None:
        begin("hidden", (R["hiddens"].at[lm], R["hidden"]))
        begin("down", *[
            (R["w_down"].at[lm, pl.ds(n * 1024, 1024)], R["wd"].at[pl.ds(n * 1024, 1024)])
            for n in range(R["wd"].shape[0] // 1024)
        ])
        begin("up", *[(R["w_up"].at[lm, i], R["wu"].at[i]) for i in range(NARROW)])
        begin("proj", (R["w_proj"].at[lm], R["wp"]))
        begin("att", (R["atts"].at[lm], R["att"]))
        begin("kv", (R["kvs"].at[lm], R["kv"]), (R["peers"].at[lm], R["peer"]), (R["lses"].at[lm], R["lse"]))
    if lq is not None:
        vec = Vectors(R["vec"], lq)

        def put(rows, value):
            if lm is None:
                for i in range(NARROW):
                    R["out"][i, rows, :] = value[:, i * 128 : (i + 1) * 128].astype(BF16)
            else:
                R["grad"][rows, :] = value

        qkv_back_stage(
            vec, R["x"], R["total2"], R["gq"], [R["part%d" % j] for j in range(group)], R["total"],
            R["g_red"], R["low"], R["wq"],
            R["reds"].at[lq, 0], R["low_qkv"].at[lq], R["up_qkv"].at[lq], R["grads_qkv"], put, waits,
        )
    else:
        waits("cotangent")
        R["grad"][...] = R["low"][...].astype(F32)
    if lm is None:
        return
    begin("q", (R["qs"].at[lm], R["gq"]))
    begin("mid", (R["mids"].at[lm], R["x" if lq is not None and R["x"].dtype == F32 else "mid"]))
    mid = R["x" if lq is not None and R["x"].dtype == F32 else "mid"]
    t = {name: R[name].at[lm] for name in TABLES}
    vec = Vectors(R["vec"], lm)
    mlp_back_stage(
        vec, R["grad"], R["hidden"], R["g_hid"], mid, R["att"], R["low"], R["total"], R["wp"], R["wu"], R["wd"],
        R["reds"].at[lm], {k: (v if k in ("low_down", "up_up") else v[...]) for k, v in t.items() if "qkv" not in k},
        R["grads_mlp"], R["total2"], waits,
    )
    out_mid = pltpu.make_async_copy(R["total2"], R["out_g_mid"], sem.at[count[0]])
    out_mid.start()
    waits("q")
    waits("kv")
    bias = pair_bias(held, R["g"][0])
    kvs = [R["kv"]] + [R["peer"].at[j] for j in range(group - 1)]
    gkvs = [R["part%d" % j] for j in range(group)]
    each(NARROW, lambda i: attend_back_strip(
        held, bias, i, R["gq"], R["lse"], R["att"], R["low"], kvs, R["gq"], gkvs
    ))
    outs = [(R["gq"], R["out_gq"])] + [(R["part%d" % j], R["out_part%d" % j]) for j in range(group)]
    copies = [pltpu.make_async_copy(src, dst, sem.at[count[0] + 1 + n]) for n, (src, dst) in enumerate(outs)]
    for copy in copies:
        copy.start()
    for copy in copies:
        copy.wait()
    out_mid.wait()


def back_kernel(lq, lm, group, g, outs, tables, carried):
    layers, _, dim, _ = outs["qkv"].shape
    hidden = outs["down"].shape[1]
    tokens = outs["tokens"].shape[0]
    rank = tables[0].shape[1]
    strip = (NARROW, tokens)
    inputs = [("g", g, pl.BlockSpec(memory_space=pltpu.SMEM))]
    near, far = pl.BlockSpec(memory_space=pltpu.VMEM), pl.BlockSpec(memory_space=pltpu.HBM)
    inputs += [(name, table, near) for name, table in zip(TABLES, tables)]
    inputs += [("vec", outs["vec"], near), ("reds", outs["reds"], near)]
    outputs, scratch = [], []

    def vmem(name, shape, kind):
        scratch.append((name, pltpu.VMEM(shape, kind)))

    vmem("gq", strip + (128,), BF16)
    for j in range(group):
        vmem("part%d" % j, strip + (256,), BF16)
    vmem("total", (tokens, dim), F32)
    vmem("total2", (tokens, dim), F32)
    vmem("low", (tokens, dim), BF16)
    if lq is not None:
        g_mid, gq, parts = carried
        x = outs["tokens"] if lq == 0 else outs["saved_x"][lq - 1]
        inputs += [("in_gq", gq, far), ("in_g_mid", g_mid, far), ("in_x", x, far), ("w_qkv", outs["qkv"], far)]
        inputs += [("in_part%d" % j, part, far) for j, part in enumerate(parts)]
        vmem("wq", (NARROW // 2, dim, 768), BF16)
        vmem("g_red", (tokens, rank), BF16)
        vmem("x", (tokens, dim), x.dtype)
        outputs.append(("grads_qkv", (NARROW, rank, 512), BF16, near))
        if lm is None:
            outputs.append(("out", strip + (128,), BF16, near))
    if lm is not None:
        if lq is None:
            inputs.append(("cotangent", outs["cotangent"], far))
        for name in ("hidden", "mid", "att", "q", "kv", "peer", "lse"):
            inputs.append((name + "s", outs["saved_" + name], far))
        inputs += [("w_" + name, outs[name], far) for name in ("proj", "up", "down")]
        vmem("wp", (dim, dim), BF16)
        vmem("wu", (NARROW, dim, hidden // NARROW), BF16)
        vmem("wd", (hidden, dim), BF16)
        vmem("grad", (tokens, dim), F32)
        if lq is None or x.dtype != F32:
            vmem("mid", (tokens, dim), F32)
        vmem("att", (tokens, dim), BF16)
        vmem("hidden", (tokens, hidden), BF16)
        vmem("g_hid", (tokens, hidden), BF16)
        vmem("kv", strip + (256,), BF16)
        vmem("peer", (group - 1,) + strip + (256,), BF16)
        vmem("lse", (NARROW, 8, tokens), F32)
        outputs.append(("grads_mlp", (NARROW, rank, 512 + 2 * hidden // NARROW), BF16, near))
        outputs += [("out_g_mid", (tokens, dim), F32, far), ("out_gq", strip + (128,), BF16, far)]
        outputs += [("out_part%d" % j, strip + (256,), BF16, far) for j in range(group)]
    scratch.append(("sem", pltpu.SemaphoreType.DMA((64,))))
    names = [x[0] for x in inputs] + [x[0] for x in outputs] + [x[0] for x in scratch]
    made = pl.pallas_call(
        functools.partial(back_body, lq, lm, group, tuple(names)),
        out_shape=[shape_of(shape, kind) for _, shape, kind, _ in outputs],
        in_specs=[spec for _, _, spec in inputs],
        out_specs=[spec for _, _, _, spec in outputs],
        scratch_shapes=[shape for _, shape in scratch],
        compiler_params=PARAMS,
        name="back",
    )(*[array for _, array, _ in inputs])
    return dict(zip([x[0] for x in outputs], made))


def to_rows_body(held, x, out):
    n = 0
    for s in range(x.shape[0] // (len(held) * len(held[0]))):
        for g in range(len(held)):
            for place in held[g]:
                start = (s * BLOCKS + place) * BLOCK
                out[start : start + BLOCK, :] = x[n].astype(F32)
                n += 1


def to_rows(held, x):
    blocks, _, width = x.shape
    return pl.pallas_call(
        functools.partial(to_rows_body, held),
        out_shape=shape_of((blocks * BLOCK, width), F32),
        compiler_params=PARAMS,
        name="to_rows",
    )(x)


def pick_body(count, ids, *refs):
    for ref, out in zip(refs[:count], refs[count:]):
        out[...] = ref[...]


def pick_tables(ids, tables):
    def chosen(site, shape):
        return pl.BlockSpec((shape[0], None) + shape[2:], lambda i, ids: (0, ids[site], 0, 0))

    return pl.pallas_call(
        functools.partial(pick_body, len(tables)),
        grid_spec=pltpu.PrefetchScalarGridSpec(
            num_scalar_prefetch=1,
            grid=(1,),
            in_specs=[chosen(site, table.shape) for site, table in tables],
            out_specs=[
                pl.BlockSpec(table.shape[:1] + table.shape[2:], lambda i, ids: (0, 0, 0)) for _, table in tables
            ],
        ),
        out_shape=[shape_of(table.shape[:1] + table.shape[2:], BF16) for _, table in tables],
        compiler_params=PARAMS,
        name="pick",
    )(ids, *[table for _, table in tables])


def shards(mesh_shape, *args):
    (
        tokens, cotangent, adapter_ids, qkv_weight, qkv_bias, proj_weight, proj_bias,
        up_weight, up_bias, down_weight, down_bias, first_gain, first_shift, second_gain,
        second_shift, qkv_lower, qkv_raise, proj_lower, proj_raise, up_lower, up_raise,
        down_lower, down_raise,
    ) = args
    n_row, n_col = mesh_shape
    layers, adapters, dim, rank = qkv_lower.shape
    rows, width = tokens.shape
    units = up_weight.shape[2]
    seqs = rows // LEN
    group = n_col // seqs
    held = positions(group)
    per = BLOCKS // group
    mine = per * BLOCK
    merge = 128 // width
    c = lax.axis_index("col")
    g = lax.rem(c, group)
    ids = lax.dynamic_index_in_dim(adapter_ids, c // group, 0, keepdims=False)

    def line(pieces):
        row = jnp.concatenate([piece.reshape(layers, -1).astype(F32) for piece in pieces], axis=1)
        return jnp.pad(row, ((0, 0), (0, 512 - row.shape[1])))

    vector = jnp.stack(
        [
            line([qkv_bias]), line([up_bias]), line([proj_bias, down_bias, first_gain, first_shift]),
            line([second_gain, second_shift]),
        ],
        axis=1,
    ).reshape(layers * 4, 512)

    def turned(table):
        return jnp.swapaxes(table, 2, 3)

    tables = pick_tables(ids, [
        (0, turned(qkv_lower)), (1, turned(proj_lower)), (1, proj_raise), (2, turned(up_lower)), (2, up_raise),
        (3, turned(down_lower)), (3, down_raise),
    ])
    raise_qkv = lax.dynamic_index_in_dim(qkv_raise, ids[0], 1, keepdims=False)
    raise_qkv = raise_qkv.reshape(layers, rank, 3, NARROW, 128).transpose(0, 3, 1, 2, 4)
    tables = [tables[0], raise_qkv.reshape(layers, NARROW, rank, 384)] + list(tables[1:])
    fused = FUSED and width == 128
    outs = gather_inputs(
        n_row, n_col, group, qkv_weight.reshape(layers, -1, 3 * width), proj_weight, up_weight,
        down_weight, tokens, cotangent, vector, tables if fused else None
    )
    g_one = g.reshape(1)

    def peer_values(x, step):
        pairs = [(q, q - q % group + (q + step) % group) for q in range(n_col)]
        return lax.ppermute(x, "col", pairs)

    def to_columns(x):
        if merge > 1:
            x = x.reshape(NARROW, mine, merge, width).transpose(0, 2, 1, 3).reshape(n_col, mine, width)
        x = lax.all_to_all(x, "col", split_axis=0, concat_axis=0, tiled=True)
        return to_rows(held, x.reshape(n_col * per, BLOCK, width))

    if not fused:
        x = outs["tokens"].astype(F32)
        kept = {name: [] for name in SAVED + ("reds",)}
        for l in range(layers):
            q, kv, red = qkv_kernel(l, x, outs["vec"], outs["qkv"], tables[0], tables[1])
            kvs = [kv] + [peer_values(kv, s) for s in range(1, group)]
            att, lse = attend_kernel(group, g_one, q, kvs)
            mid, x, hidden, reds = mlp_kernel(
                l, l == layers - 1, x, att, outs["vec"], outs["proj"], outs["up"], outs["down"], tables[2:]
            )
            reds = jnp.concatenate([red[None], reds])
            peer = jnp.stack(kvs[1:]) if group > 1 else kv[None][:0]
            for name, value in zip(SAVED + ("reds",), (q, kv, peer, att, lse, mid, hidden, x, reds)):
                kept[name].append(value)
        for name in SAVED:
            outs["saved_" + name] = jnp.stack(kept[name][: layers - 1] if name == "x" else kept[name])
        outs["reds"] = jnp.stack(kept["reds"])
        outs["result"] = x
    result = to_columns(outs["result"])

    onehot = (adapter_ids.T[:, :, None] == jnp.arange(adapters)[None, None, :]).astype(BF16)

    def all_rows(x):
        pairs = [[(q, (q + s) % n_row) for q in range(n_row)] for s in range(1, n_row)]
        return [x] + [lax.ppermute(x, "row", pair) for pair in pairs]

    onehots = jnp.concatenate(all_rows(onehot), axis=1)

    def collect(parts, named):
        if merge > 1:
            pieces, at = [], 0
            for _, size in named:
                piece = parts[:, :, at : at + size]
                at += size
                if size == 384:
                    piece = piece.reshape(NARROW, rank, 3, merge, width).transpose(0, 3, 1, 2, 4)
                else:
                    piece = piece.reshape(NARROW, rank, merge, size // merge).transpose(0, 2, 1, 3)
                pieces.append(piece.reshape(n_col, rank, size // merge))
            parts = jnp.concatenate(pieces, axis=2)
        parts = lax.all_to_all(parts, "col", split_axis=0, concat_axis=0, tiled=True)
        parts = parts.reshape((seqs, group) + parts.shape[1:]).astype(F32).sum(axis=1).astype(BF16)
        parts = jnp.concatenate(all_rows(parts), axis=0)
        sums, at = [], 0
        for site, size in named:
            piece = parts[:, :, at : at + size // merge]
            at += size // merge
            sums.append(jnp.einsum("sa,srn->arn", onehots[site], piece, preferred_element_type=F32))
        return sums

    wide = outs["down"].shape[1] // NARROW
    grads, carried = [None] * layers, None
    for l in reversed(range(layers + 1)):
        lq, lm = (l if l < layers else None), (l - 1 if l > 0 else None)
        made = back_kernel(lq, lm, group, g_one, outs, tables, carried)
        if lm is not None:
            grads[lm] = collect(made["grads_mlp"], [(1, 128), (1, 128), (2, 128), (2, wide), (3, wide), (3, 128)])
            parts = [made["out_part%d" % s] for s in range(group)]
            parts = [parts[0]] + [peer_values(parts[s], group - s) for s in range(1, group)]
            carried = (made["out_g_mid"], made["out_gq"], parts)
        if lq is not None:
            grads[lq] = collect(made["grads_qkv"], [(0, 128), (0, 384)]) + grads[lq]
    grad = made["out"]
    input_grad = to_columns(grad)

    final = []
    for number in range(8):
        p = jnp.stack([grads[l][number] for l in range(layers)])
        if number == 1:
            p = p.reshape(layers, adapters, rank, 3, width)
        elif number % 2 == 0:
            p = p.transpose(0, 1, 3, 2)
        final.append(p)
    return (result, input_grad) + tuple(final)


def solution(mesh):
    mesh_shape = (mesh.shape["row"], mesh.shape["col"])
    return jax.shard_map(
        functools.partial(shards, mesh_shape),
        mesh=mesh,
        in_specs=(
            P("row", "col"), P("row", "col"), P("row", None),
            P(None, "row", None, "col"), P(None, None, "col"),
            P(None, "col", "row"), P(None, "col"),
            P(None, "row", "col"), P(None, "col"),
            P(None, "col", "row"), P(None, "col"),
            P(None, "col"), P(None, "col"), P(None, "col"), P(None, "col"),
            P(), P(), P(), P(), P(), P(), P(), P(),
        ),
        out_specs=(
            P("row", "col"), P("row", "col"),
            P(None, None, "col", None), P(None, None, None, None, "col"),
            P(None, None, "col", None), P(None, None, None, "col"),
            P(None, None, "col", None), P(None, None, None, "col"),
            P(None, None, "col", None), P(None, None, None, "col"),
        ),
        check_vma=False,
    )
```

time: 1180 us -> 550 us (0.47)
  matrix products: 359 us -> 4.57 us
  local copies, waits for them, and re-layouts: 191 us -> 17 us
  other arithmetic: 127 us -> 1.36 us
  Pallas kernels: 306 us -> 417 us
  blocking collectives: 68.2 us -> 0 us
  starting transfers between devices: 23.5 us -> 58.2 us
  waiting for transfers between devices: 70.2 us -> 39.2 us
  between operations: 24.7 us -> 1.71 us
    dot_general x84 -> x16, matrix products: 359 us -> 4.57 us  [collect(): jnp.einsum('sa,srn->arn', onehots[site], piece, preferred_element_type=F32)]
    pallas_call x1 -> x7, Pallas kernels: 306 us -> 417 us  [the longest x1 275 us: gather_inputs(): pl.pallas_call(functools.partial(gather_body, n_row, n_col, layers, group...]
    all_gather x8 -> x0, blocking collectives: 68.2 us -> none  [the longest x7 59.4 us: vectors(): return lax.all_gather(v, 'col', axis=v.ndim - 1, tiled=True).astype(F32)]
    convert_element_type x10 -> x1, other arithmetic: 63.1 us -> 0.01 us  [shards(): (adapter_ids.T[:, :, None] == jnp.arange(adapters)[None, None, :]).astype...]
    unnamed x385 -> x42, local copies, waits for them, and re-layouts: 63.7 us -> 8.67 us
    psum x1 -> x0, waiting for transfers between devices: 53.9 us -> none  [shards(): summed = lax.psum([p.astype(BF16) for p in placed], 'row')]
    slice x26 -> x0, local copies, waits for them, and re-layouts: 46.8 us -> none  [the longest x1 11.7 us: shards(): up_full[l]]
    reshape x19 -> x2, local copies, waits for them, and re-layouts: 45.4 us -> 1.48 us  [the longest x1 0.87 us: shards(): raise_qkv.reshape(layers, NARROW, rank, 384)]
  transfers between devices with their start and end apart: 10 -> 23, of which waited for: 3 -> 12; matrix products, arithmetic and copies ran while one was open for 17% -> 3% of each run, Pallas kernels for 26% -> 12%
where the time goes in v3:
time: 550 us; the launch traced here: 539 us
  Pallas kernels  417 us (76%)
  starting transfers between devices  58.2 us (11%)
  waiting for transfers between devices  39.2 us (7%)
  local copies, waits for them, and re-layouts  17 us (3%)
    pallas_call x1, Pallas kernels, gather_inputs(): pl.pallas_call(functools.partial(gather_body, n_row, n_col, layers, group...  275 us
    pallas_call x3, Pallas kernels, back_kernel(): pl.pallas_call(functools.partial(back_body, lq, lm, group, tuple(names)),...  134 us
    ppermute x15, starting transfers between devices, all_rows(): return [x] + [lax.ppermute(x, 'row', pair) for pair in pairs]  33.4 us
    ppermute x15, waiting for transfers between devices, all_rows(): return [x] + [lax.ppermute(x, 'row', pair) for pair in pairs]  27.3 us
    all_to_all x4, starting transfers between devices, collect(): lax.all_to_all(parts, 'col', split_axis=0, concat_axis=0, tiled=True)  15.1 us
  transfers between devices with their start and end apart: 23, of which 12 were waited for; matrix products, arithmetic and copies ran while one was open for 3% of the time, Pallas kernels for 12%

profile of v3, /device:TPU:0, one launch (start us, length us, event | category | flops | bytes accessed | tf_op | source)
XLA Modules:
  0.0 539.2 jit_solution(16401295470001793449)
XLA Ops:
  0.8 0.8 constant_dynamic-slice_fusion.1
  1.6 1.2 fusion.103.ids
  3.1 0.9 reshape.93.refs_8_.refs_2_
  4.0 1.2 copy.126
  5.1 0.9 copy.133.refs_0_
  6.9 2.7 pick.1
  9.6 275.3 %gather_inputs.1 = (bf16[2,8,4,2,128,384]{5,4,3,2,1,0:T(8,128)(2,1)}, bf16[2,8,2,64,1024]{4,3,2,1,0:T(8,128)(2,1)}, bf16[2,8,4,4,64,512]{5,4,3,2,1,0:T(8,128)(2,...) custom-call(bf16[2,256,384]{2,1,0:T(8,128)(2,1)} %copy.133.refs_0_, ...), custom_call_target="tpu_custom_call" | custom-call | tf_op jit(solution)/shard_map/gather_inputs/pallas_call | solution.py:796
  284.9 57.7 %back.3 = (bf16[8,16,1536]{2,1,0:T(8,128)(2,1)}, f32[512,1024]{1,0:T(8,128)}, bf16[8,512,128]{2,1,0:T(8,128)(2,1)}, bf16[8,512,256]{2,1,0:T(8,128)(2,1)}, bf16[8,512,256]{2,1,0:T(8,128)(2,1)}) custom-call(s32[1]{0:T(128)} %bitcast.14.refs_0_, bf16[2,16,1024]{2,1,0:T(8,128)(2,1)} %get-tuple-element.47.refs_7_.refs_1_, ...), custom_call_target="tpu_custom_call" | custom-call | tf_op jit(solution)/shard_map/back/pallas_call | solution.py:1173
  342.7 2.5 collective-permute-start
  345.2 3.5 all-to-all-start.5
  348.8 2.8 collective-permute-start.2
  351.5 3.5 collective-permute-start.3
  355.0 1.1 collective-permute-start.4
  356.1 0.9 all-to-all-done.5
  356.9 3.6 all-to-all-start
  360.7 2.8 collective-permute-start.14
  363.5 3.6 collective-permute-start.15
  367.1 1.1 collective-permute-start.16
  368.1 3.2 slice_bitcast_fusion.refs_13_
  371.4 1.0 collective-permute-done.14
  372.4 8.1 %collective-permute-done.15 = bf16[4,16,1536]{2,0,1:T(4,128)(2,1)S(1)} collective-permute-done((bf16[4,16,1536]{2,0,1:T(4,128)(2,1)S(1)}, bf16[4,16,1536]{2,0,1:T(4,128)(2,1)S(1)}, u32[]{:S(2)}, u32[]{:S(2)}) %collective-permute-start.15) | collective-permute-done | bytes 196640 | tf_op jit(solution)/shard_map/ppermute | solution.py:1314
  380.5 0.8 convolution_bitcast_fusion.6
  381.9 62.1 %back.4 = (bf16[8,16,512]{2,1,0:T(8,128)(2,1)}, bf16[8,16,1536]{2,1,0:T(8,128)(2,1)}, f32[512,1024]{1,0:T(8,128)}, bf16[8,512,128]{2,1,0:T(8,128)(2,1)}, bf16[8,...) custom-call(s32[1]{0:T(128)} %bitcast.14.refs_0_, bf16[2,16,1024]{2,1,0:T(8,128)(2,1)} %get-tuple-element.47.refs_7_.refs_1_, ...), custom_call_target="tpu_custom_call" | custom-call | tf_op jit(solution)/shard_map/back/pallas_call | solution.py:1173
  444.1 0.8 convolution_bitcast_fusion.8
  444.9 4.0 all-to-all-start.3
  448.9 0.8 convolution_bitcast_fusion.10
  449.7 4.7 all-to-all-done.3
  454.5 3.5 all-to-all-start.4
  458.3 2.7 to_rows.2
  461.0 5.5 %collective-permute-start.10 = (bf16[4,16,512]{2,0,1:T(4,128)(2,1)S(1)}, bf16[4,16,512]{2,0,1:T(4,128)(2,1)S(1)}, u32[]{:S(2)}, u32[]{:S(2)}) collective-permute-start(bf16[4,16,512]{2,0,1:T(4,128)(2,1)S(1)} %copy.142), channel_id=1, source_target_pairs={{0,24},{8,0},{16,8},{24,16},{1,25},{9,1},{17,9},{25,17},{2,26},{10... | collective-permute-start | bytes 196616 | tf_op jit(solution)/shard_map/ppermute | solution.py:1314
  467.5 4.0 collective-permute-start.11
  471.5 1.3 collective-permute-start.12
  473.9 9.6 %collective-permute-done.9 = bf16[4,16,512]{2,0,1:T(4,128)(2,1)S(1)} collective-permute-done((bf16[4,16,512]{2,0,1:T(4,128)(2,1)S(1)}, bf16[4,16,512]{2,0,1:T(4,128)(2,1)S(1)}, u32[]{:S(2)}, u32[]{:S(2)}) %collective-permute-start.9) | collective-permute-done | bytes 65568 | tf_op jit(solution)/shard_map/ppermute | solution.py:1314
  483.9 3.8 collective-permute-done.12
  489.3 1.1 copy.159
  490.6 1.1 copy.158
  492.5 14.0 %back.5 = (bf16[8,16,512]{2,1,0:T(8,128)(2,1)}, bf16[8,512,128]{2,1,0:T(8,128)(2,1)}) custom-call(s32[1]{0:T(128)} %bitcast.14.refs_0_, bf16[2,16,1024]{2,1,0:T(8,128)(2,1)} %get-tuple-element.47.refs_7_.refs_1_, bf16[2,8,16,384]{3,2,1,0:T(8,128)(2,1)} %reshape.93.refs_8_.refs_2_, bf16[2,16,1024]{2,1,0:T(8,128)(2,1)} %get-tuple-element.48.refs_9_.refs_3_, ...), custom_call_target="tpu_custom_call" | custom-call | tf_op jit(solution)/shard_map/back/pallas_call | solution.py:1173
  506.5 4.1 all-to-all-start.2
  510.8 5.4 all-to-all-done.2
  516.2 3.6 all-to-all-start.1
  520.7 4.3 collective-permute-start.5
  525.0 1.9 collective-permute-start.6
  528.1 1.3 collective-permute-done.5
  529.4 2.5 collective-permute-done.6
  532.6 0.8 copy.154
  534.3 0.8 all-to-all-done.1
  535.1 1.0 copy-done.3
  536.1 2.7 to_rows.3
  (100 shorter events, 11.5 us)
Async XLA Ops:
  0.6 2.2 copy-start
  0.7 5.4 %copy-start.9 = (bf16[2,3,128]{2,0,1:T(2,128)(2,1)S(1)}, bf16[2,3,128]{2,0,1:T(2,128)(2,1)}, u32[]{:S(2)}) copy-start(bf16[2,3,128]{2,0,1:T(2,128)(2,1)} %param.27) | copy-start | bytes 4612
  0.7 5.4 %copy-start.15 = (bf16[2,128]{1,0:T(2,128)(2,1)S(1)}, bf16[2,128]{1,0:T(2,128)(2,1)}, u32[]{:S(2)}) copy-start(bf16[2,128]{1,0:T(2,128)(2,1)} %param.29) | copy-start | bytes 1540
  0.7 5.4 %copy-start.14 = (bf16[2,128]{1,0:T(2,128)(2,1)S(1)}, bf16[2,128]{1,0:T(2,128)(2,1)}, u32[]{:S(2)}) copy-start(bf16[2,128]{1,0:T(2,128)(2,1)} %param.33) | copy-start | bytes 1540
  0.7 5.4 %copy-start.13 = (bf16[2,128]{1,0:T(2,128)(2,1)S(1)}, bf16[2,128]{1,0:T(2,128)(2,1)}, u32[]{:S(2)}) copy-start(bf16[2,128]{1,0:T(2,128)(2,1)} %param.34) | copy-start | bytes 1540
  0.7 5.4 %copy-start.12 = (bf16[2,128]{1,0:T(2,128)(2,1)S(1)}, bf16[2,128]{1,0:T(2,128)(2,1)}, u32[]{:S(2)}) copy-start(bf16[2,128]{1,0:T(2,128)(2,1)} %param.35) | copy-start | bytes 1540
  0.7 5.4 %copy-start.11 = (bf16[2,128]{1,0:T(2,128)(2,1)S(1)}, bf16[2,128]{1,0:T(2,128)(2,1)}, u32[]{:S(2)}) copy-start(bf16[2,128]{1,0:T(2,128)(2,1)} %param.36) | copy-start | bytes 1540
  0.7 5.4 %copy-start.10 = (bf16[2,128]{1,0:T(2,128)(2,1)S(1)}, bf16[2,128]{1,0:T(2,128)(2,1)}, u32[]{:S(2)}) copy-start(bf16[2,128]{1,0:T(2,128)(2,1)} %param.37) | copy-start | bytes 1540
  0.7 5.5 %copy-start.7 = (bf16[2,512]{1,0:T(2,128)(2,1)S(1)}, bf16[2,512]{1,0:T(2,128)(2,1)}, u32[]{:S(2)}) copy-start(bf16[2,512]{1,0:T(2,128)(2,1)} %param.31) | copy-start | bytes 6148
  284.9 63.7 %copy-start.8 = (s32[4,4]{1,0:T(4,128)S(1)}, s32[4,4]{1,0:T(4,128)}, u32[]{:S(2)}) copy-start(s32[4,4]{1,0:T(4,128)} %param.25) | copy-start | bytes 196
  342.7 39.2 %collective-permute-start = (bf16[8,512,256]{2,1,0:T(8,128)(2,1)}, bf16[8,512,256]{2,1,0:T(8,128)(2,1)}, u32[]{:S(2)}, u32[]{:S(2)}) collective-permute-start(bf16[8,512,256]{2,1,0:T(8,128)(2,1)} %get-tuple-element.73), channel_id=1, source_target_pairs={{0,1},{1,0},{2,3},{3,2},{4,5},{5,4},{6,7},{7,6},{8,9},{9,8},{10,11... | collective-permute-start | bytes 6291464 | tf_op jit(solution)/shard_map/ppermute | solution.py:1282
  345.2 11.7 %all-to-all-start.5 = ((bf16[8,16,1536]{2,1,0:T(8,128)(2,1)}), bf16[8,16,1536]{2,1,0:T(8,128)(2,1)S(1)}, u32[]{:S(2)}, u32[]{:S(2)}) async-start(bf16[8,16,1536]{2,1,0:T(8,128)(2,1)} %get-tuple-element.83), calls=%async_computation.5 | async-start | bytes 786432 | tf_op jit(solution)/shard_map/all_to_all | solution.py:1330
  348.8 14.7 %collective-permute-start.2 = (bf16[4,4,8]{1,2,0:T(8,128)(2,1)S(1)}, bf16[4,4,8]{1,2,0:T(8,128)(2,1)S(1)}, u32[]{:S(2)}, u32[]{:S(2)}) collective-permute-start(bf16[4,4,8]{1,2,0:T(8,128)(2,1)S(1)} %fusion.80), channel_id=1, source_target_pairs={{0,8},{8,16},{16,24},{24,0},{1,9},{9,17},{17,25},{25,1},{2,10},{10... | collective-permute-start | bytes 776 | tf_op jit(solution)/shard_map/ppermute | solution.py:1314
  351.5 15.6 %collective-permute-start.3 = (bf16[4,4,8]{1,2,0:T(8,128)(2,1)S(1)}, bf16[4,4,8]{1,2,0:T(8,128)(2,1)S(1)}, u32[]{:S(2)}, u32[]{:S(2)}) collective-permute-start(bf16[4,4,8]{1,2,0:T(8,128)(2,1)S(1)} %fusion.80), channel_id=1, source_target_pairs={{0,16},{8,24},{16,0},{24,8},{1,17},{9,25},{17,1},{25,9},{2,18},{10... | collective-permute-start | bytes 776 | tf_op jit(solution)/shard_map/ppermute | solution.py:1314
  355.0 16.3 %collective-permute-start.4 = (bf16[4,4,8]{1,2,0:T(8,128)(2,1)S(1)}, bf16[4,4,8]{1,2,0:T(8,128)(2,1)S(1)}, u32[]{:S(2)}, u32[]{:S(2)}) collective-permute-start(bf16[4,4,8]{1,2,0:T(8,128)(2,1)S(1)} %fusion.80), channel_id=1, source_target_pairs={{0,24},{8,0},{16,8},{24,16},{1,25},{9,1},{17,9},{25,17},{2,26},{10... | collective-permute-start | bytes 776 | tf_op jit(solution)/shard_map/ppermute | solution.py:1314
  356.9 88.0 %all-to-all-start = ((bf16[8,512,128]{2,1,0:T(8,128)(2,1)}), bf16[8,512,128]{2,1,0:T(8,128)(2,1)S(1)}, u32[]{:S(2)}, u32[]{:S(2)}) async-start(bf16[8,512,128]{2,1,0:T(8,128)(2,1)} %get-tuple-element.54), calls=%async_computation | async-start | bytes 2097152 | tf_op jit(solution)/shard_map/all_to_all | solution.py:1287
  360.7 11.7 %collective-permute-start.14 = (bf16[4,16,1536]{2,0,1:T(4,128)(2,1)S(1)}, bf16[4,16,1536]{2,0,1:T(4,128)(2,1)S(1)}, u32[]{:S(2)}, u32[]{:S(2)}) collective-permute-start(bf16[4,16,1536]{2,0,1:T(4,128)(2,1)S(1)} %copy.152), channel_id=1, source_target_pairs={{0,8},{8,16},{16,24},{24,0},{1,9},{9,17},{17,25},{25,1},{2,10},{10... | collective-permute-start | bytes 589832 | tf_op jit(solution)/shard_map/ppermute | solution.py:1314
  363.5 17.0 %collective-permute-start.15 = (bf16[4,16,1536]{2,0,1:T(4,128)(2,1)S(1)}, bf16[4,16,1536]{2,0,1:T(4,128)(2,1)S(1)}, u32[]{:S(2)}, u32[]{:S(2)}) collective-permute-start(bf16[4,16,1536]{2,0,1:T(4,128)(2,1)S(1)} %copy.152), channel_id=1, source_target_pairs={{0,16},{8,24},{16,0},{24,8},{1,17},{9,25},{17,1},{25,9},{2,18},{10... | collective-permute-start | bytes 589832 | tf_op jit(solution)/shard_map/ppermute | solution.py:1314
  367.1 13.4 %collective-permute-start.16 = (bf16[4,16,1536]{2,0,1:T(4,128)(2,1)S(1)}, bf16[4,16,1536]{2,0,1:T(4,128)(2,1)S(1)}, u32[]{:S(2)}, u32[]{:S(2)}) collective-permute-start(bf16[4,16,1536]{2,0,1:T(4,128)(2,1)S(1)} %copy.152), channel_id=1, source_target_pairs={{0,24},{8,0},{16,8},{24,16},{1,25},{9,1},{17,9},{25,17},{2,26},{10... | collective-permute-start | bytes 589832 | tf_op jit(solution)/shard_map/ppermute | solution.py:1314
  444.0 48.5 %collective-permute-start.1 = (bf16[8,512,256]{2,1,0:T(8,128)(2,1)}, bf16[8,512,256]{2,1,0:T(8,128)(2,1)}, u32[]{:S(2)}, u32[]{:S(2)}) collective-permute-start(bf16[8,512,256]{2,1,0:T(8,128)(2,1)} %get-tuple-element.78), channel_id=1, source_target_pairs={{0,1},{1,0},{2,3},{3,2},{4,5},{5,4},{6,7},{7,6},{8,9},{9,8},{10,11... | collective-permute-start | bytes 6291464 | tf_op jit(solution)/shard_map/ppermute | solution.py:1282
  444.9 13.3 %copy-start.2 = (bf16[8,512,128]{2,1,0:T(8,128)(2,1)}, bf16[8,512,128]{2,1,0:T(8,128)(2,1)S(1)}, u32[]{:S(2)}) copy-start(bf16[8,512,128]{2,1,0:T(8,128)(2,1)S(1)} %all-to-all-done) | copy-start | bytes 3145732
  444.9 9.6 %all-to-all-start.3 = ((bf16[8,16,512]{2,1,0:T(8,128)(2,1)}), bf16[8,16,512]{2,1,0:T(8,128)(2,1)S(1)}, u32[]{:S(2)}, u32[]{:S(2)}) async-start(bf16[8,16,512]{2,1,0:T(8,128)(2,1)} %get-tuple-element.81), calls=%async_computation.3 | async-start | bytes 262144 | tf_op jit(solution)/shard_map/all_to_all | solution.py:1330
  454.5 12.8 %all-to-all-start.4 = ((bf16[8,16,1536]{2,1,0:T(8,128)(2,1)}), bf16[8,16,1536]{2,1,0:T(8,128)(2,1)S(1)}, u32[]{:S(2)}, u32[]{:S(2)}) async-start(bf16[8,16,1536]{2,1,0:T(8,128)(2,1)} %get-tuple-element.82), calls=%async_computation.4 | async-start | bytes 786432 | tf_op jit(solution)/shard_map/all_to_all | solution.py:1330
  460.9 26.9 %copy-start.5 = (f32[1,8,16,128]{3,1,2,0:T(8,128)S(1)}, f32[1,8,16,128]{3,1,2,0:T(8,128)}, u32[]{:S(2)}) copy-start(f32[1,8,16,128]{3,1,2,0:T(8,128)} %convolution_bitcast_fusion.6) | copy-start | bytes 196612
  461.0 10.4 %collective-permute-start.10 = (bf16[4,16,512]{2,0,1:T(4,128)(2,1)S(1)}, bf16[4,16,512]{2,0,1:T(4,128)(2,1)S(1)}, u32[]{:S(2)}, u32[]{:S(2)}) collective-permute-start(bf16[4,16,512]{2,0,1:T(4,128)(2,1)S(1)} %copy.142), channel_id=1, source_target_pairs={{0,24},{8,0},{16,8},{24,16},{1,25},{9,1},{17,9},{25,17},{2,26},{10... | collective-permute-start | bytes 196616 | tf_op jit(solution)/shard_map/ppermute | solution.py:1314
  466.5 6.8 %collective-permute-start.8 = (bf16[4,16,512]{2,0,1:T(4,128)(2,1)S(1)}, bf16[4,16,512]{2,0,1:T(4,128)(2,1)S(1)}, u32[]{:S(2)}, u32[]{:S(2)}) collective-permute-start(bf16[4,16,512]{2,0,1:T(4,128)(2,1)S(1)} %copy.142), channel_id=1, source_target_pairs={{0,8},{8,16},{16,24},{24,0},{1,9},{9,17},{17,25},{25,1},{2,10},{10... | collective-permute-start | bytes 196616 | tf_op jit(solution)/shard_map/ppermute | solution.py:1314
  466.5 17.0 %collective-permute-start.9 = (bf16[4,16,512]{2,0,1:T(4,128)(2,1)S(1)}, bf16[4,16,512]{2,0,1:T(4,128)(2,1)S(1)}, u32[]{:S(2)}, u32[]{:S(2)}) collective-permute-start(bf16[4,16,512]{2,0,1:T(4,128)(2,1)S(1)} %copy.142), channel_id=1, source_target_pairs={{0,16},{8,24},{16,0},{24,8},{1,17},{9,25},{17,1},{25,9},{2,18},{10... | collective-permute-start | bytes 196616 | tf_op jit(solution)/shard_map/ppermute | solution.py:1314
  467.5 16.4 %collective-permute-start.11 = (bf16[4,16,1536]{2,0,1:T(4,128)(2,1)S(1)}, bf16[4,16,1536]{2,0,1:T(4,128)(2,1)S(1)}, u32[]{:S(2)}, u32[]{:S(2)}) collective-permute-start(bf16[4,16,1536]{2,0,1:T(4,128)(2,1)S(1)} %copy.148), channel_id=1, source_target_pairs={{0,8},{8,16},{16,24},{24,0},{1,9},{9,17},{17,25},{25,1},{2,10},{10... | collective-permute-start | bytes 589832 | tf_op jit(solution)/shard_map/ppermute | solution.py:1314
  471.5 16.3 %collective-permute-start.12 = (bf16[4,16,1536]{2,0,1:T(4,128)(2,1)S(1)}, bf16[4,16,1536]{2,0,1:T(4,128)(2,1)S(1)}, u32[]{:S(2)}, u32[]{:S(2)}) collective-permute-start(bf16[4,16,1536]{2,0,1:T(4,128)(2,1)S(1)} %copy.148), channel_id=1, source_target_pairs={{0,16},{8,24},{16,0},{24,8},{1,17},{9,25},{17,1},{25,9},{2,18},{10... | collective-permute-start | bytes 589832 | tf_op jit(solution)/shard_map/ppermute | solution.py:1314
  473.4 14.4 %collective-permute-start.13 = (bf16[4,16,1536]{2,0,1:T(4,128)(2,1)S(1)}, bf16[4,16,1536]{2,0,1:T(4,128)(2,1)S(1)}, u32[]{:S(2)}, u32[]{:S(2)}) collective-permute-start(bf16[4,16,1536]{2,0,1:T(4,128)(2,1)S(1)} %copy.148), channel_id=1, source_target_pairs={{0,24},{8,0},{16,8},{24,16},{1,25},{9,1},{17,9},{25,17},{2,26},{10... | collective-permute-start | bytes 589832 | tf_op jit(solution)/shard_map/ppermute | solution.py:1314
  489.3 2.6 copy-start.6
  506.5 13.3 %copy-start.4 = (f32[1,8,16,128]{3,1,2,0:T(8,128)S(1)}, f32[1,8,16,128]{3,1,2,0:T(8,128)}, u32[]{:S(2)}) copy-start(f32[1,8,16,128]{3,1,2,0:T(8,128)} %convolution_bitcast_fusion.10) | copy-start | bytes 196612
  506.5 9.7 %all-to-all-start.2 = ((bf16[8,16,512]{2,1,0:T(8,128)(2,1)}), bf16[8,16,512]{2,1,0:T(8,128)(2,1)S(1)}, u32[]{:S(2)}, u32[]{:S(2)}) async-start(bf16[8,16,512]{2,1,0:T(8,128)(2,1)} %get-tuple-element.80), calls=%async_computation.2 | async-start | bytes 262144 | tf_op jit(solution)/shard_map/all_to_all | solution.py:1330
  516.2 18.9 %all-to-all-start.1 = ((bf16[8,512,128]{2,1,0:T(8,128)(2,1)}), bf16[8,512,128]{2,1,0:T(8,128)(2,1)S(1)}, u32[]{:S(2)}, u32[]{:S(2)}) async-start(bf16[8,512,128]{2,1,0:T(8,128)(2,1)} %get-tuple-element.79), calls=%async_computation.1 | async-start | bytes 2097152 | tf_op jit(solution)/shard_map/all_to_all | solution.py:1287
  520.7 8.7 %collective-permute-start.5 = (bf16[4,16,512]{2,0,1:T(4,128)(2,1)S(1)}, bf16[4,16,512]{2,0,1:T(4,128)(2,1)S(1)}, u32[]{:S(2)}, u32[]{:S(2)}) collective-permute-start(bf16[4,16,512]{2,0,1:T(4,128)(2,1)S(1)} %copy.138), channel_id=1, source_target_pairs={{0,8},{8,16},{16,24},{24,0},{1,9},{9,17},{17,25},{25,1},{2,10},{10... | collective-permute-start | bytes 196616 | tf_op jit(solution)/shard_map/ppermute | solution.py:1314
  525.0 6.9 %collective-permute-start.6 = (bf16[4,16,512]{2,0,1:T(4,128)(2,1)S(1)}, bf16[4,16,512]{2,0,1:T(4,128)(2,1)S(1)}, u32[]{:S(2)}, u32[]{:S(2)}) collective-permute-start(bf16[4,16,512]{2,0,1:T(4,128)(2,1)S(1)} %copy.138), channel_id=1, source_target_pairs={{0,16},{8,24},{16,0},{24,8},{1,17},{9,25},{17,1},{25,9},{2,18},{10... | collective-permute-start | bytes 196616 | tf_op jit(solution)/shard_map/ppermute | solution.py:1314
  526.9 5.5 %collective-permute-start.7 = (bf16[4,16,512]{2,0,1:T(4,128)(2,1)S(1)}, bf16[4,16,512]{2,0,1:T(4,128)(2,1)S(1)}, u32[]{:S(2)}, u32[]{:S(2)}) collective-permute-start(bf16[4,16,512]{2,0,1:T(4,128)(2,1)S(1)} %copy.138), channel_id=1, source_target_pairs={{0,24},{8,0},{16,8},{24,16},{1,25},{9,1},{17,9},{25,17},{2,26},{10... | collective-permute-start | bytes 196616 | tf_op jit(solution)/shard_map/ppermute | solution.py:1314
  532.6 6.2 %copy-start.1 = (bf16[2,8,16,3,1024]{4,2,3,1,0:T(8,128)(2,1)S(1)}, bf16[2,8,16,3,1024]{4,2,3,1,0:T(8,128)(2,1)}, u32[]{:S(2)}) copy-start(bf16[2,8,16,3,1024]{4,2,3,1,0:T(8,128)(2,1)} %param.39) | copy-start | bytes 4718596
  535.1 1.0 copy-start.3
